TPU v7x, 256 devices: a whole 4x4x8 slice. The times are simulated.
256 devices in a mesh: row: 16 (over y, x_lo, core), col: 16 (over z, x_hi).
Axes of the slice: x: 4 (x_hi: 2, x_lo: 2; x = x_hi * 2 + x_lo), y: 4, z: 8, core: 2. Of those that a mesh axis runs over, the one named last changes fastest.
Arguments:
- weight_tiles: bfloat16 [4096, 8192], P('row', 'col'), may hold values from -6 to 6
- expand_rows: bfloat16 [5120, 4096], P(None, 'row'), may hold values from -0.125 to 0.125
- expand_cols: bfloat16 [10240, 8192], P('row', 'col'), may hold values from -0.09375 to 0.09375
Outputs:
- grown: bfloat16 [5120, 10240], P('row', 'col')
All inputs are finite; a program needn't handle non-finite values.
Results may differ from a plain program's by a relative error of at most 0.0049.
Values may be sent and summed in bfloat16 or wider, within the bound.
No kernel may reach another device: no remote copies, remote signals or barrier semaphores. Data moves between devices by JAX's collectives and lax.ppermute only.
A program may use at most 128 MiB of HBM per device.

v0:
```python
import jax
import jax.numpy as jnp
from jax import lax
from jax.sharding import PartitionSpec as P


def contract_last(left, right):
    return lax.dot_general(
        left, right, (((1,), (1,)), ((), ())), preferred_element_type=jnp.float32
    )


def on_device(weight_tiles, expand_rows, expand_cols):
    gathered = lax.all_gather(expand_cols, "row", axis=0, tiled=True)
    rows_part = gathered
    stretched = lax.psum_scatter(
        contract_last(rows_part, weight_tiles), "col", scatter_dimension=0, tiled=True
    )
    stretched = stretched.astype(jnp.bfloat16)
    rows_part = expand_rows
    grown = lax.psum_scatter(
        contract_last(rows_part, stretched), "row", scatter_dimension=0, tiled=True
    )
    return grown.astype(jnp.bfloat16)


def solution(mesh):
    return jax.shard_map(
        on_device,
        mesh=mesh,
        in_specs=(P("row", "col"), P(None, "row"), P("row", "col")),
        out_specs=P("row", "col"),
        check_vma=False,
    )
```

profile of v0, /device:TPU:6, one launch (start us, length us, event | category | flops | bytes accessed | tf_op | source)
XLA Modules:
  0.0 500.3 jit_solution(391718990354344512)
XLA Ops:
  6.5 0.0 copy-start
  6.5 0.0 all-gather.2.cloned.1.call-start
  6.5 0.7 all-gather.2.cloned.1.call-update
  7.3 0.0 reduce-scatter.5.cloned.1.call-start
  7.3 69.3 %all-gather.2.cloned.1.call-done = bf16[10240,512]{1,0:T(8,128)(2,1)} async-done(((bf16[640,512]{1,0:T(8,128)(2,1)}), bf16[10240,512]{1,0:T(8,128)(2,1)}) %all-gather.2.cloned.1.call-update) | async-done | bytes 10485776 | tf_op jit(solution)/shard_map/all_gather | solution.py:14
  76.6 10.9 %fusion.1 = f32[10240,256]{1,0:T(8,128)} fusion(bf16[10240,512]{1,0:T(8,128)(2,1)} %all-gather.2.cloned.1.call-done, bf16[256,512]{1,0:T(8,128)(2,1)} %param.3), kind=kOutput, calls=%fused_computation.2 | convolution fusion | flops 2684354560 | bytes 21233664 | tf_op jit(solution)/shard_map/dot_general | solution.py:8
  87.5 0.0 reduce-scatter.5.cloned.1.call-update
  87.5 0.0 reduce-scatter.7.cloned.1.call-start
  87.5 238.3 %reduce-scatter.5.cloned.1.call-done = f32[640,256]{1,0:T(8,128)} async-done(((f32[10240,256]{1,0:T(8,128)}), f32[640,256]{1,0:T(8,128)}) %reduce-scatter.5.cloned.1.call-update) | async-done | bytes 655376 | tf_op jit(solution)/shard_map/reduce_scatter | solution.py:16
  325.8 0.0 copy-done
  325.8 7.7 %convolution_bitcast_fusion = f32[5120,640]{0,1:T(8,128)} fusion(bf16[5120,256]{1,0:T(8,128)(2,1)S(1)} %copy-done, f32[640,256]{1,0:T(8,128)} %reduce-scatter.5.cloned.1.call-done), kind=kOutput, calls=%fused_computation | convolution fusion | flops 1677885440 | bytes 16384000 | tf_op jit(solution)/shard_map/dot_general | solution.py:8
  333.5 14.0 %copy.7 = f32[5120,640]{1,0:T(8,128)} copy(f32[5120,640]{0,1:T(8,128)} %convolution_bitcast_fusion) | data formatting | bytes 26214400
  347.5 0.0 reduce-scatter.7.cloned.1.call-update
  347.5 144.3 %reduce-scatter.7.cloned.1.call-done = f32[320,640]{1,0:T(8,128)} async-done(((f32[5120,640]{1,0:T(8,128)}), f32[320,640]{1,0:T(8,128)}) %reduce-scatter.7.cloned.1.call-update) | async-done | bytes 819216 | tf_op jit(solution)/shard_map/reduce_scatter | solution.py:21
  491.8 1.9 convert_element_type.7
Async XLA Ops:
  6.5 319.3 %copy-start = (bf16[5120,256]{1,0:T(8,128)(2,1)S(1)}, bf16[5120,256]{1,0:T(8,128)(2,1)}, u32[]{:S(2)}) copy-start(bf16[5120,256]{1,0:T(8,128)(2,1)} %param.4) | copy-start | bytes 7864324
  6.5 70.0 %all-gather.2.cloned.1.call-start = ((), (), s32[]{:S(2)}) async-start(), calls=%async_computation.2 | async-start | bytes 11141120 | tf_op jit(solution)/shard_map/all_gather | solution.py:14
  7.3 318.6 %reduce-scatter.5.cloned.1.call-start = ((), (), s32[]{:S(2)}) async-start(), calls=%async_computation.3 | async-start | bytes 11141120 | tf_op jit(solution)/shard_map/reduce_scatter | solution.py:16
  87.5 404.4 %reduce-scatter.7.cloned.1.call-start = ((), (), s32[]{:S(2)}) async-start(), calls=%async_computation.4 | async-start | bytes 13926400 | tf_op jit(solution)/shard_map/reduce_scatter | solution.py:21
Sparse Core Ops, SparseCore 0:
  9.2 67.3 all-gather.1
  87.6 238.1 reduce-scatter.4
  347.6 144.1 reduce-scatter.6
where the time goes:
time: 503 us; the launch traced here: 500 us
  waiting for transfers between devices  453 us (90%)
  matrix products  18.5 us (4%)
  local copies, waits for them, and re-layouts  14 us (3%)
  between operations  13.1 us (3%)
    reduce_scatter x1, waiting for transfers between devices, on_device(): lax.psum_scatter(contract_last(rows_part, weight_tiles), 'col', scatter_d...  238 us
    reduce_scatter x1, waiting for transfers between devices, on_device(): lax.psum_scatter(contract_last(rows_part, stretched), 'row', scatter_dime...  144 us
    all_gather x1, waiting for transfers between devices, on_device(): gathered = lax.all_gather(expand_cols, 'row', axis=0, tiled=True)  69.3 us
    dot_general x2, matrix products, contract_last(): lax.dot_general(left, right, (((1,), (1,)), ((), ())), preferred_element_...  18.5 us
    unnamed x3, local copies, waits for them, and re-layouts  14 us
  transfers between devices with their start and end apart: 3, of which 3 were waited for; matrix products, arithmetic and copies ran while one was open for 0% of the time, Pallas kernels for 0%

commit v1 on v0

v1 whole, which is shorter than its diff:
```python
import jax
import jax.numpy as jnp
from jax import lax
from jax.sharding import Mesh, PartitionSpec as P

AXES = ("y", "xl", "core", "z", "xh")
SIZES = (4, 2, 2, 8, 2)


def pairs(move):
    ids = {}
    for i in range(256):
        rest, at = i, []
        for size in reversed(SIZES):
            at.append(rest % size)
            rest //= size
        ids[tuple(reversed(at))] = i
    return [(i, ids[move(*at)]) for at, i in ids.items()]


def send(value, move):
    return lax.ppermute(value, AXES, pairs(move))


def other_core(y, xl, co, z, xh):
    return y, xl, 1 - co, z, xh


def y_up(y, xl, co, z, xh):
    return (y + 1) % 4, xl, co, z, xh


def y_down(y, xl, co, z, xh):
    return (y - 1) % 4, xl, co, z, xh


def z_up(y, xl, co, z, xh):
    return y, xl, co, (z + 1) % 8, xh


def z_down(y, xl, co, z, xh):
    return y, xl, co, (z - 1) % 8, xh


def in_run(y, xl, co, z, xh):
    return y, 1 - xl, co, z, xh


def out_run(y, xl, co, z, xh):
    return y, 1 - xl, co, z, 1 - xh


def dispatch(j):
    def move(y, xl, co, z, xh):
        p = (z + j) % 8
        return p // 2, p % 2, co, 2 * y + xl, xh

    return move


def rotated(stack, start):
    n = stack.shape[0]
    return lax.dynamic_slice_in_dim(jnp.concatenate([stack, stack]), start, n, 0)


def dot_f32(left, right):
    return lax.dot_general(
        left, right, (((0, 2), (0, 2)), ((), ())), preferred_element_type=jnp.float32
    )


def on_device(weight_tiles, expand_rows, expand_cols):
    y, xl, co, z, xh = (lax.axis_index(a) for a in AXES)
    p = 2 * y + xl
    bf16 = jnp.bfloat16
    k1, width = weight_tiles.shape
    half = width // 2
    m = expand_rows.shape[0] // 16
    n = expand_cols.shape[0]
    quarter = n // 4

    rows = expand_rows.reshape(4, 2, 2, m, k1)
    mine = lax.dynamic_index_in_dim(rows, co, 2, keepdims=False)
    theirs = lax.dynamic_index_in_dim(rows, 1 - co, 2, keepdims=False)
    got_rows = send(theirs, other_core)
    got_tiles = send(weight_tiles, other_core)

    pieces = expand_cols.reshape(4, quarter, 2, half).transpose(0, 2, 1, 3)
    pieces = rotated(pieces.reshape(8, quarter, half), z)
    got = [send(pieces[j], dispatch(j)) for j in range(8)]

    left = jnp.concatenate([mine, got_rows], -1).reshape(8 * m, 2 * k1)
    right = jnp.concatenate([weight_tiles, got_tiles], 0)
    part = [
        jnp.dot(left, right[:, i * half : (i + 1) * half], preferred_element_type=jnp.float32)
        .astype(bf16).reshape(4, 2 * m, half)
        for i in range(2)
    ]
    part = jnp.stack(part, 1).reshape(8, 2 * m, half)
    part = lax.all_to_all(part, ("y", "xl"), 0, 0, tiled=True)
    inner = jnp.sum(part.astype(jnp.float32), 0).astype(bf16)
    inner = jnp.where(xl == 0, inner, jnp.concatenate([inner[m:], inner[:m]]))

    cols = rotated(jnp.stack(got[::-1]), (7 - p + z) % 8)
    below = send(cols, y_up)
    above = send(cols, y_down)
    far = jnp.concatenate([send(below[:4], y_up), send(above[4:], y_down)])
    full = jnp.zeros((8, n, half), bf16)
    for shift, block in ((0, cols), (1, above), (2, far), (3, below)):
        full = lax.dynamic_update_slice_in_dim(full, block, (y + shift) % 4 * quarter, 1)
    other = send(full, other_core)
    near_cols = jnp.where(xh == co, full, other)
    far_cols = jnp.where(xh == co, other, full)

    slots = [inner] + [None] * 7
    for i in range(1, 4):
        slots[i] = send(slots[i - 1], z_down)
        slots[-i] = send(slots[(-i + 1) % 8], z_up)
    slots[4] = jnp.concatenate([send(slots[3][:m], z_down), send(slots[5][m:], z_up)])
    inner_all = jnp.stack(slots)

    cross = dot_f32(inner_all, far_cols)
    cut = m // 2
    via_in = send(cross[:cut].astype(bf16), in_run)
    via_out = send(cross[cut:m].astype(bf16), out_run)
    straight = dot_f32(inner_all, near_cols)
    to_out = cross[m:] + jnp.pad(via_in.astype(jnp.float32), ((0, m - cut), (0, 0)))
    to_in = straight[m:] + jnp.pad(via_out.astype(jnp.float32), ((cut, 0), (0, 0)))
    from_out = send(to_out.astype(bf16), out_run)
    from_in = send(to_in.astype(bf16), in_run)
    total = straight[:m] + from_out.astype(jnp.float32) + from_in.astype(jnp.float32)
    return total.astype(bf16)


def solution(mesh):
    fine = Mesh(mesh.devices.reshape(SIZES), AXES)
    row, col = ("y", "xl", "core"), ("z", "xh")
    return jax.shard_map(
        on_device,
        mesh=fine,
        in_specs=(P(row, col), P(None, row), P(row, col)),
        out_specs=P(row, col),
        check_vma=False,
    )
```

time: 503 us -> 203 us (0.40)
  waiting for transfers between devices: 453 us -> 103 us
  starting transfers between devices: 0.08 us -> 66.4 us
  between operations: 13.1 us -> 0.4 us
  matrix products: 18.5 us -> 9.66 us
    reduce_scatter x2 -> x0, waiting for transfers between devices: 383 us -> none  [the longest x1 238 us: on_device(): lax.psum_scatter(contract_last(rows_part, weight_tiles), 'col', scatter_d...]
    ppermute x0 -> x27, waiting for transfers between devices: none -> 103 us  [send(): return lax.ppermute(value, AXES, pairs(move))]
    all_gather x1 -> x0, waiting for transfers between devices: 69.3 us -> none  [on_device(): gathered = lax.all_gather(expand_cols, 'row', axis=0, tiled=True)]
    ppermute x0 -> x27, starting transfers between devices: none -> 62.2 us  [send(): return lax.ppermute(value, AXES, pairs(move))]
    unnamed x3 -> x33, local copies, waits for them, and re-layouts: 14 us -> 3.11 us
    dot_general x2 -> x4, matrix products: 18.5 us -> 9.66 us  [the longest x2 7.98 us: dot_f32(): lax.dot_general(left, right, (((0, 2), (0, 2)), ((), ())), preferred_elem...]
  transfers between devices with their start and end apart: 3 -> 28, of which waited for: 3 -> 14; matrix products, arithmetic and copies ran while one was open for 0% -> 9% of each run, Pallas kernels for 0% -> 0%
where the time goes in v1:
time: 203 us; the launch traced here: 201 us
  waiting for transfers between devices  103 us (51%)
  starting transfers between devices  66.4 us (33%)
  local copies, waits for them, and re-layouts  15.2 us (7%)
  matrix products  9.66 us (5%)
  other arithmetic  5.7 us (3%)
    ppermute x27, waiting for transfers between devices, send(): return lax.ppermute(value, AXES, pairs(move))  103 us
    ppermute x27, starting transfers between devices, send(): return lax.ppermute(value, AXES, pairs(move))  62.2 us
    dot_general x2, matrix products, dot_f32(): lax.dot_general(left, right, (((0, 2), (0, 2)), ((), ())), preferred_elem...  7.98 us
    all_to_all x1, starting transfers between devices, on_device(): part = lax.all_to_all(part, ('y', 'xl'), 0, 0, tiled=True)  4.25 us
  transfers between devices with their start and end apart: 28, of which 14 were waited for; matrix products, arithmetic and copies ran while one was open for 9% of the time, Pallas kernels for 0%

profile of v1, /device:TPU:6, one launch (start us, length us, event | category | flops | bytes accessed | tf_op | source)
XLA Modules:
  0.0 200.6 jit_solution(12686769602132587145)
XLA Ops:
  0.0 2.0 %reshape.51 = bf16[4,160,2,256]{3,2,1,0:T(2,128)(2,1)S(1)} reshape(bf16[640,512]{1,0:T(8,128)(2,1)} %param.5) | data formatting | bytes 1310720 | tf_op jit(solution)/shard_map/reshape | solution.py:88
  3.2 4.4 %collective-permute-start.10 = (bf16[160,256]{1,0:T(8,128)(2,1)S(1)}, bf16[160,256]{1,0:T(8,128)(2,1)S(1)}, u32[]{:S(2)}, u32[]{:S(2)}) collective-permute-start(bf16[160,256]{1,0:T(8,128)(2,1)S(1)} %get-tuple-element.18), channel_id=1, source_target_pairs={{0,224},{1,225},{2,0},{3,1},{4,32},{5,33},{6,64},{7,65},{8,96},{9,... | collective-permute-start | bytes 245768 | tf_op jit(solution)/shard_map/ppermute | solution.py:22
  7.5 5.8 %collective-permute-start.11 = (bf16[160,256]{1,0:T(8,128)(2,1)S(1)}, bf16[160,256]{1,0:T(8,128)(2,1)S(1)}, u32[]{:S(2)}, u32[]{:S(2)}) collective-permute-start(bf16[160,256]{1,0:T(8,128)(2,1)S(1)} %get-tuple-element.17), channel_id=1, source_target_pairs={{0,192},{1,193},{2,224},{3,225},{4,0},{5,1},{6,32},{7,33},{8,64},{... | collective-permute-start | bytes 245768 | tf_op jit(solution)/shard_map/ppermute | solution.py:22
  13.3 3.3 %collective-permute-start.12 = (bf16[160,256]{1,0:T(8,128)(2,1)S(1)}, bf16[160,256]{1,0:T(8,128)(2,1)S(1)}, u32[]{:S(2)}, u32[]{:S(2)}) collective-permute-start(bf16[160,256]{1,0:T(8,128)(2,1)S(1)} %get-tuple-element.16), channel_id=1, source_target_pairs={{0,160},{1,161},{2,192},{3,193},{4,224},{5,225},{6,0},{7,1},{8,32}... | collective-permute-start | bytes 245768 | tf_op jit(solution)/shard_map/ppermute | solution.py:22
  16.6 2.2 %collective-permute-start.13 = (bf16[160,256]{1,0:T(8,128)(2,1)S(1)}, bf16[160,256]{1,0:T(8,128)(2,1)S(1)}, u32[]{:S(2)}, u32[]{:S(2)}) collective-permute-start(bf16[160,256]{1,0:T(8,128)(2,1)S(1)} %get-tuple-element.15), channel_id=1, source_target_pairs={{0,128},{1,129},{2,160},{3,161},{4,192},{5,193},{6,224},{7,225},{8... | collective-permute-start | bytes 245768 | tf_op jit(solution)/shard_map/ppermute | solution.py:22
  19.2 1.5 collective-permute-start.14
  20.7 9.3 %collective-permute-done.11 = bf16[160,256]{1,0:T(8,128)(2,1)S(1)} collective-permute-done((bf16[160,256]{1,0:T(8,128)(2,1)S(1)}, bf16[160,256]{1,0:T(8,128)(2,1)S(1)}, u32[]{:S(2)}, u32[]{:S(2)}) %collective-permute-start.11) | collective-permute-done | bytes 81952 | tf_op jit(solution)/shard_map/ppermute | solution.py:22
  30.0 17.0 %collective-permute-start.15 = (bf16[160,256]{1,0:T(8,128)(2,1)}, bf16[160,256]{1,0:T(8,128)(2,1)S(1)}, u32[]{:S(2)}, u32[]{:S(2)}) collective-permute-start(bf16[160,256]{1,0:T(8,128)(2,1)} %get-tuple-element.13), channel_id=1, source_target_pairs={{0,64},{1,65},{2,96},{3,97},{4,128},{5,129},{6,160},{7,161},{8,192... | collective-permute-start | bytes 245768 | tf_op jit(solution)/shard_map/ppermute | solution.py:22
  47.1 3.1 %collective-permute-start.17 = (bf16[160,256]{1,0:T(8,128)(2,1)S(1)}, bf16[160,256]{1,0:T(8,128)(2,1)S(1)}, u32[]{:S(2)}, u32[]{:S(2)}) collective-permute-start(bf16[160,256]{1,0:T(8,128)(2,1)S(1)} %copy-done.5), channel_id=1, source_target_pairs={{0,0},{1,1},{2,32},{3,33},{4,64},{5,65},{6,96},{7,97},{8,128},{9,1... | collective-permute-start | bytes 245768 | tf_op jit(solution)/shard_map/ppermute | solution.py:22
  50.4 4.6 %collective-permute-done.15 = bf16[160,256]{1,0:T(8,128)(2,1)S(1)} collective-permute-done((bf16[160,256]{1,0:T(8,128)(2,1)}, bf16[160,256]{1,0:T(8,128)(2,1)S(1)}, u32[]{:S(2)}, u32[]{:S(2)}) %collective-permute-start.15) | collective-permute-done | bytes 81952 | tf_op jit(solution)/shard_map/ppermute | solution.py:22
  55.0 13.0 %collective-permute-done.16 = bf16[160,256]{1,0:T(8,128)(2,1)S(1)} collective-permute-done((bf16[160,256]{1,0:T(8,128)(2,1)}, bf16[160,256]{1,0:T(8,128)(2,1)S(1)}, u32[]{:S(2)}, u32[]{:S(2)}) %collective-permute-start.16) | collective-permute-done | bytes 81952 | tf_op jit(solution)/shard_map/ppermute | solution.py:22
  68.2 1.2 constant_dynamic-update-slice_fusion
  69.4 0.8 convolution_convert_fusion.1
  70.2 0.8 convolution_convert_fusion
  71.1 1.7 pad_maximum_fusion.1
  72.8 4.2 %all-to-all-start = ((bf16[8,640,256]{2,1,0:T(8,128)(2,1)}), bf16[8,640,256]{2,1,0:T(8,128)(2,1)S(1)}, u32[]{:S(2)}, u32[]{:S(2)}) async-start(bf16[8,640,256]{2,1,0:T(8,128)(2,1)} %bitcast.82), calls=%async_computation | async-start | bytes 5242880 | tf_op jit(solution)/shard_map/all_to_all | solution.py:100
  79.6 1.7 broadcast_in_dim.3
  81.4 1.0 constant_dynamic-update-slice_fusion.4
  82.4 1.5 collective-permute-start.19
  83.8 1.8 collective-permute-start.18
  85.6 36.4 %collective-permute-done.19 = bf16[8,160,256]{2,1,0:T(8,128)(2,1)S(1)} collective-permute-done((bf16[8,160,256]{2,1,0:T(8,128)(2,1)S(1)}, bf16[8,160,256]{2,1,0:T(8,128)(2,1)S(1)}, u32[]{:S(2)}, u32[]{:S(2)}) %collective-permute-start.19) | collective-permute-done | bytes 655392 | tf_op jit(solution)/shard_map/ppermute | solution.py:22
  122.0 0.8 slice.100
  122.8 0.8 copy-done.1
  123.7 0.7 slice.101
  124.4 3.2 %collective-permute-start.21 = (bf16[4,160,256]{2,1,0:T(8,128)(2,1)}, bf16[4,160,256]{2,1,0:T(8,128)(2,1)}, u32[]{:S(2)}, u32[]{:S(2)}) collective-permute-start(bf16[4,160,256]{2,1,0:T(8,128)(2,1)} %slice.101), channel_id=1, source_target_pairs={{0,192},{1,193},{2,194},{3,195},{4,196},{5,197},{6,198},{7,199},{8... | collective-permute-start | bytes 983048 | tf_op jit(solution)/shard_map/ppermute | solution.py:22
  127.6 2.0 constant_dynamic-update-slice_fusion.3
  129.6 2.9 %collective-permute-done.20 = bf16[4,160,256]{2,1,0:T(8,128)(2,1)} collective-permute-done((bf16[4,160,256]{2,1,0:T(8,128)(2,1)}, bf16[4,160,256]{2,1,0:T(8,128)(2,1)}, u32[]{:S(2)}, u32[]{:S(2)}) %collective-permute-start.20) | collective-permute-done | bytes 327712 | tf_op jit(solution)/shard_map/ppermute | solution.py:22
  132.5 0.9 collective-permute-done.21
  133.4 2.0 maximum_dynamic-update-slice_fusion
  135.4 0.9 constant_dynamic-update-slice_fusion.2
  136.9 3.1 %collective-permute-start.2 = (bf16[640,256]{1,0:T(8,128)(2,1)S(1)}, bf16[640,256]{1,0:T(8,128)(2,1)S(1)}, u32[]{:S(2)}, u32[]{:S(2)}) collective-permute-start(bf16[640,256]{1,0:T(8,128)(2,1)S(1)} %maximum_select_fusion.1), channel_id=1, source_target_pairs={{0,14},{1,15},{2,0},{3,1},{4,2},{5,3},{6,4},{7,5},{8,6},{9,7},{10,... | collective-permute-start | bytes 983048 | tf_op jit(solution)/shard_map/ppermute | solution.py:22
  140.0 7.6 %collective-permute-done.2 = bf16[640,256]{1,0:T(8,128)(2,1)S(1)} collective-permute-done((bf16[640,256]{1,0:T(8,128)(2,1)S(1)}, bf16[640,256]{1,0:T(8,128)(2,1)S(1)}, u32[]{:S(2)}, u32[]{:S(2)}) %collective-permute-start.2) | collective-permute-done | bytes 327712 | tf_op jit(solution)/shard_map/ppermute | solution.py:22
  147.7 3.7 %collective-permute-start.3 = (bf16[640,256]{1,0:T(8,128)(2,1)S(1)}, bf16[640,256]{1,0:T(8,128)(2,1)S(1)}, u32[]{:S(2)}, u32[]{:S(2)}) collective-permute-start(bf16[640,256]{1,0:T(8,128)(2,1)S(1)} %collective-permute-done.2), channel_id=1, source_target_pairs={{0,14},{1,15},{2,0},{3,1},{4,2},{5,3},{6,4},{7,5},{8,6},{9,7},{10,... | collective-permute-start | bytes 983048 | tf_op jit(solution)/shard_map/ppermute | solution.py:22
  151.6 7.7 %collective-permute-done.3 = bf16[640,256]{1,0:T(8,128)(2,1)S(1)} collective-permute-done((bf16[640,256]{1,0:T(8,128)(2,1)S(1)}, bf16[640,256]{1,0:T(8,128)(2,1)S(1)}, u32[]{:S(2)}, u32[]{:S(2)}) %collective-permute-start.3) | collective-permute-done | bytes 327712 | tf_op jit(solution)/shard_map/ppermute | solution.py:22
  159.3 2.6 %collective-permute-start.4 = (bf16[640,256]{1,0:T(8,128)(2,1)S(1)}, bf16[640,256]{1,0:T(8,128)(2,1)S(1)}, u32[]{:S(2)}, u32[]{:S(2)}) collective-permute-start(bf16[640,256]{1,0:T(8,128)(2,1)S(1)} %collective-permute-done.3), channel_id=1, source_target_pairs={{0,14},{1,15},{2,0},{3,1},{4,2},{5,3},{6,4},{7,5},{8,6},{9,7},{10,... | collective-permute-start | bytes 983048 | tf_op jit(solution)/shard_map/ppermute | solution.py:22
  162.0 6.3 %collective-permute-done.4 = bf16[640,256]{1,0:T(8,128)(2,1)S(1)} collective-permute-done((bf16[640,256]{1,0:T(8,128)(2,1)S(1)}, bf16[640,256]{1,0:T(8,128)(2,1)S(1)}, u32[]{:S(2)}, u32[]{:S(2)}) %collective-permute-start.4) | collective-permute-done | bytes 327712 | tf_op jit(solution)/shard_map/ppermute | solution.py:22
  168.3 3.4 %collective-permute-start.5 = (bf16[320,256]{1,0:T(8,128)(2,1)S(1)}, bf16[320,256]{1,0:T(8,128)(2,1)S(1)}, u32[]{:S(2)}, u32[]{:S(2)}) collective-permute-start(bf16[320,256]{1,0:T(8,128)(2,1)S(1)} %slice.90), channel_id=1, source_target_pairs={{0,14},{1,15},{2,0},{3,1},{4,2},{5,3},{6,4},{7,5},{8,6},{9,7},{10,... | collective-permute-start | bytes 491528 | tf_op jit(solution)/shard_map/ppermute | solution.py:22
  171.8 2.7 %collective-permute-done.5 = bf16[320,256]{1,0:T(8,128)(2,1)S(1)} collective-permute-done((bf16[320,256]{1,0:T(8,128)(2,1)S(1)}, bf16[320,256]{1,0:T(8,128)(2,1)S(1)}, u32[]{:S(2)}, u32[]{:S(2)}) %collective-permute-start.5) | collective-permute-done | bytes 163872 | tf_op jit(solution)/shard_map/ppermute | solution.py:22
  174.5 3.8 %collective-permute-done.9 = bf16[320,256]{1,0:T(8,128)(2,1)S(1)} collective-permute-done((bf16[320,256]{1,0:T(8,128)(2,1)S(1)}, bf16[320,256]{1,0:T(8,128)(2,1)S(1)}, u32[]{:S(2)}, u32[]{:S(2)}) %collective-permute-start.9) | collective-permute-done | bytes 163872 | tf_op jit(solution)/shard_map/ppermute | solution.py:22
  178.4 4.0 %fusion.25 = (bf16[640,640]{1,0:T(8,128)(2,1)S(1)}, f32[640,640]{1,0:T(8,128)S(1)}) fusion(bf16[8,640,256]{2,1,0:T(8,128)(2,1)S(1)} %bitcast_dynamic-update-slice_fusion, bf16[8,640,256]{2,1,0:T(8,128)(2,1)} %collective-permute-done.22, bf16[8,640,256]{2,1,0:T(8,128)(2,1)} %constant_dynamic-update-slice_fusion.2, pred[]{:T(512)S(6)} %eq.14), kind=kOutput, calls=%fused_computation.74 | convolution fusion | flops 1679441920 | bytes 10321921 | tf_op jit(solution)/shard_map/dot_general | solution.py:67
  182.5 0.8 collective-permute-start.23
  183.3 1.8 collective-permute-start.25
  185.1 4.0 %fusion.6 = f32[640,640]{1,0:T(8,128)S(1)} fusion(bf16[8,640,256]{2,1,0:T(8,128)(2,1)S(1)} %bitcast_dynamic-update-slice_fusion, bf16[8,640,256]{2,1,0:T(8,128)(2,1)} %constant_dynamic-update-slice_fusion.2, bf16[8,640,256]{2,1,0:T(8,128)(2,1)} %collective-permute-done.22, pred[]{:T(512)S(6)} %eq.14), kind=kOutput, calls=%fused_computation.10 | convolution fusion | flops 1679032320 | bytes 9502721 | tf_op jit(solution)/shard_map/dot_general | solution.py:67
  189.1 1.6 collective-permute-start.24
  190.7 0.9 collective-permute-done.25
  191.6 1.0 collective-permute-start.26
  192.7 6.3 %collective-permute-done.24 = bf16[320,640]{1,0:T(8,128)(2,1)S(1)} collective-permute-done((bf16[320,640]{1,0:T(8,128)(2,1)S(1)}, bf16[320,640]{1,0:T(8,128)(2,1)S(1)}, u32[]{:S(2)}, u32[]{:S(2)}) %collective-permute-start.24) | collective-permute-done | bytes 409632 | tf_op jit(solution)/shard_map/ppermute | solution.py:22
  199.7 0.9 fusion.15
  (72 shorter events, 6.2 us)
Async XLA Ops:
  2.0 16.8 %copy-start.4 = (bf16[256,512]{1,0:T(8,128)(2,1)S(1)}, bf16[256,512]{1,0:T(8,128)(2,1)}, u32[]{:S(2)}) copy-start(bf16[256,512]{1,0:T(8,128)(2,1)} %param.3) | copy-start | bytes 786436
  2.1 16.7 %copy-start = (bf16[5120,256]{1,0:T(8,128)(2,1)S(1)}, bf16[5120,256]{1,0:T(8,128)(2,1)}, u32[]{:S(2)}) copy-start(bf16[5120,256]{1,0:T(8,128)(2,1)} %param.4) | copy-start | bytes 7864324
  3.2 16.0 %collective-permute-start.10 = (bf16[160,256]{1,0:T(8,128)(2,1)S(1)}, bf16[160,256]{1,0:T(8,128)(2,1)S(1)}, u32[]{:S(2)}, u32[]{:S(2)}) collective-permute-start(bf16[160,256]{1,0:T(8,128)(2,1)S(1)} %get-tuple-element.18), channel_id=1, source_target_pairs={{0,224},{1,225},{2,0},{3,1},{4,32},{5,33},{6,64},{7,65},{8,96},{9,... | collective-permute-start | bytes 245768 | tf_op jit(solution)/shard_map/ppermute | solution.py:22
  7.5 22.5 %collective-permute-start.11 = (bf16[160,256]{1,0:T(8,128)(2,1)S(1)}, bf16[160,256]{1,0:T(8,128)(2,1)S(1)}, u32[]{:S(2)}, u32[]{:S(2)}) collective-permute-start(bf16[160,256]{1,0:T(8,128)(2,1)S(1)} %get-tuple-element.17), channel_id=1, source_target_pairs={{0,192},{1,193},{2,224},{3,225},{4,0},{5,1},{6,32},{7,33},{8,64},{... | collective-permute-start | bytes 245768 | tf_op jit(solution)/shard_map/ppermute | solution.py:22
  13.3 33.7 %collective-permute-start.12 = (bf16[160,256]{1,0:T(8,128)(2,1)S(1)}, bf16[160,256]{1,0:T(8,128)(2,1)S(1)}, u32[]{:S(2)}, u32[]{:S(2)}) collective-permute-start(bf16[160,256]{1,0:T(8,128)(2,1)S(1)} %get-tuple-element.16), channel_id=1, source_target_pairs={{0,160},{1,161},{2,192},{3,193},{4,224},{5,225},{6,0},{7,1},{8,32}... | collective-permute-start | bytes 245768 | tf_op jit(solution)/shard_map/ppermute | solution.py:22
  16.6 30.5 %collective-permute-start.13 = (bf16[160,256]{1,0:T(8,128)(2,1)S(1)}, bf16[160,256]{1,0:T(8,128)(2,1)S(1)}, u32[]{:S(2)}, u32[]{:S(2)}) collective-permute-start(bf16[160,256]{1,0:T(8,128)(2,1)S(1)} %get-tuple-element.15), channel_id=1, source_target_pairs={{0,128},{1,129},{2,160},{3,161},{4,192},{5,193},{6,224},{7,225},{8... | collective-permute-start | bytes 245768 | tf_op jit(solution)/shard_map/ppermute | solution.py:22
  18.9 49.3 %collective-permute-start.1 = (bf16[256,512]{1,0:T(8,128)(2,1)S(1)}, bf16[256,512]{1,0:T(8,128)(2,1)}, u32[]{:S(2)}, u32[]{:S(2)}) collective-permute-start(bf16[256,512]{1,0:T(8,128)(2,1)S(1)} %copy-done.4), channel_id=1, source_target_pairs={{0,16},{1,17},{2,18},{3,19},{4,20},{5,21},{6,22},{7,23},{8,24},{9,... | collective-permute-start | bytes 786440 | tf_op jit(solution)/shard_map/ppermute | solution.py:22
  18.9 28.2 %copy-start.5 = (bf16[160,256]{1,0:T(8,128)(2,1)S(1)}, bf16[160,256]{1,0:T(8,128)(2,1)}, u32[]{:S(2)}) copy-start(bf16[160,256]{1,0:T(8,128)(2,1)} %get-tuple-element.11) | copy-start | bytes 245764
  19.2 31.1 %collective-permute-start.14 = (bf16[160,256]{1,0:T(8,128)(2,1)}, bf16[160,256]{1,0:T(8,128)(2,1)S(1)}, u32[]{:S(2)}, u32[]{:S(2)}) collective-permute-start(bf16[160,256]{1,0:T(8,128)(2,1)} %get-tuple-element.14), channel_id=1, source_target_pairs={{0,96},{1,97},{2,128},{3,129},{4,160},{5,161},{6,192},{7,193},{8,2... | collective-permute-start | bytes 245768 | tf_op jit(solution)/shard_map/ppermute | solution.py:22
  30.0 25.0 %collective-permute-start.15 = (bf16[160,256]{1,0:T(8,128)(2,1)}, bf16[160,256]{1,0:T(8,128)(2,1)S(1)}, u32[]{:S(2)}, u32[]{:S(2)}) collective-permute-start(bf16[160,256]{1,0:T(8,128)(2,1)} %get-tuple-element.13), channel_id=1, source_target_pairs={{0,64},{1,65},{2,96},{3,97},{4,128},{5,129},{6,160},{7,161},{8,192... | collective-permute-start | bytes 245768 | tf_op jit(solution)/shard_map/ppermute | solution.py:22
  47.0 21.1 %collective-permute-start.16 = (bf16[160,256]{1,0:T(8,128)(2,1)}, bf16[160,256]{1,0:T(8,128)(2,1)S(1)}, u32[]{:S(2)}, u32[]{:S(2)}) collective-permute-start(bf16[160,256]{1,0:T(8,128)(2,1)} %get-tuple-element.12), channel_id=1, source_target_pairs={{0,32},{1,33},{2,64},{3,65},{4,96},{5,97},{6,128},{7,129},{8,160},... | collective-permute-start | bytes 245768 | tf_op jit(solution)/shard_map/ppermute | solution.py:22
  47.1 20.9 %collective-permute-start.17 = (bf16[160,256]{1,0:T(8,128)(2,1)S(1)}, bf16[160,256]{1,0:T(8,128)(2,1)S(1)}, u32[]{:S(2)}, u32[]{:S(2)}) collective-permute-start(bf16[160,256]{1,0:T(8,128)(2,1)S(1)} %copy-done.5), channel_id=1, source_target_pairs={{0,0},{1,1},{2,32},{3,33},{4,64},{5,65},{6,96},{7,97},{8,128},{9,1... | collective-permute-start | bytes 245768 | tf_op jit(solution)/shard_map/ppermute | solution.py:22
  50.3 19.1 %collective-permute-start = (bf16[4,2,320,256]{3,2,1,0:T(8,128)(2,1)S(1)}, bf16[4,2,320,256]{3,2,1,0:T(8,128)(2,1)S(1)}, u32[]{:S(2)}, u32[]{:S(2)}) collective-permute-start(bf16[4,2,320,256]{3,2,1,0:T(8,128)(2,1)S(1)} %get-tuple-element.8), channel_id=1, source_target_pairs={{0,16},{1,17},{2,18},{3,19},{4,20},{5,21},{6,22},{7,23},{8,24},{9,... | collective-permute-start | bytes 3932168 | tf_op jit(solution)/shard_map/ppermute | solution.py:22
  68.1 1.2 copy-start.2
  72.8 63.5 %all-to-all-start = ((bf16[8,640,256]{2,1,0:T(8,128)(2,1)}), bf16[8,640,256]{2,1,0:T(8,128)(2,1)S(1)}, u32[]{:S(2)}, u32[]{:S(2)}) async-start(bf16[8,640,256]{2,1,0:T(8,128)(2,1)} %bitcast.82), calls=%async_computation | async-start | bytes 5242880 | tf_op jit(solution)/shard_map/all_to_all | solution.py:100
  79.6 1.8 copy-start.3
  82.4 39.7 %collective-permute-start.19 = (bf16[8,160,256]{2,1,0:T(8,128)(2,1)S(1)}, bf16[8,160,256]{2,1,0:T(8,128)(2,1)S(1)}, u32[]{:S(2)}, u32[]{:S(2)}) collective-permute-start(bf16[8,160,256]{2,1,0:T(8,128)(2,1)S(1)} %get-tuple-element.6), channel_id=1, source_target_pairs={{0,64},{1,65},{2,66},{3,67},{4,68},{5,69},{6,70},{7,71},{8,72},{9,... | collective-permute-start | bytes 1966088 | tf_op jit(solution)/shard_map/ppermute | solution.py:22
  83.8 39.0 %collective-permute-start.18 = (bf16[8,160,256]{2,1,0:T(8,128)(2,1)S(1)}, bf16[8,160,256]{2,1,0:T(8,128)(2,1)S(1)}, u32[]{:S(2)}, u32[]{:S(2)}) collective-permute-start(bf16[8,160,256]{2,1,0:T(8,128)(2,1)S(1)} %get-tuple-element.6), channel_id=1, source_target_pairs={{0,192},{1,193},{2,194},{3,195},{4,196},{5,197},{6,198},{7,199},{8... | collective-permute-start | bytes 1966088 | tf_op jit(solution)/shard_map/ppermute | solution.py:22
  122.8 9.7 %collective-permute-start.20 = (bf16[4,160,256]{2,1,0:T(8,128)(2,1)}, bf16[4,160,256]{2,1,0:T(8,128)(2,1)}, u32[]{:S(2)}, u32[]{:S(2)}) collective-permute-start(bf16[4,160,256]{2,1,0:T(8,128)(2,1)} %slice.100), channel_id=1, source_target_pairs={{0,64},{1,65},{2,66},{3,67},{4,68},{5,69},{6,70},{7,71},{8,72},{9,... | collective-permute-start | bytes 983048 | tf_op jit(solution)/shard_map/ppermute | solution.py:22
  122.8 0.9 copy-start.1
  124.4 9.0 %collective-permute-start.21 = (bf16[4,160,256]{2,1,0:T(8,128)(2,1)}, bf16[4,160,256]{2,1,0:T(8,128)(2,1)}, u32[]{:S(2)}, u32[]{:S(2)}) collective-permute-start(bf16[4,160,256]{2,1,0:T(8,128)(2,1)} %slice.101), channel_id=1, source_target_pairs={{0,192},{1,193},{2,194},{3,195},{4,196},{5,197},{6,198},{7,199},{8... | collective-permute-start | bytes 983048 | tf_op jit(solution)/shard_map/ppermute | solution.py:22
  136.2 42.2 %collective-permute-start.22 = (bf16[8,640,256]{2,1,0:T(8,128)(2,1)}, bf16[8,640,256]{2,1,0:T(8,128)(2,1)}, u32[]{:S(2)}, u32[]{:S(2)}) collective-permute-start(bf16[8,640,256]{2,1,0:T(8,128)(2,1)} %constant_dynamic-update-slice_fusion.2), channel_id=1, source_target_pairs={{0,16},{1,17},{2,18},{3,19},{4,20},{5,21},{6,22},{7,23},{8,24},{9,... | collective-permute-start | bytes 7864328 | tf_op jit(solution)/shard_map/ppermute | solution.py:22
  136.9 10.8 %collective-permute-start.2 = (bf16[640,256]{1,0:T(8,128)(2,1)S(1)}, bf16[640,256]{1,0:T(8,128)(2,1)S(1)}, u32[]{:S(2)}, u32[]{:S(2)}) collective-permute-start(bf16[640,256]{1,0:T(8,128)(2,1)S(1)} %maximum_select_fusion.1), channel_id=1, source_target_pairs={{0,14},{1,15},{2,0},{3,1},{4,2},{5,3},{6,4},{7,5},{8,6},{9,7},{10,... | collective-permute-start | bytes 983048 | tf_op jit(solution)/shard_map/ppermute | solution.py:22
  140.0 11.3 %collective-permute-start.6 = (bf16[640,256]{1,0:T(8,128)(2,1)S(1)}, bf16[640,256]{1,0:T(8,128)(2,1)S(1)}, u32[]{:S(2)}, u32[]{:S(2)}) collective-permute-start(bf16[640,256]{1,0:T(8,128)(2,1)S(1)} %maximum_select_fusion.1), channel_id=1, source_target_pairs={{0,2},{1,3},{2,4},{3,5},{4,6},{5,7},{6,8},{7,9},{8,10},{9,11},{10,... | collective-permute-start | bytes 983048 | tf_op jit(solution)/shard_map/ppermute | solution.py:22
  147.7 11.6 %collective-permute-start.3 = (bf16[640,256]{1,0:T(8,128)(2,1)S(1)}, bf16[640,256]{1,0:T(8,128)(2,1)S(1)}, u32[]{:S(2)}, u32[]{:S(2)}) collective-permute-start(bf16[640,256]{1,0:T(8,128)(2,1)S(1)} %collective-permute-done.2), channel_id=1, source_target_pairs={{0,14},{1,15},{2,0},{3,1},{4,2},{5,3},{6,4},{7,5},{8,6},{9,7},{10,... | collective-permute-start | bytes 983048 | tf_op jit(solution)/shard_map/ppermute | solution.py:22
  151.4 10.6 %collective-permute-start.7 = (bf16[640,256]{1,0:T(8,128)(2,1)S(1)}, bf16[640,256]{1,0:T(8,128)(2,1)S(1)}, u32[]{:S(2)}, u32[]{:S(2)}) collective-permute-start(bf16[640,256]{1,0:T(8,128)(2,1)S(1)} %collective-permute-done.6), channel_id=1, source_target_pairs={{0,2},{1,3},{2,4},{3,5},{4,6},{5,7},{6,8},{7,9},{8,10},{9,11},{10,... | collective-permute-start | bytes 983048 | tf_op jit(solution)/shard_map/ppermute | solution.py:22
  159.3 9.0 %collective-permute-start.4 = (bf16[640,256]{1,0:T(8,128)(2,1)S(1)}, bf16[640,256]{1,0:T(8,128)(2,1)S(1)}, u32[]{:S(2)}, u32[]{:S(2)}) collective-permute-start(bf16[640,256]{1,0:T(8,128)(2,1)S(1)} %collective-permute-done.3), channel_id=1, source_target_pairs={{0,14},{1,15},{2,0},{3,1},{4,2},{5,3},{6,4},{7,5},{8,6},{9,7},{10,... | collective-permute-start | bytes 983048 | tf_op jit(solution)/shard_map/ppermute | solution.py:22
  161.9 9.8 %collective-permute-start.8 = (bf16[640,256]{1,0:T(8,128)(2,1)S(1)}, bf16[640,256]{1,0:T(8,128)(2,1)S(1)}, u32[]{:S(2)}, u32[]{:S(2)}) collective-permute-start(bf16[640,256]{1,0:T(8,128)(2,1)S(1)} %collective-permute-done.7), channel_id=1, source_target_pairs={{0,2},{1,3},{2,4},{3,5},{4,6},{5,7},{6,8},{7,9},{8,10},{9,11},{10,... | collective-permute-start | bytes 983048 | tf_op jit(solution)/shard_map/ppermute | solution.py:22
  168.3 6.2 %collective-permute-start.5 = (bf16[320,256]{1,0:T(8,128)(2,1)S(1)}, bf16[320,256]{1,0:T(8,128)(2,1)S(1)}, u32[]{:S(2)}, u32[]{:S(2)}) collective-permute-start(bf16[320,256]{1,0:T(8,128)(2,1)S(1)} %slice.90), channel_id=1, source_target_pairs={{0,14},{1,15},{2,0},{3,1},{4,2},{5,3},{6,4},{7,5},{8,6},{9,7},{10,... | collective-permute-start | bytes 491528 | tf_op jit(solution)/shard_map/ppermute | solution.py:22
  171.7 6.6 %collective-permute-start.9 = (bf16[320,256]{1,0:T(8,128)(2,1)S(1)}, bf16[320,256]{1,0:T(8,128)(2,1)S(1)}, u32[]{:S(2)}, u32[]{:S(2)}) collective-permute-start(bf16[320,256]{1,0:T(8,128)(2,1)S(1)} %slice.91), channel_id=1, source_target_pairs={{0,2},{1,3},{2,4},{3,5},{4,6},{5,7},{6,8},{7,9},{8,10},{9,11},{10,... | collective-permute-start | bytes 491528 | tf_op jit(solution)/shard_map/ppermute | solution.py:22
  182.5 6.6 %collective-permute-start.23 = (bf16[160,640]{1,0:T(8,128)(2,1)S(1)}, bf16[160,640]{1,0:T(8,128)(2,1)S(1)}, u32[]{:S(2)}, u32[]{:S(2)}) collective-permute-start(bf16[160,640]{1,0:T(8,128)(2,1)S(1)} %get-tuple-element.9), channel_id=1, source_target_pairs={{0,32},{1,33},{2,34},{3,35},{4,36},{5,37},{6,38},{7,39},{8,40},{9,... | collective-permute-start | bytes 614408 | tf_op jit(solution)/shard_map/ppermute | solution.py:22
  183.3 8.3 %collective-permute-start.25 = (bf16[160,640]{1,0:T(8,128)(2,1)S(1)}, bf16[160,640]{1,0:T(8,128)(2,1)S(1)}, u32[]{:S(2)}, u32[]{:S(2)}) collective-permute-start(bf16[160,640]{1,0:T(8,128)(2,1)S(1)} %get-tuple-element.10), channel_id=1, source_target_pairs={{0,33},{1,32},{2,35},{3,34},{4,37},{5,36},{6,39},{7,38},{8,41},{9,... | collective-permute-start | bytes 614408 | tf_op jit(solution)/shard_map/ppermute | solution.py:22
  189.1 9.9 %collective-permute-start.24 = (bf16[320,640]{1,0:T(8,128)(2,1)S(1)}, bf16[320,640]{1,0:T(8,128)(2,1)S(1)}, u32[]{:S(2)}, u32[]{:S(2)}) collective-permute-start(bf16[320,640]{1,0:T(8,128)(2,1)S(1)} %fusion.13), channel_id=1, source_target_pairs={{0,33},{1,32},{2,35},{3,34},{4,37},{5,36},{6,39},{7,38},{8,41},{9,... | collective-permute-start | bytes 1228808 | tf_op jit(solution)/shard_map/ppermute | solution.py:22
  191.6 8.0 %collective-permute-start.26 = (bf16[320,640]{1,0:T(8,128)(2,1)S(1)}, bf16[320,640]{1,0:T(8,128)(2,1)S(1)}, u32[]{:S(2)}, u32[]{:S(2)}) collective-permute-start(bf16[320,640]{1,0:T(8,128)(2,1)S(1)} %fusion.12), channel_id=1, source_target_pairs={{0,32},{1,33},{2,34},{3,35},{4,36},{5,37},{6,38},{7,39},{8,40},{9,... | collective-permute-start | bytes 1228808 | tf_op jit(solution)/shard_map/ppermute | solution.py:22

commit v2 on v1

--- a/solution.py
+++ b/solution.py
@@ -26,20 +26,12 @@
     return y, xl, 1 - co, z, xh
 
 
-def y_up(y, xl, co, z, xh):
-    return (y + 1) % 4, xl, co, z, xh
+def z_by(step):
+    return lambda y, xl, co, z, xh: (y, xl, co, (z + step) % 8, xh)
 
 
-def y_down(y, xl, co, z, xh):
-    return (y - 1) % 4, xl, co, z, xh
-
-
-def z_up(y, xl, co, z, xh):
-    return y, xl, co, (z + 1) % 8, xh
-
-
-def z_down(y, xl, co, z, xh):
-    return y, xl, co, (z - 1) % 8, xh
+def y_by(step):
+    return lambda y, xl, co, z, xh: ((y + step) % 4, xl, co, z, xh)
 
 
 def in_run(y, xl, co, z, xh):
@@ -50,14 +42,6 @@
     return y, 1 - xl, co, z, 1 - xh
 
 
-def dispatch(j):
-    def move(y, xl, co, z, xh):
-        p = (z + j) % 8
-        return p // 2, p % 2, co, 2 * y + xl, xh
-
-    return move
-
-
 def rotated(stack, start):
     n = stack.shape[0]
     return lax.dynamic_slice_in_dim(jnp.concatenate([stack, stack]), start, n, 0)
@@ -65,13 +49,12 @@
 
 def dot_f32(left, right):
     return lax.dot_general(
-        left, right, (((0, 2), (0, 2)), ((), ())), preferred_element_type=jnp.float32
+        left, right, (((1,), (1,)), ((), ())), preferred_element_type=jnp.float32
     )
 
 
 def on_device(weight_tiles, expand_rows, expand_cols):
     y, xl, co, z, xh = (lax.axis_index(a) for a in AXES)
-    p = 2 * y + xl
     bf16 = jnp.bfloat16
     k1, width = weight_tiles.shape
     half = width // 2
@@ -86,8 +69,9 @@
     got_tiles = send(weight_tiles, other_core)
 
     pieces = expand_cols.reshape(4, quarter, 2, half).transpose(0, 2, 1, 3)
-    pieces = rotated(pieces.reshape(8, quarter, half), z)
-    got = [send(pieces[j], dispatch(j)) for j in range(8)]
+    pieces = pieces.reshape(8, quarter, half)
+    got_rows, got_tiles, pieces = lax.optimization_barrier((got_rows, got_tiles, pieces))
+    pieces = lax.all_to_all(pieces, ("y", "xl"), 0, 0, tiled=True)
 
     left = jnp.concatenate([mine, got_rows], -1).reshape(8 * m, 2 * k1)
     right = jnp.concatenate([weight_tiles, got_tiles], 0)
@@ -97,27 +81,34 @@
         for i in range(2)
     ]
     part = jnp.stack(part, 1).reshape(8, 2 * m, half)
+    pieces = rotated(pieces, z)
+    part, pieces = lax.optimization_barrier((part, pieces))
     part = lax.all_to_all(part, ("y", "xl"), 0, 0, tiled=True)
+    got = [pieces[0]] + [send(pieces[-i % 8], z_by(-i)) for i in range(1, 8)]
     inner = jnp.sum(part.astype(jnp.float32), 0).astype(bf16)
     inner = jnp.where(xl == 0, inner, jnp.concatenate([inner[m:], inner[:m]]))
 
-    cols = rotated(jnp.stack(got[::-1]), (7 - p + z) % 8)
-    below = send(cols, y_up)
-    above = send(cols, y_down)
-    far = jnp.concatenate([send(below[:4], y_up), send(above[4:], y_down)])
-    full = jnp.zeros((8, n, half), bf16)
+    cols = jnp.concatenate(got, 1)
+    below = send(cols, y_by(1))
+    above = send(cols, y_by(-1))
+    far = jnp.concatenate([send(below[:, : 4 * half], y_by(1)), send(above[:, 4 * half :], y_by(-1))], 1)
+    full = jnp.zeros((n, 8 * half), bf16)
     for shift, block in ((0, cols), (1, above), (2, far), (3, below)):
-        full = lax.dynamic_update_slice_in_dim(full, block, (y + shift) % 4 * quarter, 1)
+        full = lax.dynamic_update_slice_in_dim(full, block, (y + shift) % 4 * quarter, 0)
+    slots = [inner] + [None] * 7
+    up = down = inner
+    for i in range(1, 4):
+        up, down = send(up, z_by(-1)), send(down, z_by(1))
+        if i < 3:
+            up, down = lax.optimization_barrier((up, down))
+        else:
+            up, down, full = lax.optimization_barrier((up, down, full))
+        slots[i], slots[-i] = up, down
     other = send(full, other_core)
+    slots[4] = jnp.concatenate([send(up[:m], z_by(-1)), send(down[m:], z_by(1))])
+    inner_all = jnp.concatenate(slots, 1)
     near_cols = jnp.where(xh == co, full, other)
     far_cols = jnp.where(xh == co, other, full)
-
-    slots = [inner] + [None] * 7
-    for i in range(1, 4):
-        slots[i] = send(slots[i - 1], z_down)
-        slots[-i] = send(slots[(-i + 1) % 8], z_up)
-    slots[4] = jnp.concatenate([send(slots[3][:m], z_down), send(slots[5][m:], z_up)])
-    inner_all = jnp.stack(slots)
 
     cross = dot_f32(inner_all, far_cols)
     cut = m // 2

time: 203 us -> 142 us (0.70)
  waiting for transfers between devices: 103 us -> 42.6 us
  starting transfers between devices: 66.4 us -> 56.7 us
  local copies, waits for them, and re-layouts: 15.2 us -> 23.6 us
  matrix products: 9.66 us -> 12.4 us
    ppermute x27 -> x26, waiting for transfers between devices: 103 us -> 38.9 us  [send(): return lax.ppermute(value, AXES, pairs(move))]
    ppermute x27 -> x26, starting transfers between devices: 62.2 us -> 46.1 us  [send(): return lax.ppermute(value, AXES, pairs(move))]
    unnamed x33 -> x29, local copies, waits for them, and re-layouts: 3.11 us -> 10.5 us
    all_to_all x0 -> x1, starting transfers between devices: none -> 5.93 us  [on_device(): pieces = lax.all_to_all(pieces, ('y', 'xl'), 0, 0, tiled=True)]
    all_to_all x0 -> x1, waiting for transfers between devices: none -> 3.62 us  [on_device(): pieces = lax.all_to_all(pieces, ('y', 'xl'), 0, 0, tiled=True)]
    dot_general x2, matrix products: 1.68 us -> 4.31 us  [on_device(): jnp.dot(left, right[:, i * half:(i + 1) * half], preferred_element_type=j...]
  transfers between devices with their start and end apart: 28 -> 28, of which waited for: 14 -> 16; matrix products, arithmetic and copies ran while one was open for 9% -> 24% of each run, Pallas kernels for 0% -> 0%
where the time goes in v2:
time: 142 us; the launch traced here: 141 us
  starting transfers between devices  56.7 us (40%)
  waiting for transfers between devices  42.6 us (30%)
  local copies, waits for them, and re-layouts  23.6 us (17%)
  matrix products  12.4 us (9%)
  other arithmetic  5.2 us (4%)
    ppermute x26, starting transfers between devices, send(): return lax.ppermute(value, AXES, pairs(move))  46.1 us
    ppermute x26, waiting for transfers between devices, send(): return lax.ppermute(value, AXES, pairs(move))  38.9 us
    unnamed x29, local copies, waits for them, and re-layouts  10.5 us
    dot_general x2, matrix products, dot_f32(): lax.dot_general(left, right, (((1,), (1,)), ((), ())), preferred_element_...  8.09 us
    all_to_all x1, starting transfers between devices, on_device(): pieces = lax.all_to_all(pieces, ('y', 'xl'), 0, 0, tiled=True)  5.93 us
    all_to_all x1, starting transfers between devices, on_device(): part = lax.all_to_all(part, ('y', 'xl'), 0, 0, tiled=True)  4.71 us
    dot_general x2, matrix products, on_device(): jnp.dot(left, right[:, i * half:(i + 1) * half], preferred_element_type=j...  4.31 us
    all_to_all x1, waiting for transfers between devices, on_device(): pieces = lax.all_to_all(pieces, ('y', 'xl'), 0, 0, tiled=True)  3.62 us
  transfers between devices with their start and end apart: 28, of which 16 were waited for; matrix products, arithmetic and copies ran while one was open for 24% of the time, Pallas kernels for 0%

profile of v2, /device:TPU:6, one launch (start us, length us, event | category | flops | bytes accessed | tf_op | source)
XLA Modules:
  0.0 140.8 jit_solution(11598558877223881751)
XLA Ops:
  0.0 1.9 %constant_dynamic-slice_fusion = (bf16[4,2,1,320,256]{4,3,2,1,0:T(8,128)(2,1)S(1)}, bf16[4,2,320,256]{3,2,1,0:T(8,128)(2,1)S(1)}) fusion(bf16[4,2,2,320,256]{4,3,2,1,0:T(8,128)(2,1)} %bitcast.33, s32[]{:T(128)S(6)} %select_n.62, s32[]{:T(128)S(6)} %select_n.63), kind=kLoop, calls=%fused_computation.53 | loop fusion | bytes 5242888 | tf_op jit(solution)/shard_map/jit(dynamic_index_in_dim)/dynamic_slice | solution.py:66
  2.5 2.0 %reshape.17 = bf16[4,160,2,256]{3,2,1,0:T(2,128)(2,1)S(1)} reshape(bf16[640,512]{1,0:T(8,128)(2,1)} %param.5) | data formatting | bytes 1310720 | tf_op jit(solution)/shard_map/reshape | solution.py:71
  4.6 0.9 copy.6
  5.6 5.9 %all-to-all-start = ((bf16[8,160,256]{2,1,0:T(8,128)(2,1)}), bf16[8,160,256]{2,1,0:T(8,128)(2,1)S(1)}, u32[]{:S(2)}, u32[]{:S(2)}) async-start(bf16[8,160,256]{2,1,0:T(8,128)(2,1)} %bitcast.4), calls=%async_computation | async-start | bytes 1310720 | tf_op jit(solution)/shard_map/all_to_all | solution.py:74
  11.5 1.0 constant_dynamic-update-slice_fusion
  12.5 2.2 %convolution_convert_fusion.1 = bf16[2560,256]{1,0:T(8,128)(2,1)S(1)} fusion(bf16[2560,256]{1,0:T(8,128)(2,1)} %bitcast.5, bf16[2560,256]{1,0:T(8,128)(2,1)S(1)} %bitcast.36, bf16[512,512]{1,0:T(8,128)(2,1)S(1)} %constant_dynamic-update-slice_fusion), kind=kOutput, calls=%fused_computation.1 | convolution fusion | flops 676986880 | bytes 4194304 | tf_op jit(solution)/shard_map/dot_general | solution.py:79
  14.6 2.2 %convolution_convert_fusion = bf16[2560,256]{1,0:T(8,128)(2,1)S(1)} fusion(bf16[2560,256]{1,0:T(8,128)(2,1)} %bitcast.5, bf16[2560,256]{1,0:T(8,128)(2,1)S(1)} %bitcast.37, bf16[512,512]{1,0:T(8,128)(2,1)S(1)} %constant_dynamic-update-slice_fusion), kind=kOutput, calls=%fused_computation | convolution fusion | flops 676986880 | bytes 4194304 | tf_op jit(solution)/shard_map/dot_general | solution.py:79
  16.8 1.7 %pad_maximum_fusion.1 = bf16[4,2,640,256]{3,2,1,0:T(8,128)(2,1)} fusion(bf16[4,1,640,256]{3,2,1,0:T(8,128)(2,1)S(1)} %bitcast.35, bf16[4,1,640,256]{3,2,1,0:T(8,128)(2,1)S(1)} %bitcast.34), kind=kLoop, calls=%fused_computation.3 | loop fusion | flops 1310720 | bytes 5242880 | tf_op jit(solution)/shard_map/stack | solution.py:83
  18.5 3.6 %all-to-all-done = bf16[8,160,256]{2,1,0:T(8,128)(2,1)S(1)} async-done(((bf16[8,160,256]{2,1,0:T(8,128)(2,1)}), bf16[8,160,256]{2,1,0:T(8,128)(2,1)S(1)}, u32[]{:S(2)}, u32[]{:S(2)}) %all-to-all-start) | async-done | bytes 655392 | tf_op jit(solution)/shard_map/all_to_all | solution.py:74
  22.4 4.7 %all-to-all-start.1 = ((bf16[8,640,256]{2,1,0:T(8,128)(2,1)}), bf16[8,640,256]{2,1,0:T(8,128)(2,1)S(1)}, u32[]{:S(2)}, u32[]{:S(2)}) async-start(bf16[8,640,256]{2,1,0:T(8,128)(2,1)} %bitcast.10), calls=%async_computation.1 | async-start | bytes 5242880 | tf_op jit(solution)/shard_map/all_to_all | solution.py:86
  27.1 5.9 %collective-permute-start.8 = (bf16[160,256]{1,0:T(8,128)(2,1)S(1)}, bf16[160,256]{1,0:T(8,128)(2,1)S(1)}, u32[]{:S(2)}, u32[]{:S(2)}) collective-permute-start(bf16[160,256]{1,0:T(8,128)(2,1)S(1)} %get-tuple-element.41), channel_id=1, source_target_pairs={{0,14},{1,15},{2,0},{3,1},{4,2},{5,3},{6,4},{7,5},{8,6},{9,7},{10,... | collective-permute-start | bytes 245768 | tf_op jit(solution)/shard_map/ppermute | solution.py:22
  33.7 1.5 %collective-permute-start.9 = (bf16[160,256]{1,0:T(8,128)(2,1)S(1)}, bf16[160,256]{1,0:T(8,128)(2,1)S(1)}, u32[]{:S(2)}, u32[]{:S(2)}) collective-permute-start(bf16[160,256]{1,0:T(8,128)(2,1)S(1)} %get-tuple-element.40), channel_id=1, source_target_pairs={{0,12},{1,13},{2,14},{3,15},{4,0},{5,1},{6,2},{7,3},{8,4},{9,5},{1... | collective-permute-start | bytes 245768 | tf_op jit(solution)/shard_map/ppermute | solution.py:22
  35.6 5.0 %collective-permute-start.11 = (bf16[160,256]{1,0:T(8,128)(2,1)S(1)}, bf16[160,256]{1,0:T(8,128)(2,1)S(1)}, u32[]{:S(2)}, u32[]{:S(2)}) collective-permute-start(bf16[160,256]{1,0:T(8,128)(2,1)S(1)} %get-tuple-element.38), channel_id=1, source_target_pairs={{0,8},{1,9},{2,10},{3,11},{4,12},{5,13},{6,14},{7,15},{8,0},{9,1},... | collective-permute-start | bytes 245768 | tf_op jit(solution)/shard_map/ppermute | solution.py:22
  40.6 2.5 %collective-permute-start.13 = (bf16[160,256]{1,0:T(8,128)(2,1)S(1)}, bf16[160,256]{1,0:T(8,128)(2,1)S(1)}, u32[]{:S(2)}, u32[]{:S(2)}) collective-permute-start(bf16[160,256]{1,0:T(8,128)(2,1)S(1)} %get-tuple-element.36), channel_id=1, source_target_pairs={{0,4},{1,5},{2,6},{3,7},{4,8},{5,9},{6,10},{7,11},{8,12},{9,13},{1... | collective-permute-start | bytes 245768 | tf_op jit(solution)/shard_map/ppermute | solution.py:22
  43.8 1.9 %collective-permute-start.14 = (bf16[160,256]{1,0:T(8,128)(2,1)S(1)}, bf16[160,256]{1,0:T(8,128)(2,1)S(1)}, u32[]{:S(2)}, u32[]{:S(2)}) collective-permute-start(bf16[160,256]{1,0:T(8,128)(2,1)S(1)} %get-tuple-element.35), channel_id=1, source_target_pairs={{0,2},{1,3},{2,4},{3,5},{4,6},{5,7},{6,8},{7,9},{8,10},{9,11},{10,... | collective-permute-start | bytes 245768 | tf_op jit(solution)/shard_map/ppermute | solution.py:22
  48.1 3.5 %collective-permute-done.12 = bf16[160,256]{1,0:T(8,128)(2,1)S(1)} collective-permute-done((bf16[160,256]{1,0:T(8,128)(2,1)S(1)}, bf16[160,256]{1,0:T(8,128)(2,1)S(1)}, u32[]{:S(2)}, u32[]{:S(2)}) %collective-permute-start.12) | collective-permute-done | bytes 81952 | tf_op jit(solution)/shard_map/ppermute | solution.py:22
  52.2 2.1 %collective-permute-done.13 = bf16[160,256]{1,0:T(8,128)(2,1)S(1)} collective-permute-done((bf16[160,256]{1,0:T(8,128)(2,1)S(1)}, bf16[160,256]{1,0:T(8,128)(2,1)S(1)}, u32[]{:S(2)}, u32[]{:S(2)}) %collective-permute-start.13) | collective-permute-done | bytes 81952 | tf_op jit(solution)/shard_map/ppermute | solution.py:22
  55.6 2.7 %collective-permute-start.15 = (bf16[160,2048]{1,0:T(8,128)(2,1)}, bf16[160,2048]{1,0:T(8,128)(2,1)}, u32[]{:S(2)}, u32[]{:S(2)}) collective-permute-start(bf16[160,2048]{1,0:T(8,128)(2,1)} %constant_dynamic-update-slice_fusion.2), channel_id=1, source_target_pairs={{0,192},{1,193},{2,194},{3,195},{4,196},{5,197},{6,198},{7,199},{8... | collective-permute-start | bytes 1966088 | tf_op jit(solution)/shard_map/ppermute | solution.py:22
  58.8 0.8 constant_dynamic-update-slice_fusion.15
  59.7 7.5 %collective-permute-start.2 = (bf16[640,256]{1,0:T(8,128)(2,1)S(1)}, bf16[640,256]{1,0:T(8,128)(2,1)S(1)}, u32[]{:S(2)}, u32[]{:S(2)}) collective-permute-start(bf16[640,256]{1,0:T(8,128)(2,1)S(1)} %get-tuple-element.30), channel_id=1, source_target_pairs={{0,14},{1,15},{2,0},{3,1},{4,2},{5,3},{6,4},{7,5},{8,6},{9,7},{10,... | collective-permute-start | bytes 983048 | tf_op jit(solution)/shard_map/ppermute | solution.py:22
  67.2 6.0 %collective-permute-done.16 = bf16[160,2048]{1,0:T(8,128)(2,1)} collective-permute-done((bf16[160,2048]{1,0:T(8,128)(2,1)}, bf16[160,2048]{1,0:T(8,128)(2,1)}, u32[]{:S(2)}, u32[]{:S(2)}) %collective-permute-start.16) | collective-permute-done | bytes 655392 | tf_op jit(solution)/shard_map/ppermute | solution.py:22
  73.2 1.0 slice.90
  74.3 1.0 slice.91
  75.3 3.3 %collective-permute-start.18 = (bf16[160,1024]{1,0:T(8,128)(2,1)S(1)}, bf16[160,1024]{1,0:T(8,128)(2,1)S(1)}, u32[]{:S(2)}, u32[]{:S(2)}) collective-permute-start(bf16[160,1024]{1,0:T(8,128)(2,1)S(1)} %slice.91), channel_id=1, source_target_pairs={{0,192},{1,193},{2,194},{3,195},{4,196},{5,197},{6,198},{7,199},{8... | collective-permute-start | bytes 983048 | tf_op jit(solution)/shard_map/ppermute | solution.py:22
  78.6 4.6 %collective-permute-start.4 = (bf16[640,256]{1,0:T(8,128)(2,1)S(1)}, bf16[640,256]{1,0:T(8,128)(2,1)S(1)}, u32[]{:S(2)}, u32[]{:S(2)}) collective-permute-start(bf16[640,256]{1,0:T(8,128)(2,1)S(1)} %collective-permute-done.2), channel_id=1, source_target_pairs={{0,14},{1,15},{2,0},{3,1},{4,2},{5,3},{6,4},{7,5},{8,6},{9,7},{10,... | collective-permute-start | bytes 983048 | tf_op jit(solution)/shard_map/ppermute | solution.py:22
  83.5 1.1 constant_dynamic-update-slice_fusion.18
  84.7 1.1 constant_dynamic-update-slice_fusion.17
  85.8 2.6 %collective-permute-done.4 = bf16[640,256]{1,0:T(8,128)(2,1)S(1)} collective-permute-done((bf16[640,256]{1,0:T(8,128)(2,1)S(1)}, bf16[640,256]{1,0:T(8,128)(2,1)S(1)}, u32[]{:S(2)}, u32[]{:S(2)}) %collective-permute-start.4) | collective-permute-done | bytes 327712 | tf_op jit(solution)/shard_map/ppermute | solution.py:22
  88.4 3.4 %collective-permute-done.5 = bf16[640,256]{1,0:T(8,128)(2,1)S(1)} collective-permute-done((bf16[640,256]{1,0:T(8,128)(2,1)S(1)}, bf16[640,256]{1,0:T(8,128)(2,1)S(1)}, u32[]{:S(2)}, u32[]{:S(2)}) %collective-permute-start.5) | collective-permute-done | bytes 327712 | tf_op jit(solution)/shard_map/ppermute | solution.py:22
  92.2 1.7 %collective-permute-start.7 = (bf16[640,256]{1,0:T(8,128)(2,1)S(1)}, bf16[640,256]{1,0:T(8,128)(2,1)S(1)}, u32[]{:S(2)}, u32[]{:S(2)}) collective-permute-start(bf16[640,256]{1,0:T(8,128)(2,1)S(1)} %collective-permute-done.5), channel_id=1, source_target_pairs={{0,2},{1,3},{2,4},{3,5},{4,6},{5,7},{6,8},{7,9},{8,10},{9,11},{10,... | collective-permute-start | bytes 983048 | tf_op jit(solution)/shard_map/ppermute | solution.py:22
  94.0 1.1 constant_dynamic-update-slice_fusion.16
  95.1 3.8 %collective-permute-done.6 = bf16[640,256]{1,0:T(8,128)(2,1)S(1)} collective-permute-done((bf16[640,256]{1,0:T(8,128)(2,1)S(1)}, bf16[640,256]{1,0:T(8,128)(2,1)S(1)}, u32[]{:S(2)}, u32[]{:S(2)}) %collective-permute-start.6) | collective-permute-done | bytes 327712 | tf_op jit(solution)/shard_map/ppermute | solution.py:22
  98.9 1.6 %collective-permute-done.7 = bf16[640,256]{1,0:T(8,128)(2,1)S(1)} collective-permute-done((bf16[640,256]{1,0:T(8,128)(2,1)S(1)}, bf16[640,256]{1,0:T(8,128)(2,1)S(1)}, u32[]{:S(2)}, u32[]{:S(2)}) %collective-permute-start.7) | collective-permute-done | bytes 327712 | tf_op jit(solution)/shard_map/ppermute | solution.py:22
  100.5 1.8 %constant_dynamic-update-slice_fusion.14 = bf16[640,2048]{1,0:T(8,128)(2,1)} fusion(bf16[640,2048]{1,0:T(8,128)(2,1)} %get-tuple-element.29, bf16[640,256]{1,0:T(8,128)(2,1)} %copy-done.2), kind=kLoop, calls=%fused_computation.48 | loop fusion | bytes 655360
  102.6 2.0 %collective-permute-start.20 = (bf16[320,256]{1,0:T(8,128)(2,1)S(1)}, bf16[320,256]{1,0:T(8,128)(2,1)S(1)}, u32[]{:S(2)}, u32[]{:S(2)}) collective-permute-start(bf16[320,256]{1,0:T(8,128)(2,1)S(1)} %slice.80), channel_id=1, source_target_pairs={{0,2},{1,3},{2,4},{3,5},{4,6},{5,7},{6,8},{7,9},{8,10},{9,11},{10,... | collective-permute-start | bytes 491528 | tf_op jit(solution)/shard_map/ppermute | solution.py:22
  104.6 1.7 %constant_dynamic-update-slice_fusion.13 = bf16[640,2048]{1,0:T(8,128)(2,1)} fusion(bf16[640,2048]{1,0:T(8,128)(2,1)} %constant_dynamic-update-slice_fusion.14, bf16[640,256]{1,0:T(8,128)(2,1)} %copy-done.5), kind=kLoop, calls=%fused_computation.47 | loop fusion | bytes 655360
  107.1 1.9 %collective-permute-done.19 = bf16[320,256]{1,0:T(8,128)(2,1)S(1)} collective-permute-done((bf16[320,256]{1,0:T(8,128)(2,1)S(1)}, bf16[320,256]{1,0:T(8,128)(2,1)S(1)}, u32[]{:S(2)}, u32[]{:S(2)}) %collective-permute-start.19) | collective-permute-done | bytes 163872 | tf_op jit(solution)/shard_map/ppermute | solution.py:22
  109.0 1.3 collective-permute-done.20
  112.0 0.8 constant_dynamic-update-slice_fusion.10
  113.6 4.1 %fusion.17 = (bf16[640,640]{1,0:T(8,128)(2,1)S(1)}, f32[640,640]{1,0:T(8,128)S(1)}) fusion(bf16[640,2048]{1,0:T(8,128)(2,1)} %constant_dynamic-update-slice_fusion.9, bf16[640,2048]{1,0:T(8,128)(2,1)} %collective-permute-done.21, bf16[640,2048]{1,0:T(8,128)(2,1)S(1)} %constant_dynamic-update-slice_fusion.16, pred[]{:T(512)S(6)} %eq.13), kind=kOutput, calls=%fused_computation.58 | convolution fusion | flops 1679441920 | bytes 10321921 | tf_op jit(solution)/shard_map/dot_general | solution.py:51
  117.7 3.6 %collective-permute-start.22 = (bf16[160,640]{1,0:T(8,128)(2,1)S(1)}, bf16[160,640]{1,0:T(8,128)(2,1)S(1)}, u32[]{:S(2)}, u32[]{:S(2)}) collective-permute-start(bf16[160,640]{1,0:T(8,128)(2,1)S(1)} %get-tuple-element.33), channel_id=1, source_target_pairs={{0,32},{1,33},{2,34},{3,35},{4,36},{5,37},{6,38},{7,39},{8,40},{9,... | collective-permute-start | bytes 614408 | tf_op jit(solution)/shard_map/ppermute | solution.py:22
  121.3 1.0 collective-permute-start.24
  122.4 4.0 %fusion.2 = f32[640,640]{1,0:T(8,128)S(1)} fusion(bf16[640,2048]{1,0:T(8,128)(2,1)S(1)} %copy-done.7, bf16[640,2048]{1,0:T(8,128)(2,1)S(1)} %constant_dynamic-update-slice_fusion.16, bf16[640,2048]{1,0:T(8,128)(2,1)} %collective-permute-done.21, pred[]{:T(512)S(6)} %eq.13), kind=kOutput, calls=%fused_computation.6 | convolution fusion | flops 1679032320 | bytes 9502721 | tf_op jit(solution)/shard_map/dot_general | solution.py:51
  126.8 1.2 collective-permute-start.23
  128.0 1.4 %collective-permute-done.24 = bf16[160,640]{1,0:T(8,128)(2,1)S(1)} collective-permute-done((bf16[160,640]{1,0:T(8,128)(2,1)S(1)}, bf16[160,640]{1,0:T(8,128)(2,1)S(1)}, u32[]{:S(2)}, u32[]{:S(2)}) %collective-permute-start.24) | collective-permute-done | bytes 204832 | tf_op jit(solution)/shard_map/ppermute | solution.py:22
  129.6 9.5 %collective-permute-done.23 = bf16[320,640]{1,0:T(8,128)(2,1)S(1)} collective-permute-done((bf16[320,640]{1,0:T(8,128)(2,1)S(1)}, bf16[320,640]{1,0:T(8,128)(2,1)S(1)}, u32[]{:S(2)}, u32[]{:S(2)}) %collective-permute-start.23) | collective-permute-done | bytes 409632 | tf_op jit(solution)/shard_map/ppermute | solution.py:22
  139.1 0.8 collective-permute-done.25
  139.9 0.9 fusion.9
  (67 shorter events, 12.5 us)
Async XLA Ops:
  0.0 2.0 %copy-start.6 = (bf16[256,512]{1,0:T(8,128)(2,1)S(1)}, bf16[256,512]{1,0:T(8,128)(2,1)}, u32[]{:S(2)}) copy-start(bf16[256,512]{1,0:T(8,128)(2,1)} %param.3) | copy-start | bytes 786436
  1.9 3.6 %collective-permute-start = (bf16[4,2,320,256]{3,2,1,0:T(8,128)(2,1)S(1)}, bf16[4,2,320,256]{3,2,1,0:T(8,128)(2,1)}, u32[]{:S(2)}, u32[]{:S(2)}) collective-permute-start(bf16[4,2,320,256]{3,2,1,0:T(8,128)(2,1)S(1)} %get-tuple-element.32), channel_id=1, source_target_pairs={{0,16},{1,17},{2,18},{3,19},{4,20},{5,21},{6,22},{7,23},{8,24},{9,... | collective-permute-start | bytes 3932168 | tf_op jit(solution)/shard_map/ppermute | solution.py:22
  2.0 3.5 %collective-permute-start.1 = (bf16[256,512]{1,0:T(8,128)(2,1)S(1)}, bf16[256,512]{1,0:T(8,128)(2,1)}, u32[]{:S(2)}, u32[]{:S(2)}) collective-permute-start(bf16[256,512]{1,0:T(8,128)(2,1)S(1)} %copy-done.6), channel_id=1, source_target_pairs={{0,16},{1,17},{2,18},{3,19},{4,20},{5,21},{6,22},{7,23},{8,24},{9,... | collective-permute-start | bytes 786440 | tf_op jit(solution)/shard_map/ppermute | solution.py:22
  5.6 16.6 %all-to-all-start = ((bf16[8,160,256]{2,1,0:T(8,128)(2,1)}), bf16[8,160,256]{2,1,0:T(8,128)(2,1)S(1)}, u32[]{:S(2)}, u32[]{:S(2)}) async-start(bf16[8,160,256]{2,1,0:T(8,128)(2,1)} %bitcast.4), calls=%async_computation | async-start | bytes 1310720 | tf_op jit(solution)/shard_map/all_to_all | solution.py:74
  22.4 35.9 %all-to-all-start.1 = ((bf16[8,640,256]{2,1,0:T(8,128)(2,1)}), bf16[8,640,256]{2,1,0:T(8,128)(2,1)S(1)}, u32[]{:S(2)}, u32[]{:S(2)}) async-start(bf16[8,640,256]{2,1,0:T(8,128)(2,1)} %bitcast.10), calls=%async_computation.1 | async-start | bytes 5242880 | tf_op jit(solution)/shard_map/all_to_all | solution.py:86
  27.1 13.5 %collective-permute-start.8 = (bf16[160,256]{1,0:T(8,128)(2,1)S(1)}, bf16[160,256]{1,0:T(8,128)(2,1)S(1)}, u32[]{:S(2)}, u32[]{:S(2)}) collective-permute-start(bf16[160,256]{1,0:T(8,128)(2,1)S(1)} %get-tuple-element.41), channel_id=1, source_target_pairs={{0,14},{1,15},{2,0},{3,1},{4,2},{5,3},{6,4},{7,5},{8,6},{9,7},{10,... | collective-permute-start | bytes 245768 | tf_op jit(solution)/shard_map/ppermute | solution.py:22
  33.7 10.1 %collective-permute-start.9 = (bf16[160,256]{1,0:T(8,128)(2,1)S(1)}, bf16[160,256]{1,0:T(8,128)(2,1)S(1)}, u32[]{:S(2)}, u32[]{:S(2)}) collective-permute-start(bf16[160,256]{1,0:T(8,128)(2,1)S(1)} %get-tuple-element.40), channel_id=1, source_target_pairs={{0,12},{1,13},{2,14},{3,15},{4,0},{5,1},{6,2},{7,3},{8,4},{9,5},{1... | collective-permute-start | bytes 245768 | tf_op jit(solution)/shard_map/ppermute | solution.py:22
  35.1 11.5 %collective-permute-start.10 = (bf16[160,256]{1,0:T(8,128)(2,1)S(1)}, bf16[160,256]{1,0:T(8,128)(2,1)S(1)}, u32[]{:S(2)}, u32[]{:S(2)}) collective-permute-start(bf16[160,256]{1,0:T(8,128)(2,1)S(1)} %get-tuple-element.39), channel_id=1, source_target_pairs={{0,10},{1,11},{2,12},{3,13},{4,14},{5,15},{6,0},{7,1},{8,2},{9,3},... | collective-permute-start | bytes 245768 | tf_op jit(solution)/shard_map/ppermute | solution.py:22
  35.6 11.8 %collective-permute-start.11 = (bf16[160,256]{1,0:T(8,128)(2,1)S(1)}, bf16[160,256]{1,0:T(8,128)(2,1)S(1)}, u32[]{:S(2)}, u32[]{:S(2)}) collective-permute-start(bf16[160,256]{1,0:T(8,128)(2,1)S(1)} %get-tuple-element.38), channel_id=1, source_target_pairs={{0,8},{1,9},{2,10},{3,11},{4,12},{5,13},{6,14},{7,15},{8,0},{9,1},... | collective-permute-start | bytes 245768 | tf_op jit(solution)/shard_map/ppermute | solution.py:22
  40.6 10.9 %collective-permute-start.12 = (bf16[160,256]{1,0:T(8,128)(2,1)S(1)}, bf16[160,256]{1,0:T(8,128)(2,1)S(1)}, u32[]{:S(2)}, u32[]{:S(2)}) collective-permute-start(bf16[160,256]{1,0:T(8,128)(2,1)S(1)} %get-tuple-element.37), channel_id=1, source_target_pairs={{0,6},{1,7},{2,8},{3,9},{4,10},{5,11},{6,12},{7,13},{8,14},{9,15},... | collective-permute-start | bytes 245768 | tf_op jit(solution)/shard_map/ppermute | solution.py:22
  40.6 13.7 %collective-permute-start.13 = (bf16[160,256]{1,0:T(8,128)(2,1)S(1)}, bf16[160,256]{1,0:T(8,128)(2,1)S(1)}, u32[]{:S(2)}, u32[]{:S(2)}) collective-permute-start(bf16[160,256]{1,0:T(8,128)(2,1)S(1)} %get-tuple-element.36), channel_id=1, source_target_pairs={{0,4},{1,5},{2,6},{3,7},{4,8},{5,9},{6,10},{7,11},{8,12},{9,13},{1... | collective-permute-start | bytes 245768 | tf_op jit(solution)/shard_map/ppermute | solution.py:22
  43.8 11.2 %collective-permute-start.14 = (bf16[160,256]{1,0:T(8,128)(2,1)S(1)}, bf16[160,256]{1,0:T(8,128)(2,1)S(1)}, u32[]{:S(2)}, u32[]{:S(2)}) collective-permute-start(bf16[160,256]{1,0:T(8,128)(2,1)S(1)} %get-tuple-element.35), channel_id=1, source_target_pairs={{0,2},{1,3},{2,4},{3,5},{4,6},{5,7},{6,8},{7,9},{8,10},{9,11},{10,... | collective-permute-start | bytes 245768 | tf_op jit(solution)/shard_map/ppermute | solution.py:22
  55.6 18.7 %collective-permute-start.15 = (bf16[160,2048]{1,0:T(8,128)(2,1)}, bf16[160,2048]{1,0:T(8,128)(2,1)}, u32[]{:S(2)}, u32[]{:S(2)}) collective-permute-start(bf16[160,2048]{1,0:T(8,128)(2,1)} %constant_dynamic-update-slice_fusion.2), channel_id=1, source_target_pairs={{0,192},{1,193},{2,194},{3,195},{4,196},{5,197},{6,198},{7,199},{8... | collective-permute-start | bytes 1966088 | tf_op jit(solution)/shard_map/ppermute | solution.py:22
  58.3 14.9 %collective-permute-start.16 = (bf16[160,2048]{1,0:T(8,128)(2,1)}, bf16[160,2048]{1,0:T(8,128)(2,1)}, u32[]{:S(2)}, u32[]{:S(2)}) collective-permute-start(bf16[160,2048]{1,0:T(8,128)(2,1)} %constant_dynamic-update-slice_fusion.2), channel_id=1, source_target_pairs={{0,64},{1,65},{2,66},{3,67},{4,68},{5,69},{6,70},{7,71},{8,72},{9,... | collective-permute-start | bytes 1966088 | tf_op jit(solution)/shard_map/ppermute | solution.py:22
  59.7 18.9 %collective-permute-start.2 = (bf16[640,256]{1,0:T(8,128)(2,1)S(1)}, bf16[640,256]{1,0:T(8,128)(2,1)S(1)}, u32[]{:S(2)}, u32[]{:S(2)}) collective-permute-start(bf16[640,256]{1,0:T(8,128)(2,1)S(1)} %get-tuple-element.30), channel_id=1, source_target_pairs={{0,14},{1,15},{2,0},{3,1},{4,2},{5,3},{6,4},{7,5},{8,6},{9,7},{10,... | collective-permute-start | bytes 983048 | tf_op jit(solution)/shard_map/ppermute | solution.py:22
  67.2 11.4 %collective-permute-start.3 = (bf16[640,256]{1,0:T(8,128)(2,1)S(1)}, bf16[640,256]{1,0:T(8,128)(2,1)S(1)}, u32[]{:S(2)}, u32[]{:S(2)}) collective-permute-start(bf16[640,256]{1,0:T(8,128)(2,1)S(1)} %get-tuple-element.30), channel_id=1, source_target_pairs={{0,2},{1,3},{2,4},{3,5},{4,6},{5,7},{6,8},{7,9},{8,10},{9,11},{10,... | collective-permute-start | bytes 983048 | tf_op jit(solution)/shard_map/ppermute | solution.py:22
  74.2 19.7 %collective-permute-start.17 = (bf16[160,1024]{1,0:T(8,128)(2,1)S(1)}, bf16[160,1024]{1,0:T(8,128)(2,1)S(1)}, u32[]{:S(2)}, u32[]{:S(2)}) collective-permute-start(bf16[160,1024]{1,0:T(8,128)(2,1)S(1)} %slice.90), channel_id=1, source_target_pairs={{0,64},{1,65},{2,66},{3,67},{4,68},{5,69},{6,70},{7,71},{8,72},{9,... | collective-permute-start | bytes 983048 | tf_op jit(solution)/shard_map/ppermute | solution.py:22
  75.3 18.6 %collective-permute-start.18 = (bf16[160,1024]{1,0:T(8,128)(2,1)S(1)}, bf16[160,1024]{1,0:T(8,128)(2,1)S(1)}, u32[]{:S(2)}, u32[]{:S(2)}) collective-permute-start(bf16[160,1024]{1,0:T(8,128)(2,1)S(1)} %slice.91), channel_id=1, source_target_pairs={{0,192},{1,193},{2,194},{3,195},{4,196},{5,197},{6,198},{7,199},{8... | collective-permute-start | bytes 983048 | tf_op jit(solution)/shard_map/ppermute | solution.py:22
  78.6 7.2 %copy-start.2 = (bf16[640,256]{1,0:T(8,128)(2,1)}, bf16[640,256]{1,0:T(8,128)(2,1)S(1)}, u32[]{:S(2)}) copy-start(bf16[640,256]{1,0:T(8,128)(2,1)S(1)} %collective-permute-done.2) | copy-start | bytes 983044
  78.6 7.2 %copy-start = (bf16[640,256]{1,0:T(8,128)(2,1)}, bf16[640,256]{1,0:T(8,128)(2,1)S(1)}, u32[]{:S(2)}) copy-start(bf16[640,256]{1,0:T(8,128)(2,1)S(1)} %collective-permute-done.3) | copy-start | bytes 983044
  78.6 9.8 %collective-permute-start.4 = (bf16[640,256]{1,0:T(8,128)(2,1)S(1)}, bf16[640,256]{1,0:T(8,128)(2,1)S(1)}, u32[]{:S(2)}, u32[]{:S(2)}) collective-permute-start(bf16[640,256]{1,0:T(8,128)(2,1)S(1)} %collective-permute-done.2), channel_id=1, source_target_pairs={{0,14},{1,15},{2,0},{3,1},{4,2},{5,3},{6,4},{7,5},{8,6},{9,7},{10,... | collective-permute-start | bytes 983048 | tf_op jit(solution)/shard_map/ppermute | solution.py:22
  83.2 8.7 %collective-permute-start.5 = (bf16[640,256]{1,0:T(8,128)(2,1)S(1)}, bf16[640,256]{1,0:T(8,128)(2,1)S(1)}, u32[]{:S(2)}, u32[]{:S(2)}) collective-permute-start(bf16[640,256]{1,0:T(8,128)(2,1)S(1)} %collective-permute-done.3), channel_id=1, source_target_pairs={{0,2},{1,3},{2,4},{3,5},{4,6},{5,7},{6,8},{7,9},{8,10},{9,11},{10,... | collective-permute-start | bytes 983048 | tf_op jit(solution)/shard_map/ppermute | solution.py:22
  88.4 12.1 %copy-start.5 = (bf16[640,256]{1,0:T(8,128)(2,1)}, bf16[640,256]{1,0:T(8,128)(2,1)S(1)}, u32[]{:S(2)}) copy-start(bf16[640,256]{1,0:T(8,128)(2,1)S(1)} %collective-permute-done.4) | copy-start | bytes 983044
  91.9 8.6 %copy-start.3 = (bf16[640,256]{1,0:T(8,128)(2,1)}, bf16[640,256]{1,0:T(8,128)(2,1)S(1)}, u32[]{:S(2)}) copy-start(bf16[640,256]{1,0:T(8,128)(2,1)S(1)} %collective-permute-done.5) | copy-start | bytes 983044
  91.9 7.1 %collective-permute-start.6 = (bf16[640,256]{1,0:T(8,128)(2,1)S(1)}, bf16[640,256]{1,0:T(8,128)(2,1)S(1)}, u32[]{:S(2)}, u32[]{:S(2)}) collective-permute-start(bf16[640,256]{1,0:T(8,128)(2,1)S(1)} %collective-permute-done.4), channel_id=1, source_target_pairs={{0,14},{1,15},{2,0},{3,1},{4,2},{5,3},{6,4},{7,5},{8,6},{9,7},{10,... | collective-permute-start | bytes 983048 | tf_op jit(solution)/shard_map/ppermute | solution.py:22
  92.2 8.3 %collective-permute-start.7 = (bf16[640,256]{1,0:T(8,128)(2,1)S(1)}, bf16[640,256]{1,0:T(8,128)(2,1)S(1)}, u32[]{:S(2)}, u32[]{:S(2)}) collective-permute-start(bf16[640,256]{1,0:T(8,128)(2,1)S(1)} %collective-permute-done.5), channel_id=1, source_target_pairs={{0,2},{1,3},{2,4},{3,5},{4,6},{5,7},{6,8},{7,9},{8,10},{9,11},{10,... | collective-permute-start | bytes 983048 | tf_op jit(solution)/shard_map/ppermute | solution.py:22
  100.5 13.1 %collective-permute-start.21 = (bf16[640,2048]{1,0:T(8,128)(2,1)S(1)}, bf16[640,2048]{1,0:T(8,128)(2,1)}, u32[]{:S(2)}, u32[]{:S(2)}) collective-permute-start(bf16[640,2048]{1,0:T(8,128)(2,1)S(1)} %constant_dynamic-update-slice_fusion.16), channel_id=1, source_target_pairs={{0,16},{1,17},{2,18},{3,19},{4,20},{5,21},{6,22},{7,23},{8,24},{9,... | collective-permute-start | bytes 7864328 | tf_op jit(solution)/shard_map/ppermute | solution.py:22
  100.5 11.5 %copy-start.4 = (bf16[640,256]{1,0:T(8,128)(2,1)S(1)}, bf16[640,256]{1,0:T(8,128)(2,1)}, u32[]{:S(2)}) copy-start(bf16[640,256]{1,0:T(8,128)(2,1)} %copy-done.3) | copy-start | bytes 983044
  100.5 12.3 %copy-start.1 = (bf16[640,256]{1,0:T(8,128)(2,1)S(1)}, bf16[640,256]{1,0:T(8,128)(2,1)}, u32[]{:S(2)}) copy-start(bf16[640,256]{1,0:T(8,128)(2,1)} %copy-done) | copy-start | bytes 983044
  102.4 6.7 %collective-permute-start.19 = (bf16[320,256]{1,0:T(8,128)(2,1)S(1)}, bf16[320,256]{1,0:T(8,128)(2,1)S(1)}, u32[]{:S(2)}, u32[]{:S(2)}) collective-permute-start(bf16[320,256]{1,0:T(8,128)(2,1)S(1)} %slice.79), channel_id=1, source_target_pairs={{0,14},{1,15},{2,0},{3,1},{4,2},{5,3},{6,4},{7,5},{8,6},{9,7},{10,... | collective-permute-start | bytes 491528 | tf_op jit(solution)/shard_map/ppermute | solution.py:22
  102.6 7.8 %collective-permute-start.20 = (bf16[320,256]{1,0:T(8,128)(2,1)S(1)}, bf16[320,256]{1,0:T(8,128)(2,1)S(1)}, u32[]{:S(2)}, u32[]{:S(2)}) collective-permute-start(bf16[320,256]{1,0:T(8,128)(2,1)S(1)} %slice.80), channel_id=1, source_target_pairs={{0,2},{1,3},{2,4},{3,5},{4,6},{5,7},{6,8},{7,9},{8,10},{9,11},{10,... | collective-permute-start | bytes 491528 | tf_op jit(solution)/shard_map/ppermute | solution.py:22
  113.6 8.8 %copy-start.7 = (bf16[640,2048]{1,0:T(8,128)(2,1)S(1)}, bf16[640,2048]{1,0:T(8,128)(2,1)}, u32[]{:S(2)}) copy-start(bf16[640,2048]{1,0:T(8,128)(2,1)} %constant_dynamic-update-slice_fusion.9) | copy-start | bytes 7864324
  117.7 9.0 %collective-permute-start.22 = (bf16[160,640]{1,0:T(8,128)(2,1)S(1)}, bf16[160,640]{1,0:T(8,128)(2,1)S(1)}, u32[]{:S(2)}, u32[]{:S(2)}) collective-permute-start(bf16[160,640]{1,0:T(8,128)(2,1)S(1)} %get-tuple-element.33), channel_id=1, source_target_pairs={{0,32},{1,33},{2,34},{3,35},{4,36},{5,37},{6,38},{7,39},{8,40},{9,... | collective-permute-start | bytes 614408 | tf_op jit(solution)/shard_map/ppermute | solution.py:22
  121.3 8.1 %collective-permute-start.24 = (bf16[160,640]{1,0:T(8,128)(2,1)S(1)}, bf16[160,640]{1,0:T(8,128)(2,1)S(1)}, u32[]{:S(2)}, u32[]{:S(2)}) collective-permute-start(bf16[160,640]{1,0:T(8,128)(2,1)S(1)} %get-tuple-element.34), channel_id=1, source_target_pairs={{0,33},{1,32},{2,35},{3,34},{4,37},{5,36},{6,39},{7,38},{8,41},{9,... | collective-permute-start | bytes 614408 | tf_op jit(solution)/shard_map/ppermute | solution.py:22
  126.8 12.3 %collective-permute-start.23 = (bf16[320,640]{1,0:T(8,128)(2,1)S(1)}, bf16[320,640]{1,0:T(8,128)(2,1)S(1)}, u32[]{:S(2)}, u32[]{:S(2)}) collective-permute-start(bf16[320,640]{1,0:T(8,128)(2,1)S(1)} %fusion.7), channel_id=1, source_target_pairs={{0,33},{1,32},{2,35},{3,34},{4,37},{5,36},{6,39},{7,38},{8,41},{9,... | collective-permute-start | bytes 1228808 | tf_op jit(solution)/shard_map/ppermute | solution.py:22
  129.4 10.5 %collective-permute-start.25 = (bf16[320,640]{1,0:T(8,128)(2,1)S(1)}, bf16[320,640]{1,0:T(8,128)(2,1)S(1)}, u32[]{:S(2)}, u32[]{:S(2)}) collective-permute-start(bf16[320,640]{1,0:T(8,128)(2,1)S(1)} %fusion.6), channel_id=1, source_target_pairs={{0,32},{1,33},{2,34},{3,35},{4,36},{5,37},{6,38},{7,39},{8,40},{9,... | collective-permute-start | bytes 1228808 | tf_op jit(solution)/shard_map/ppermute | solution.py:22

commit v3 on v2

--- a/solution.py
+++ b/solution.py
@@ -5,6 +5,7 @@
 
 AXES = ("y", "xl", "core", "z", "xh")
 SIZES = (4, 2, 2, 8, 2)
+ORDER = (0, 1, 7, 2, 6, 3, 5, 4)
 
 
 def pairs(move):
@@ -34,17 +35,21 @@
     return lambda y, xl, co, z, xh: ((y + step) % 4, xl, co, z, xh)
 
 
+def rotated(stack, start):
+    n = stack.shape[0]
+    return lax.dynamic_slice_in_dim(jnp.concatenate([stack, stack]), start, n, 0)
+
+
+def row_by(step, other):
+    return lambda y, xl, co, z, xh: ((y + step) % 4, xl ^ other, co, z, xh)
+
+
 def in_run(y, xl, co, z, xh):
     return y, 1 - xl, co, z, xh
 
 
 def out_run(y, xl, co, z, xh):
     return y, 1 - xl, co, z, 1 - xh
-
-
-def rotated(stack, start):
-    n = stack.shape[0]
-    return lax.dynamic_slice_in_dim(jnp.concatenate([stack, stack]), start, n, 0)
 
 
 def dot_f32(left, right):
@@ -68,8 +73,8 @@
     got_rows = send(theirs, other_core)
     got_tiles = send(weight_tiles, other_core)
 
-    pieces = expand_cols.reshape(4, quarter, 2, half).transpose(0, 2, 1, 3)
-    pieces = pieces.reshape(8, quarter, half)
+    pieces = [expand_cols[:, i * half : (i + 1) * half].reshape(4, 1, quarter, half) for i in range(2)]
+    pieces = jnp.concatenate(pieces, 1).reshape(8, quarter, half)
     got_rows, got_tiles, pieces = lax.optimization_barrier((got_rows, got_tiles, pieces))
     pieces = lax.all_to_all(pieces, ("y", "xl"), 0, 0, tiled=True)
 
@@ -77,44 +82,54 @@
     right = jnp.concatenate([weight_tiles, got_tiles], 0)
     part = [
         jnp.dot(left, right[:, i * half : (i + 1) * half], preferred_element_type=jnp.float32)
-        .astype(bf16).reshape(4, 2 * m, half)
+        .astype(bf16).reshape(4, 2, m, half)
         for i in range(2)
     ]
-    part = jnp.stack(part, 1).reshape(8, 2 * m, half)
+    part = jnp.stack([part[0], part[1][:, ::-1]], 1).reshape(8, 2 * m, half)
     pieces = rotated(pieces, z)
     part, pieces = lax.optimization_barrier((part, pieces))
+    barrier = lax.optimization_barrier
     part = lax.all_to_all(part, ("y", "xl"), 0, 0, tiled=True)
-    got = [pieces[0]] + [send(pieces[-i % 8], z_by(-i)) for i in range(1, 8)]
+
+    got = {0: pieces[0]}
+    for group in ((1, 7, 2, 6), (3, 5, 4)):
+        got.update({i: send(pieces[-i % 8], z_by(-i)) for i in group})
+        got, pieces = barrier((got, pieces))
+    cols = jnp.concatenate([got[i] for i in ORDER], 1)
+    part, cols = barrier((part, cols))
     inner = jnp.sum(part.astype(jnp.float32), 0).astype(bf16)
-    inner = jnp.where(xl == 0, inner, jnp.concatenate([inner[m:], inner[:m]]))
 
-    cols = jnp.concatenate(got, 1)
-    below = send(cols, y_by(1))
-    above = send(cols, y_by(-1))
-    far = jnp.concatenate([send(below[:, : 4 * half], y_by(1)), send(above[:, 4 * half :], y_by(-1))], 1)
+    up1, down1 = send(inner, z_by(-1)), send(inner, z_by(1))
+    below, above = send(cols, y_by(1)), send(cols, y_by(-1))
+    up1, down1 = barrier((up1, down1))
+    up2, down2 = send(up1, z_by(-1)), send(down1, z_by(1))
+    first = jnp.concatenate((inner, up1, down1), 1)
+    up2, down2, below, above, first = barrier((up2, down2, below, above, first))
+    up3, down3 = send(up2, z_by(-1)), send(down2, z_by(1))
+    far = [send(below[:, : 4 * half], y_by(1)), send(above[:, 4 * half :], y_by(-1))]
+    second = jnp.concatenate((up2, down2), 1)
+    up3, down3, far, second = barrier((up3, down3, far, second))
     full = jnp.zeros((n, 8 * half), bf16)
-    for shift, block in ((0, cols), (1, above), (2, far), (3, below)):
+    for shift, block in ((0, cols), (1, above), (3, below), (2, jnp.concatenate(far, 1))):
         full = lax.dynamic_update_slice_in_dim(full, block, (y + shift) % 4 * quarter, 0)
-    slots = [inner] + [None] * 7
-    up = down = inner
-    for i in range(1, 4):
-        up, down = send(up, z_by(-1)), send(down, z_by(1))
-        if i < 3:
-            up, down = lax.optimization_barrier((up, down))
-        else:
-            up, down, full = lax.optimization_barrier((up, down, full))
-        slots[i], slots[-i] = up, down
     other = send(full, other_core)
-    slots[4] = jnp.concatenate([send(up[:m], z_by(-1)), send(down[m:], z_by(1))])
-    inner_all = jnp.concatenate(slots, 1)
-    near_cols = jnp.where(xh == co, full, other)
-    far_cols = jnp.where(xh == co, other, full)
+    across = jnp.concatenate([send(up3[:m], z_by(-1)), send(down3[m:], z_by(1))])
+    third = jnp.concatenate((up3, down3, across), 1)
+    near = jnp.where(xh == co, full, other)
+    far = jnp.where(xh == co, other, full)
 
-    cross = dot_f32(inner_all, far_cols)
+    def product(side):
+        return (
+            dot_f32(first, side[:, : 3 * half])
+            + dot_f32(second, side[:, 3 * half : 5 * half])
+            + dot_f32(third, side[:, 5 * half :])
+        )
+
+    cross = product(far)
     cut = m // 2
     via_in = send(cross[:cut].astype(bf16), in_run)
     via_out = send(cross[cut:m].astype(bf16), out_run)
-    straight = dot_f32(inner_all, near_cols)
+    straight = product(near)
     to_out = cross[m:] + jnp.pad(via_in.astype(jnp.float32), ((0, m - cut), (0, 0)))
     to_in = straight[m:] + jnp.pad(via_out.astype(jnp.float32), ((cut, 0), (0, 0)))
     from_out = send(to_out.astype(bf16), out_run)

time: 142 us -> 131 us (0.923)
  starting transfers between devices: 56.7 us -> 45.2 us
  local copies, waits for them, and re-layouts: 23.6 us -> 17.7 us
  waiting for transfers between devices: 42.6 us -> 47.8 us
  other arithmetic: 5.2 us -> 9.39 us
  matrix products: 12.4 us -> 9.72 us
    ppermute x26, starting transfers between devices: 46.1 us -> 34.6 us  [send(): return lax.ppermute(value, AXES, pairs(move))]
    ppermute x26, waiting for transfers between devices: 38.9 us -> 45.9 us  [send(): return lax.ppermute(value, AXES, pairs(move))]
    unnamed x29 -> x26, local copies, waits for them, and re-layouts: 10.5 us -> 6.56 us
    concatenate x0 -> x3, other arithmetic: none -> 3.14 us  [the longest x1 2.2 us: on_device(): first = jnp.concatenate((inner, up1, down1), 1)]
    dot_general x2 -> x6, matrix products: 8.09 us -> 5.37 us  [dot_f32(): lax.dot_general(left, right, (((1,), (1,)), ((), ())), preferred_element_...]
    select_n x0 -> x1, other arithmetic: none -> 2.08 us  [on_device(): far = jnp.where(xh == co, other, full)]
    reshape x1 -> x0, local copies, waits for them, and re-layouts: 2.03 us -> none  [on_device(): pieces = expand_cols.reshape(4, quarter, 2, half).transpose(0, 2, 1, 3)]
    slice x3, local copies, waits for them, and re-layouts: 0.05 us -> 1.9 us  [the longest x1 0.93 us: on_device(): down3[m:]]
  transfers between devices with their start and end apart: 28 -> 28, of which waited for: 16 -> 19; matrix products, arithmetic and copies ran while one was open for 24% -> 23% of each run, Pallas kernels for 0% -> 0%
where the time goes in v3:
time: 131 us; the launch traced here: 130 us
  waiting for transfers between devices  47.8 us (36%)
  starting transfers between devices  45.2 us (35%)
  local copies, waits for them, and re-layouts  17.7 us (14%)
  matrix products  9.72 us (7%)
  other arithmetic  9.39 us (7%)
    ppermute x26, waiting for transfers between devices, send(): return lax.ppermute(value, AXES, pairs(move))  45.9 us
    ppermute x26, starting transfers between devices, send(): return lax.ppermute(value, AXES, pairs(move))  34.6 us
    unnamed x26, local copies, waits for them, and re-layouts  6.56 us
    all_to_all x1, starting transfers between devices, on_device(): pieces = lax.all_to_all(pieces, ('y', 'xl'), 0, 0, tiled=True)  5.93 us
    dot_general x6, matrix products, dot_f32(): lax.dot_general(left, right, (((1,), (1,)), ((), ())), preferred_element_...  5.37 us
    all_to_all x1, starting transfers between devices, on_device(): part = lax.all_to_all(part, ('y', 'xl'), 0, 0, tiled=True)  4.71 us
    dot_general x2, matrix products, on_device(): jnp.dot(left, right[:, i * half:(i + 1) * half], preferred_element_type=j...  4.35 us
    dynamic_update_slice x3, local copies, waits for them, and re-layouts, on_device(): lax.dynamic_update_slice_in_dim(full, block, (y + shift) % 4 * quarter, 0)  3.41 us
  transfers between devices with their start and end apart: 28, of which 19 were waited for; matrix products, arithmetic and copies ran while one was open for 23% of the time, Pallas kernels for 0%

profile of v3, /device:TPU:6, one launch (start us, length us, event | category | flops | bytes accessed | tf_op | source)
XLA Modules:
  0.0 130.1 jit_solution(758530938463745830)
XLA Ops:
  0.0 2.0 %constant_dynamic-slice_fusion = (bf16[4,2,1,320,256]{4,3,2,1,0:T(8,128)(2,1)S(1)}, bf16[4,2,320,256]{3,2,1,0:T(8,128)(2,1)S(1)}) fusion(bf16[4,2,2,320,256]{4,3,2,1,0:T(8,128)(2,1)} %bitcast.35, s32[]{:T(128)S(6)} %select_n.53, s32[]{:T(128)S(6)} %select_n.54), kind=kLoop, calls=%fused_computation.60 | loop fusion | bytes 5242888 | tf_op jit(solution)/shard_map/jit(dynamic_index_in_dim)/dynamic_slice | solution.py:71
  4.3 1.3 %collective-permute-done.1 = bf16[256,512]{1,0:T(8,128)(2,1)} collective-permute-done((bf16[256,512]{1,0:T(8,128)(2,1)S(1)}, bf16[256,512]{1,0:T(8,128)(2,1)}, u32[]{:S(2)}, u32[]{:S(2)}) %collective-permute-start.1) | collective-permute-done | bytes 262176 | tf_op jit(solution)/shard_map/ppermute | solution.py:23
  5.6 5.9 %all-to-all-start = ((bf16[8,160,256]{2,1,0:T(8,128)(2,1)}), bf16[8,160,256]{2,1,0:T(8,128)(2,1)S(1)}, u32[]{:S(2)}, u32[]{:S(2)}) async-start(bf16[8,160,256]{2,1,0:T(8,128)(2,1)} %bitcast.5), calls=%async_computation | async-start | bytes 1310720 | tf_op jit(solution)/shard_map/all_to_all | solution.py:79
  11.5 1.7 %constant_dynamic-update-slice_fusion = bf16[512,512]{1,0:T(8,128)(2,1)} fusion(bf16[512,512]{1,0:T(8,128)(2,1)} %constant_dynamic-update-slice_fusion.1, bf16[256,512]{1,0:T(8,128)(2,1)} %collective-permute-done.1), kind=kLoop, calls=%fused_computation.47 | loop fusion | bytes 524288 | tf_op jit(solution)/shard_map/concatenate | solution.py:82
  13.2 2.2 %convolution_convert_fusion = bf16[2560,256]{1,0:T(8,128)(2,1)S(1)} fusion(bf16[2560,256]{1,0:T(8,128)(2,1)} %bitcast.6, bf16[2560,256]{1,0:T(8,128)(2,1)S(1)} %bitcast.40, bf16[512,512]{1,0:T(8,128)(2,1)} %constant_dynamic-update-slice_fusion), kind=kOutput, calls=%fused_computation | convolution fusion | flops 676986880 | bytes 4194304 | tf_op jit(solution)/shard_map/dot_general | solution.py:84
  15.5 0.9 copy-done.8
  16.4 2.2 %convolution_convert_fusion.1 = bf16[2560,256]{1,0:T(8,128)(2,1)S(1)} fusion(bf16[2560,256]{1,0:T(8,128)(2,1)} %bitcast.6, bf16[2560,256]{1,0:T(8,128)(2,1)S(1)} %bitcast.41, bf16[512,512]{1,0:T(8,128)(2,1)S(1)} %copy-done.8), kind=kOutput, calls=%fused_computation.1 | convolution fusion | flops 676986880 | bytes 4194304 | tf_op jit(solution)/shard_map/dot_general | solution.py:84
  18.6 1.7 %pad_maximum_fusion.1 = bf16[4,2,2,320,256]{4,3,2,1,0:T(8,128)(2,1)} fusion(bf16[4,1,2,320,256]{4,3,2,1,0:T(8,128)(2,1)S(1)} %reverse_bitcast_fusion, bf16[4,1,2,320,256]{4,3,2,1,0:T(8,128)(2,1)S(1)} %bitcast.36), kind=kLoop, calls=%fused_computation.3 | loop fusion | flops 1310720 | bytes 5242880 | tf_op jit(solution)/shard_map/stack | solution.py:88
  20.3 1.9 %all-to-all-done = bf16[8,160,256]{2,1,0:T(8,128)(2,1)S(1)} async-done(((bf16[8,160,256]{2,1,0:T(8,128)(2,1)}), bf16[8,160,256]{2,1,0:T(8,128)(2,1)S(1)}, u32[]{:S(2)}, u32[]{:S(2)}) %all-to-all-start) | async-done | bytes 655392 | tf_op jit(solution)/shard_map/all_to_all | solution.py:79
  22.4 4.7 %all-to-all-start.1 = ((bf16[8,640,256]{2,1,0:T(8,128)(2,1)}), bf16[8,640,256]{2,1,0:T(8,128)(2,1)S(1)}, u32[]{:S(2)}, u32[]{:S(2)}) async-start(bf16[8,640,256]{2,1,0:T(8,128)(2,1)} %bitcast.11), calls=%async_computation.1 | async-start | bytes 5242880 | tf_op jit(solution)/shard_map/all_to_all | solution.py:92
  27.1 5.9 %collective-permute-start.2 = (bf16[160,256]{1,0:T(8,128)(2,1)S(1)}, bf16[160,256]{1,0:T(8,128)(2,1)S(1)}, u32[]{:S(2)}, u32[]{:S(2)}) collective-permute-start(bf16[160,256]{1,0:T(8,128)(2,1)S(1)} %get-tuple-element.83), channel_id=1, source_target_pairs={{0,14},{1,15},{2,0},{3,1},{4,2},{5,3},{6,4},{7,5},{8,6},{9,7},{10,... | collective-permute-start | bytes 245768 | tf_op jit(solution)/shard_map/ppermute | solution.py:23
  33.1 1.5 %collective-permute-start.3 = (bf16[160,256]{1,0:T(8,128)(2,1)S(1)}, bf16[160,256]{1,0:T(8,128)(2,1)S(1)}, u32[]{:S(2)}, u32[]{:S(2)}) collective-permute-start(bf16[160,256]{1,0:T(8,128)(2,1)S(1)} %get-tuple-element.82), channel_id=1, source_target_pairs={{0,12},{1,13},{2,14},{3,15},{4,0},{5,1},{6,2},{7,3},{8,4},{9,5},{1... | collective-permute-start | bytes 245768 | tf_op jit(solution)/shard_map/ppermute | solution.py:23
  34.5 1.5 %collective-permute-start.4 = (bf16[160,256]{1,0:T(8,128)(2,1)S(1)}, bf16[160,256]{1,0:T(8,128)(2,1)S(1)}, u32[]{:S(2)}, u32[]{:S(2)}) collective-permute-start(bf16[160,256]{1,0:T(8,128)(2,1)S(1)} %get-tuple-element.81), channel_id=1, source_target_pairs={{0,4},{1,5},{2,6},{3,7},{4,8},{5,9},{6,10},{7,11},{8,12},{9,13},{1... | collective-permute-start | bytes 245768 | tf_op jit(solution)/shard_map/ppermute | solution.py:23
  36.0 2.5 %collective-permute-done.3 = bf16[160,256]{1,0:T(8,128)(2,1)S(1)} collective-permute-done((bf16[160,256]{1,0:T(8,128)(2,1)S(1)}, bf16[160,256]{1,0:T(8,128)(2,1)S(1)}, u32[]{:S(2)}, u32[]{:S(2)}) %collective-permute-start.3) | collective-permute-done | bytes 81952 | tf_op jit(solution)/shard_map/ppermute | solution.py:23
  38.5 3.5 %collective-permute-done.4 = bf16[160,256]{1,0:T(8,128)(2,1)S(1)} collective-permute-done((bf16[160,256]{1,0:T(8,128)(2,1)S(1)}, bf16[160,256]{1,0:T(8,128)(2,1)S(1)}, u32[]{:S(2)}, u32[]{:S(2)}) %collective-permute-start.4) | collective-permute-done | bytes 81952 | tf_op jit(solution)/shard_map/ppermute | solution.py:23
  42.8 3.9 %collective-permute-start.7 = (bf16[160,256]{1,0:T(8,128)(2,1)S(1)}, bf16[160,256]{1,0:T(8,128)(2,1)S(1)}, u32[]{:S(2)}, u32[]{:S(2)}) collective-permute-start(bf16[160,256]{1,0:T(8,128)(2,1)S(1)} %get-tuple-element.78), channel_id=1, source_target_pairs={{0,8},{1,9},{2,10},{3,11},{4,12},{5,13},{6,14},{7,15},{8,0},{9,1},... | collective-permute-start | bytes 245768 | tf_op jit(solution)/shard_map/ppermute | solution.py:23
  47.3 2.5 %collective-permute-done.6 = bf16[160,256]{1,0:T(8,128)(2,1)S(1)} collective-permute-done((bf16[160,256]{1,0:T(8,128)(2,1)S(1)}, bf16[160,256]{1,0:T(8,128)(2,1)S(1)}, u32[]{:S(2)}, u32[]{:S(2)}) %collective-permute-start.6) | collective-permute-done | bytes 81952 | tf_op jit(solution)/shard_map/ppermute | solution.py:23
  49.9 1.6 %collective-permute-done.7 = bf16[160,256]{1,0:T(8,128)(2,1)S(1)} collective-permute-done((bf16[160,256]{1,0:T(8,128)(2,1)S(1)}, bf16[160,256]{1,0:T(8,128)(2,1)S(1)}, u32[]{:S(2)}, u32[]{:S(2)}) %collective-permute-start.7) | collective-permute-done | bytes 81952 | tf_op jit(solution)/shard_map/ppermute | solution.py:23
  51.5 5.2 %collective-permute-done.8 = bf16[160,256]{1,0:T(8,128)(2,1)S(1)} collective-permute-done((bf16[160,256]{1,0:T(8,128)(2,1)S(1)}, bf16[160,256]{1,0:T(8,128)(2,1)S(1)}, u32[]{:S(2)}, u32[]{:S(2)}) %collective-permute-start.8) | collective-permute-done | bytes 81952 | tf_op jit(solution)/shard_map/ppermute | solution.py:23
  61.9 1.2 reduce_sum.12
  63.0 1.7 %collective-permute-start.9 = (bf16[640,256]{1,0:T(8,128)(2,1)}, bf16[640,256]{1,0:T(8,128)(2,1)}, u32[]{:S(2)}, u32[]{:S(2)}) collective-permute-start(bf16[640,256]{1,0:T(8,128)(2,1)} %reduce_sum.12), channel_id=1, source_target_pairs={{0,14},{1,15},{2,0},{3,1},{4,2},{5,3},{6,4},{7,5},{8,6},{9,7},{10,... | collective-permute-start | bytes 983048 | tf_op jit(solution)/shard_map/ppermute | solution.py:23
  65.1 1.6 %collective-permute-start.13 = (bf16[160,2048]{1,0:T(8,128)(2,1)}, bf16[160,2048]{1,0:T(8,128)(2,1)S(1)}, u32[]{:S(2)}, u32[]{:S(2)}) collective-permute-start(bf16[160,2048]{1,0:T(8,128)(2,1)} %constant_dynamic-update-slice_fusion.2), channel_id=1, source_target_pairs={{0,64},{1,65},{2,66},{3,67},{4,68},{5,69},{6,70},{7,71},{8,72},{9,... | collective-permute-start | bytes 1966088 | tf_op jit(solution)/shard_map/ppermute | solution.py:23
  66.6 1.6 %collective-permute-start.14 = (bf16[160,2048]{1,0:T(8,128)(2,1)}, bf16[160,2048]{1,0:T(8,128)(2,1)}, u32[]{:S(2)}, u32[]{:S(2)}) collective-permute-start(bf16[160,2048]{1,0:T(8,128)(2,1)} %constant_dynamic-update-slice_fusion.2), channel_id=1, source_target_pairs={{0,192},{1,193},{2,194},{3,195},{4,196},{5,197},{6,198},{7,199},{8... | collective-permute-start | bytes 1966088 | tf_op jit(solution)/shard_map/ppermute | solution.py:23
  68.3 2.1 %collective-permute-done.9 = bf16[640,256]{1,0:T(8,128)(2,1)} collective-permute-done((bf16[640,256]{1,0:T(8,128)(2,1)}, bf16[640,256]{1,0:T(8,128)(2,1)}, u32[]{:S(2)}, u32[]{:S(2)}) %collective-permute-start.9) | collective-permute-done | bytes 327712 | tf_op jit(solution)/shard_map/ppermute | solution.py:23
  70.4 3.0 %collective-permute-done.10 = bf16[640,256]{1,0:T(8,128)(2,1)} collective-permute-done((bf16[640,256]{1,0:T(8,128)(2,1)}, bf16[640,256]{1,0:T(8,128)(2,1)}, u32[]{:S(2)}, u32[]{:S(2)}) %collective-permute-start.10) | collective-permute-done | bytes 327712 | tf_op jit(solution)/shard_map/ppermute | solution.py:23
  73.8 1.7 %collective-permute-start.12 = (bf16[640,256]{1,0:T(8,128)(2,1)}, bf16[640,256]{1,0:T(8,128)(2,1)S(1)}, u32[]{:S(2)}, u32[]{:S(2)}) collective-permute-start(bf16[640,256]{1,0:T(8,128)(2,1)} %collective-permute-done.10), channel_id=1, source_target_pairs={{0,2},{1,3},{2,4},{3,5},{4,6},{5,7},{6,8},{7,9},{8,10},{9,11},{10,... | collective-permute-start | bytes 983048 | tf_op jit(solution)/shard_map/ppermute | solution.py:23
  75.8 1.1 constant_dynamic-update-slice_fusion.12
  77.0 2.2 %pad_maximum_fusion.4 = bf16[640,768]{1,0:T(8,128)(2,1)} fusion(bf16[640,256]{1,0:T(8,128)(2,1)} %collective-permute-done.10, bf16[640,256]{1,0:T(8,128)(2,1)} %collective-permute-done.9, bf16[640,256]{1,0:T(8,128)(2,1)} %reduce_sum.12), kind=kLoop, calls=%fused_computation.20 | loop fusion | flops 2949120 | bytes 1966080 | tf_op jit(solution)/shard_map/concatenate | solution.py:106
  79.2 1.6 %collective-permute-done.13 = bf16[160,2048]{1,0:T(8,128)(2,1)S(1)} collective-permute-done((bf16[160,2048]{1,0:T(8,128)(2,1)}, bf16[160,2048]{1,0:T(8,128)(2,1)S(1)}, u32[]{:S(2)}, u32[]{:S(2)}) %collective-permute-start.13) | collective-permute-done | bytes 655392 | tf_op jit(solution)/shard_map/ppermute | solution.py:23
  80.8 1.0 collective-permute-done.14
  82.2 2.4 %collective-permute-start.15 = (bf16[640,256]{1,0:T(8,128)(2,1)S(1)}, bf16[640,256]{1,0:T(8,128)(2,1)S(1)}, u32[]{:S(2)}, u32[]{:S(2)}) collective-permute-start(bf16[640,256]{1,0:T(8,128)(2,1)S(1)} %collective-permute-done.11), channel_id=1, source_target_pairs={{0,14},{1,15},{2,0},{3,1},{4,2},{5,3},{6,4},{7,5},{8,6},{9,7},{10,... | collective-permute-start | bytes 983048 | tf_op jit(solution)/shard_map/ppermute | solution.py:23
  84.7 3.8 %collective-permute-start.17 = (bf16[160,1024]{1,0:T(8,128)(2,1)S(1)}, bf16[160,1024]{1,0:T(8,128)(2,1)S(1)}, u32[]{:S(2)}, u32[]{:S(2)}) collective-permute-start(bf16[160,1024]{1,0:T(8,128)(2,1)S(1)} %slice.95), channel_id=1, source_target_pairs={{0,64},{1,65},{2,66},{3,67},{4,68},{5,69},{6,70},{7,71},{8,72},{9,... | collective-permute-start | bytes 983048 | tf_op jit(solution)/shard_map/ppermute | solution.py:23
  88.5 1.0 slice.96
  89.6 1.1 constant_dynamic-update-slice_fusion.11
  90.8 1.1 constant_dynamic-update-slice_fusion.10
  92.0 1.5 %collective-permute-done.16 = bf16[640,256]{1,0:T(8,128)(2,1)S(1)} collective-permute-done((bf16[640,256]{1,0:T(8,128)(2,1)S(1)}, bf16[640,256]{1,0:T(8,128)(2,1)S(1)}, u32[]{:S(2)}, u32[]{:S(2)}) %collective-permute-start.16) | collective-permute-done | bytes 327712 | tf_op jit(solution)/shard_map/ppermute | solution.py:23
  93.6 3.1 %collective-permute-done.18 = bf16[160,1024]{1,0:T(8,128)(2,1)S(1)} collective-permute-done((bf16[160,1024]{1,0:T(8,128)(2,1)S(1)}, bf16[160,1024]{1,0:T(8,128)(2,1)S(1)}, u32[]{:S(2)}, u32[]{:S(2)}) %collective-permute-start.18) | collective-permute-done | bytes 327712 | tf_op jit(solution)/shard_map/ppermute | solution.py:23
  99.0 3.1 %collective-permute-start.20 = (bf16[320,256]{1,0:T(8,128)(2,1)S(1)}, bf16[320,256]{1,0:T(8,128)(2,1)S(1)}, u32[]{:S(2)}, u32[]{:S(2)}) collective-permute-start(bf16[320,256]{1,0:T(8,128)(2,1)S(1)} %slice.99), channel_id=1, source_target_pairs={{0,14},{1,15},{2,0},{3,1},{4,2},{5,3},{6,4},{7,5},{8,6},{9,7},{10,... | collective-permute-start | bytes 491528 | tf_op jit(solution)/shard_map/ppermute | solution.py:23
  102.2 2.1 %broadcast_select_fusion = (bf16[640,2048]{1,0:T(8,128)(2,1)S(1)}, bf16[640,2048]{1,0:T(8,128)(2,1)S(1)}) fusion(bf16[640,2048]{1,0:T(8,128)(2,1)} %collective-permute-done.19, bf16[640,2048]{1,0:T(8,128)(2,1)S(1)} %maximum_dynamic-update-slice_fusion, pred[]{:T(512)S(6)} %eq.9), kind=kLoop, calls=%fused_computation.4 | loop fusion | flops 2621440 | bytes 10485761 | tf_op jit(solution)/shard_map/jit(_where)/select_n | solution.py:119
  104.3 1.0 fusion.10
  105.9 1.0 fusion.4
  108.0 1.0 fusion.29
  109.1 1.3 %collective-permute-start.22 = (bf16[160,640]{1,0:T(8,128)(2,1)S(1)}, bf16[160,640]{1,0:T(8,128)(2,1)S(1)}, u32[]{:S(2)}, u32[]{:S(2)}) collective-permute-start(bf16[160,640]{1,0:T(8,128)(2,1)S(1)} %get-tuple-element.75), channel_id=1, source_target_pairs={{0,32},{1,33},{2,34},{3,35},{4,36},{5,37},{6,38},{7,39},{8,40},{9,... | collective-permute-start | bytes 614408 | tf_op jit(solution)/shard_map/ppermute | solution.py:23
  110.5 1.0 add_add_fusion.1
  111.5 5.7 %collective-permute-done.24 = bf16[160,640]{1,0:T(8,128)(2,1)S(1)} collective-permute-done((bf16[160,640]{1,0:T(8,128)(2,1)S(1)}, bf16[160,640]{1,0:T(8,128)(2,1)S(1)}, u32[]{:S(2)}, u32[]{:S(2)}) %collective-permute-start.24) | collective-permute-done | bytes 204832 | tf_op jit(solution)/shard_map/ppermute | solution.py:23
  117.5 1.6 %collective-permute-start.23 = (bf16[320,640]{1,0:T(8,128)(2,1)S(1)}, bf16[320,640]{1,0:T(8,128)(2,1)S(1)}, u32[]{:S(2)}, u32[]{:S(2)}) collective-permute-start(bf16[320,640]{1,0:T(8,128)(2,1)S(1)} %fusion.13), channel_id=1, source_target_pairs={{0,33},{1,32},{2,35},{3,34},{4,37},{5,36},{6,39},{7,38},{8,41},{9,... | collective-permute-start | bytes 1228808 | tf_op jit(solution)/shard_map/ppermute | solution.py:23
  119.1 8.7 %collective-permute-done.25 = bf16[320,640]{1,0:T(8,128)(2,1)S(1)} collective-permute-done((bf16[320,640]{1,0:T(8,128)(2,1)S(1)}, bf16[320,640]{1,0:T(8,128)(2,1)S(1)}, u32[]{:S(2)}, u32[]{:S(2)}) %collective-permute-start.25) | collective-permute-done | bytes 409632 | tf_op jit(solution)/shard_map/ppermute | solution.py:23
  127.8 1.4 %collective-permute-done.23 = bf16[320,640]{1,0:T(8,128)(2,1)S(1)} collective-permute-done((bf16[320,640]{1,0:T(8,128)(2,1)S(1)}, bf16[320,640]{1,0:T(8,128)(2,1)S(1)}, u32[]{:S(2)}, u32[]{:S(2)}) %collective-permute-start.23) | collective-permute-done | bytes 409632 | tf_op jit(solution)/shard_map/ppermute | solution.py:23
  (69 shorter events, 16.2 us)
Async XLA Ops:
  0.0 2.1 %copy-start.7 = (bf16[256,512]{1,0:T(8,128)(2,1)S(1)}, bf16[256,512]{1,0:T(8,128)(2,1)}, u32[]{:S(2)}) copy-start(bf16[256,512]{1,0:T(8,128)(2,1)} %param.3) | copy-start | bytes 786436
  0.0 2.6 %copy-start.6 = (bf16[640,512]{1,0:T(8,128)(2,1)S(1)}, bf16[640,512]{1,0:T(8,128)(2,1)}, u32[]{:S(2)}) copy-start(bf16[640,512]{1,0:T(8,128)(2,1)} %param.5) | copy-start | bytes 1966084
  2.0 3.6 %collective-permute-start = (bf16[4,2,320,256]{3,2,1,0:T(8,128)(2,1)S(1)}, bf16[4,2,320,256]{3,2,1,0:T(8,128)(2,1)}, u32[]{:S(2)}, u32[]{:S(2)}) collective-permute-start(bf16[4,2,320,256]{3,2,1,0:T(8,128)(2,1)S(1)} %get-tuple-element.74), channel_id=1, source_target_pairs={{0,16},{1,17},{2,18},{3,19},{4,20},{5,21},{6,22},{7,23},{8,24},{9,... | collective-permute-start | bytes 3932168 | tf_op jit(solution)/shard_map/ppermute | solution.py:23
  2.1 3.5 %collective-permute-start.1 = (bf16[256,512]{1,0:T(8,128)(2,1)S(1)}, bf16[256,512]{1,0:T(8,128)(2,1)}, u32[]{:S(2)}, u32[]{:S(2)}) collective-permute-start(bf16[256,512]{1,0:T(8,128)(2,1)S(1)} %copy-done.7), channel_id=1, source_target_pairs={{0,16},{1,17},{2,18},{3,19},{4,20},{5,21},{6,22},{7,23},{8,24},{9,... | collective-permute-start | bytes 786440 | tf_op jit(solution)/shard_map/ppermute | solution.py:23
  5.6 16.6 %all-to-all-start = ((bf16[8,160,256]{2,1,0:T(8,128)(2,1)}), bf16[8,160,256]{2,1,0:T(8,128)(2,1)S(1)}, u32[]{:S(2)}, u32[]{:S(2)}) async-start(bf16[8,160,256]{2,1,0:T(8,128)(2,1)} %bitcast.5), calls=%async_computation | async-start | bytes 1310720 | tf_op jit(solution)/shard_map/all_to_all | solution.py:79
  15.4 1.0 copy-start.8
  22.4 39.5 %all-to-all-start.1 = ((bf16[8,640,256]{2,1,0:T(8,128)(2,1)}), bf16[8,640,256]{2,1,0:T(8,128)(2,1)S(1)}, u32[]{:S(2)}, u32[]{:S(2)}) async-start(bf16[8,640,256]{2,1,0:T(8,128)(2,1)} %bitcast.11), calls=%async_computation.1 | async-start | bytes 5242880 | tf_op jit(solution)/shard_map/all_to_all | solution.py:92
  27.1 8.9 %collective-permute-start.2 = (bf16[160,256]{1,0:T(8,128)(2,1)S(1)}, bf16[160,256]{1,0:T(8,128)(2,1)S(1)}, u32[]{:S(2)}, u32[]{:S(2)}) collective-permute-start(bf16[160,256]{1,0:T(8,128)(2,1)S(1)} %get-tuple-element.83), channel_id=1, source_target_pairs={{0,14},{1,15},{2,0},{3,1},{4,2},{5,3},{6,4},{7,5},{8,6},{9,7},{10,... | collective-permute-start | bytes 245768 | tf_op jit(solution)/shard_map/ppermute | solution.py:23
  33.1 5.4 %collective-permute-start.3 = (bf16[160,256]{1,0:T(8,128)(2,1)S(1)}, bf16[160,256]{1,0:T(8,128)(2,1)S(1)}, u32[]{:S(2)}, u32[]{:S(2)}) collective-permute-start(bf16[160,256]{1,0:T(8,128)(2,1)S(1)} %get-tuple-element.82), channel_id=1, source_target_pairs={{0,12},{1,13},{2,14},{3,15},{4,0},{5,1},{6,2},{7,3},{8,4},{9,5},{1... | collective-permute-start | bytes 245768 | tf_op jit(solution)/shard_map/ppermute | solution.py:23
  34.5 7.5 %collective-permute-start.4 = (bf16[160,256]{1,0:T(8,128)(2,1)S(1)}, bf16[160,256]{1,0:T(8,128)(2,1)S(1)}, u32[]{:S(2)}, u32[]{:S(2)}) collective-permute-start(bf16[160,256]{1,0:T(8,128)(2,1)S(1)} %get-tuple-element.81), channel_id=1, source_target_pairs={{0,4},{1,5},{2,6},{3,7},{4,8},{5,9},{6,10},{7,11},{8,12},{9,13},{1... | collective-permute-start | bytes 245768 | tf_op jit(solution)/shard_map/ppermute | solution.py:23
  36.0 6.5 %collective-permute-start.5 = (bf16[160,256]{1,0:T(8,128)(2,1)S(1)}, bf16[160,256]{1,0:T(8,128)(2,1)S(1)}, u32[]{:S(2)}, u32[]{:S(2)}) collective-permute-start(bf16[160,256]{1,0:T(8,128)(2,1)S(1)} %get-tuple-element.80), channel_id=1, source_target_pairs={{0,2},{1,3},{2,4},{3,5},{4,6},{5,7},{6,8},{7,9},{8,10},{9,11},{10,... | collective-permute-start | bytes 245768 | tf_op jit(solution)/shard_map/ppermute | solution.py:23
  42.5 7.4 %collective-permute-start.6 = (bf16[160,256]{1,0:T(8,128)(2,1)S(1)}, bf16[160,256]{1,0:T(8,128)(2,1)S(1)}, u32[]{:S(2)}, u32[]{:S(2)}) collective-permute-start(bf16[160,256]{1,0:T(8,128)(2,1)S(1)} %get-tuple-element.79), channel_id=1, source_target_pairs={{0,10},{1,11},{2,12},{3,13},{4,14},{5,15},{6,0},{7,1},{8,2},{9,3},... | collective-permute-start | bytes 245768 | tf_op jit(solution)/shard_map/ppermute | solution.py:23
  42.8 8.6 %collective-permute-start.7 = (bf16[160,256]{1,0:T(8,128)(2,1)S(1)}, bf16[160,256]{1,0:T(8,128)(2,1)S(1)}, u32[]{:S(2)}, u32[]{:S(2)}) collective-permute-start(bf16[160,256]{1,0:T(8,128)(2,1)S(1)} %get-tuple-element.78), channel_id=1, source_target_pairs={{0,8},{1,9},{2,10},{3,11},{4,12},{5,13},{6,14},{7,15},{8,0},{9,1},... | collective-permute-start | bytes 245768 | tf_op jit(solution)/shard_map/ppermute | solution.py:23
  46.8 9.9 %collective-permute-start.8 = (bf16[160,256]{1,0:T(8,128)(2,1)S(1)}, bf16[160,256]{1,0:T(8,128)(2,1)S(1)}, u32[]{:S(2)}, u32[]{:S(2)}) collective-permute-start(bf16[160,256]{1,0:T(8,128)(2,1)S(1)} %get-tuple-element.77), channel_id=1, source_target_pairs={{0,6},{1,7},{2,8},{3,9},{4,10},{5,11},{6,12},{7,13},{8,14},{9,15},... | collective-permute-start | bytes 245768 | tf_op jit(solution)/shard_map/ppermute | solution.py:23
  63.0 7.4 %collective-permute-start.9 = (bf16[640,256]{1,0:T(8,128)(2,1)}, bf16[640,256]{1,0:T(8,128)(2,1)}, u32[]{:S(2)}, u32[]{:S(2)}) collective-permute-start(bf16[640,256]{1,0:T(8,128)(2,1)} %reduce_sum.12), channel_id=1, source_target_pairs={{0,14},{1,15},{2,0},{3,1},{4,2},{5,3},{6,4},{7,5},{8,6},{9,7},{10,... | collective-permute-start | bytes 983048 | tf_op jit(solution)/shard_map/ppermute | solution.py:23
  64.8 8.7 %collective-permute-start.10 = (bf16[640,256]{1,0:T(8,128)(2,1)}, bf16[640,256]{1,0:T(8,128)(2,1)}, u32[]{:S(2)}, u32[]{:S(2)}) collective-permute-start(bf16[640,256]{1,0:T(8,128)(2,1)} %reduce_sum.12), channel_id=1, source_target_pairs={{0,2},{1,3},{2,4},{3,5},{4,6},{5,7},{6,8},{7,9},{8,10},{9,11},{10,... | collective-permute-start | bytes 983048 | tf_op jit(solution)/shard_map/ppermute | solution.py:23
  65.1 15.7 %collective-permute-start.13 = (bf16[160,2048]{1,0:T(8,128)(2,1)}, bf16[160,2048]{1,0:T(8,128)(2,1)S(1)}, u32[]{:S(2)}, u32[]{:S(2)}) collective-permute-start(bf16[160,2048]{1,0:T(8,128)(2,1)} %constant_dynamic-update-slice_fusion.2), channel_id=1, source_target_pairs={{0,64},{1,65},{2,66},{3,67},{4,68},{5,69},{6,70},{7,71},{8,72},{9,... | collective-permute-start | bytes 1966088 | tf_op jit(solution)/shard_map/ppermute | solution.py:23
  66.6 15.1 %collective-permute-start.14 = (bf16[160,2048]{1,0:T(8,128)(2,1)}, bf16[160,2048]{1,0:T(8,128)(2,1)}, u32[]{:S(2)}, u32[]{:S(2)}) collective-permute-start(bf16[160,2048]{1,0:T(8,128)(2,1)} %constant_dynamic-update-slice_fusion.2), channel_id=1, source_target_pairs={{0,192},{1,193},{2,194},{3,195},{4,196},{5,197},{6,198},{7,199},{8... | collective-permute-start | bytes 1966088 | tf_op jit(solution)/shard_map/ppermute | solution.py:23
  73.5 8.3 %collective-permute-start.11 = (bf16[640,256]{1,0:T(8,128)(2,1)}, bf16[640,256]{1,0:T(8,128)(2,1)S(1)}, u32[]{:S(2)}, u32[]{:S(2)}) collective-permute-start(bf16[640,256]{1,0:T(8,128)(2,1)} %collective-permute-done.9), channel_id=1, source_target_pairs={{0,14},{1,15},{2,0},{3,1},{4,2},{5,3},{6,4},{7,5},{8,6},{9,7},{10,... | collective-permute-start | bytes 983048 | tf_op jit(solution)/shard_map/ppermute | solution.py:23
  73.8 8.5 %collective-permute-start.12 = (bf16[640,256]{1,0:T(8,128)(2,1)}, bf16[640,256]{1,0:T(8,128)(2,1)S(1)}, u32[]{:S(2)}, u32[]{:S(2)}) collective-permute-start(bf16[640,256]{1,0:T(8,128)(2,1)} %collective-permute-done.10), channel_id=1, source_target_pairs={{0,2},{1,3},{2,4},{3,5},{4,6},{5,7},{6,8},{7,9},{8,10},{9,11},{10,... | collective-permute-start | bytes 983048 | tf_op jit(solution)/shard_map/ppermute | solution.py:23
  80.8 8.9 %copy-start = (bf16[160,2048]{1,0:T(8,128)(2,1)}, bf16[160,2048]{1,0:T(8,128)(2,1)S(1)}, u32[]{:S(2)}) copy-start(bf16[160,2048]{1,0:T(8,128)(2,1)S(1)} %collective-permute-done.13) | copy-start | bytes 1966084
  82.2 9.7 %collective-permute-start.15 = (bf16[640,256]{1,0:T(8,128)(2,1)S(1)}, bf16[640,256]{1,0:T(8,128)(2,1)S(1)}, u32[]{:S(2)}, u32[]{:S(2)}) collective-permute-start(bf16[640,256]{1,0:T(8,128)(2,1)S(1)} %collective-permute-done.11), channel_id=1, source_target_pairs={{0,14},{1,15},{2,0},{3,1},{4,2},{5,3},{6,4},{7,5},{8,6},{9,7},{10,... | collective-permute-start | bytes 983048 | tf_op jit(solution)/shard_map/ppermute | solution.py:23
  84.7 8.8 %collective-permute-start.16 = (bf16[640,256]{1,0:T(8,128)(2,1)S(1)}, bf16[640,256]{1,0:T(8,128)(2,1)S(1)}, u32[]{:S(2)}, u32[]{:S(2)}) collective-permute-start(bf16[640,256]{1,0:T(8,128)(2,1)S(1)} %collective-permute-done.12), channel_id=1, source_target_pairs={{0,2},{1,3},{2,4},{3,5},{4,6},{5,7},{6,8},{7,9},{8,10},{9,11},{10,... | collective-permute-start | bytes 983048 | tf_op jit(solution)/shard_map/ppermute | solution.py:23
  84.7 8.9 %collective-permute-start.17 = (bf16[160,1024]{1,0:T(8,128)(2,1)S(1)}, bf16[160,1024]{1,0:T(8,128)(2,1)S(1)}, u32[]{:S(2)}, u32[]{:S(2)}) collective-permute-start(bf16[160,1024]{1,0:T(8,128)(2,1)S(1)} %slice.95), channel_id=1, source_target_pairs={{0,64},{1,65},{2,66},{3,67},{4,68},{5,69},{6,70},{7,71},{8,72},{9,... | collective-permute-start | bytes 983048 | tf_op jit(solution)/shard_map/ppermute | solution.py:23
  89.5 7.2 %collective-permute-start.18 = (bf16[160,1024]{1,0:T(8,128)(2,1)S(1)}, bf16[160,1024]{1,0:T(8,128)(2,1)S(1)}, u32[]{:S(2)}, u32[]{:S(2)}) collective-permute-start(bf16[160,1024]{1,0:T(8,128)(2,1)S(1)} %slice.96), channel_id=1, source_target_pairs={{0,192},{1,193},{2,194},{3,195},{4,196},{5,197},{6,198},{7,199},{8... | collective-permute-start | bytes 983048 | tf_op jit(solution)/shard_map/ppermute | solution.py:23
  92.0 4.8 %copy-start.2 = (bf16[640,256]{1,0:T(8,128)(2,1)}, bf16[640,256]{1,0:T(8,128)(2,1)S(1)}, u32[]{:S(2)}) copy-start(bf16[640,256]{1,0:T(8,128)(2,1)S(1)} %collective-permute-done.15) | copy-start | bytes 983044
  93.5 3.3 %copy-start.4 = (bf16[640,256]{1,0:T(8,128)(2,1)}, bf16[640,256]{1,0:T(8,128)(2,1)S(1)}, u32[]{:S(2)}) copy-start(bf16[640,256]{1,0:T(8,128)(2,1)S(1)} %collective-permute-done.16) | copy-start | bytes 983044
  96.8 5.4 %collective-permute-start.19 = (bf16[640,2048]{1,0:T(8,128)(2,1)S(1)}, bf16[640,2048]{1,0:T(8,128)(2,1)}, u32[]{:S(2)}, u32[]{:S(2)}) collective-permute-start(bf16[640,2048]{1,0:T(8,128)(2,1)S(1)} %maximum_dynamic-update-slice_fusion), channel_id=1, source_target_pairs={{0,16},{1,17},{2,18},{3,19},{4,20},{5,21},{6,22},{7,23},{8,24},{9,... | collective-permute-start | bytes 7864328 | tf_op jit(solution)/shard_map/ppermute | solution.py:23
  97.8 9.8 %collective-permute-start.21 = (bf16[320,256]{1,0:T(8,128)(2,1)S(1)}, bf16[320,256]{1,0:T(8,128)(2,1)S(1)}, u32[]{:S(2)}, u32[]{:S(2)}) collective-permute-start(bf16[320,256]{1,0:T(8,128)(2,1)S(1)} %slice.100), channel_id=1, source_target_pairs={{0,2},{1,3},{2,4},{3,5},{4,6},{5,7},{6,8},{7,9},{8,10},{9,11},{10,... | collective-permute-start | bytes 491528 | tf_op jit(solution)/shard_map/ppermute | solution.py:23
  99.0 5.2 %copy-start.1 = (bf16[640,768]{1,0:T(8,128)(2,1)S(1)}, bf16[640,768]{1,0:T(8,128)(2,1)}, u32[]{:S(2)}) copy-start(bf16[640,768]{1,0:T(8,128)(2,1)} %pad_maximum_fusion.4) | copy-start | bytes 2949124
  99.0 8.6 %collective-permute-start.20 = (bf16[320,256]{1,0:T(8,128)(2,1)S(1)}, bf16[320,256]{1,0:T(8,128)(2,1)S(1)}, u32[]{:S(2)}, u32[]{:S(2)}) collective-permute-start(bf16[320,256]{1,0:T(8,128)(2,1)S(1)} %slice.99), channel_id=1, source_target_pairs={{0,14},{1,15},{2,0},{3,1},{4,2},{5,3},{6,4},{7,5},{8,6},{9,7},{10,... | collective-permute-start | bytes 491528 | tf_op jit(solution)/shard_map/ppermute | solution.py:23
  106.9 1.0 copy-start.3
  106.9 1.1 copy-start.5
  109.0 8.2 %collective-permute-start.24 = (bf16[160,640]{1,0:T(8,128)(2,1)S(1)}, bf16[160,640]{1,0:T(8,128)(2,1)S(1)}, u32[]{:S(2)}, u32[]{:S(2)}) collective-permute-start(bf16[160,640]{1,0:T(8,128)(2,1)S(1)} %get-tuple-element.76), channel_id=1, source_target_pairs={{0,33},{1,32},{2,35},{3,34},{4,37},{5,36},{6,39},{7,38},{8,41},{9,... | collective-permute-start | bytes 614408 | tf_op jit(solution)/shard_map/ppermute | solution.py:23
  109.1 8.3 %collective-permute-start.22 = (bf16[160,640]{1,0:T(8,128)(2,1)S(1)}, bf16[160,640]{1,0:T(8,128)(2,1)S(1)}, u32[]{:S(2)}, u32[]{:S(2)}) collective-permute-start(bf16[160,640]{1,0:T(8,128)(2,1)S(1)} %get-tuple-element.75), channel_id=1, source_target_pairs={{0,32},{1,33},{2,34},{3,35},{4,36},{5,37},{6,38},{7,39},{8,40},{9,... | collective-permute-start | bytes 614408 | tf_op jit(solution)/shard_map/ppermute | solution.py:23
  117.3 10.5 %collective-permute-start.25 = (bf16[320,640]{1,0:T(8,128)(2,1)S(1)}, bf16[320,640]{1,0:T(8,128)(2,1)S(1)}, u32[]{:S(2)}, u32[]{:S(2)}) collective-permute-start(bf16[320,640]{1,0:T(8,128)(2,1)S(1)} %fusion.12), channel_id=1, source_target_pairs={{0,32},{1,33},{2,34},{3,35},{4,36},{5,37},{6,38},{7,39},{8,40},{9,... | collective-permute-start | bytes 1228808 | tf_op jit(solution)/shard_map/ppermute | solution.py:23
  117.5 11.7 %collective-permute-start.23 = (bf16[320,640]{1,0:T(8,128)(2,1)S(1)}, bf16[320,640]{1,0:T(8,128)(2,1)S(1)}, u32[]{:S(2)}, u32[]{:S(2)}) collective-permute-start(bf16[320,640]{1,0:T(8,128)(2,1)S(1)} %fusion.13), channel_id=1, source_target_pairs={{0,33},{1,32},{2,35},{3,34},{4,37},{5,36},{6,39},{7,38},{8,41},{9,... | collective-permute-start | bytes 1228808 | tf_op jit(solution)/shard_map/ppermute | solution.py:23

commit v4 on v3

--- a/solution.py
+++ b/solution.py
@@ -92,7 +92,7 @@
     part = lax.all_to_all(part, ("y", "xl"), 0, 0, tiled=True)
 
     got = {0: pieces[0]}
-    for group in ((1, 7, 2, 6), (3, 5, 4)):
+    for group in ((4, 3, 5, 1), (7, 2, 6)):
         got.update({i: send(pieces[-i % 8], z_by(-i)) for i in group})
         got, pieces = barrier((got, pieces))
     cols = jnp.concatenate([got[i] for i in ORDER], 1)

time: 131 us -> 130 us (level)
  waiting for transfers between devices: 47.8 us -> 45.2 us
  starting transfers between devices: 45.2 us -> 46.9 us
    ppermute x26, waiting for transfers between devices: 45.9 us -> 43.4 us  [send(): return lax.ppermute(value, AXES, pairs(move))]
    ppermute x26, starting transfers between devices: 34.6 us -> 36.3 us  [send(): return lax.ppermute(value, AXES, pairs(move))]
where the time goes in v4:
time: 130 us; the launch traced here: 129 us
  starting transfers between devices  46.9 us (36%)
  waiting for transfers between devices  45.2 us (35%)
  local copies, waits for them, and re-layouts  17.7 us (14%)
  matrix products  9.73 us (7%)
  other arithmetic  9.39 us (7%)
    ppermute x26, waiting for transfers between devices, send(): return lax.ppermute(value, AXES, pairs(move))  43.4 us
    ppermute x26, starting transfers between devices, send(): return lax.ppermute(value, AXES, pairs(move))  36.3 us
    unnamed x26, local copies, waits for them, and re-layouts  6.56 us
    all_to_all x1, starting transfers between devices, on_device(): pieces = lax.all_to_all(pieces, ('y', 'xl'), 0, 0, tiled=True)  5.93 us
    dot_general x6, matrix products, dot_f32(): lax.dot_general(left, right, (((1,), (1,)), ((), ())), preferred_element_...  5.38 us
    all_to_all x1, starting transfers between devices, on_device(): part = lax.all_to_all(part, ('y', 'xl'), 0, 0, tiled=True)  4.71 us
    dot_general x2, matrix products, on_device(): jnp.dot(left, right[:, i * half:(i + 1) * half], preferred_element_type=j...  4.35 us
    dynamic_update_slice x3, local copies, waits for them, and re-layouts, on_device(): lax.dynamic_update_slice_in_dim(full, block, (y + shift) % 4 * quarter, 0)  3.41 us
  transfers between devices with their start and end apart: 28, of which 19 were waited for; matrix products, arithmetic and copies ran while one was open for 23% of the time, Pallas kernels for 0%

profile of v4, /device:TPU:6, one launch (start us, length us, event | category | flops | bytes accessed | tf_op | source)
XLA Modules:
  0.0 129.2 jit_solution(15886932792145548544)
XLA Ops:
  0.0 2.0 %constant_dynamic-slice_fusion = (bf16[4,2,1,320,256]{4,3,2,1,0:T(8,128)(2,1)S(1)}, bf16[4,2,320,256]{3,2,1,0:T(8,128)(2,1)S(1)}) fusion(bf16[4,2,2,320,256]{4,3,2,1,0:T(8,128)(2,1)} %bitcast.35, s32[]{:T(128)S(6)} %select_n.53, s32[]{:T(128)S(6)} %select_n.54), kind=kLoop, calls=%fused_computation.60 | loop fusion | bytes 5242888 | tf_op jit(solution)/shard_map/jit(dynamic_index_in_dim)/dynamic_slice | solution.py:71
  4.3 1.3 %collective-permute-done.1 = bf16[256,512]{1,0:T(8,128)(2,1)} collective-permute-done((bf16[256,512]{1,0:T(8,128)(2,1)S(1)}, bf16[256,512]{1,0:T(8,128)(2,1)}, u32[]{:S(2)}, u32[]{:S(2)}) %collective-permute-start.1) | collective-permute-done | bytes 262176 | tf_op jit(solution)/shard_map/ppermute | solution.py:23
  5.6 5.9 %all-to-all-start = ((bf16[8,160,256]{2,1,0:T(8,128)(2,1)}), bf16[8,160,256]{2,1,0:T(8,128)(2,1)S(1)}, u32[]{:S(2)}, u32[]{:S(2)}) async-start(bf16[8,160,256]{2,1,0:T(8,128)(2,1)} %bitcast.5), calls=%async_computation | async-start | bytes 1310720 | tf_op jit(solution)/shard_map/all_to_all | solution.py:79
  11.5 1.7 %constant_dynamic-update-slice_fusion = bf16[512,512]{1,0:T(8,128)(2,1)} fusion(bf16[512,512]{1,0:T(8,128)(2,1)} %constant_dynamic-update-slice_fusion.1, bf16[256,512]{1,0:T(8,128)(2,1)} %collective-permute-done.1), kind=kLoop, calls=%fused_computation.47 | loop fusion | bytes 524288 | tf_op jit(solution)/shard_map/concatenate | solution.py:82
  13.2 2.2 %convolution_convert_fusion = bf16[2560,256]{1,0:T(8,128)(2,1)S(1)} fusion(bf16[2560,256]{1,0:T(8,128)(2,1)} %bitcast.6, bf16[2560,256]{1,0:T(8,128)(2,1)S(1)} %bitcast.40, bf16[512,512]{1,0:T(8,128)(2,1)} %constant_dynamic-update-slice_fusion), kind=kOutput, calls=%fused_computation | convolution fusion | flops 676986880 | bytes 4194304 | tf_op jit(solution)/shard_map/dot_general | solution.py:84
  15.5 0.9 copy-done.8
  16.4 2.2 %convolution_convert_fusion.1 = bf16[2560,256]{1,0:T(8,128)(2,1)S(1)} fusion(bf16[2560,256]{1,0:T(8,128)(2,1)} %bitcast.6, bf16[2560,256]{1,0:T(8,128)(2,1)S(1)} %bitcast.41, bf16[512,512]{1,0:T(8,128)(2,1)S(1)} %copy-done.8), kind=kOutput, calls=%fused_computation.1 | convolution fusion | flops 676986880 | bytes 4194304 | tf_op jit(solution)/shard_map/dot_general | solution.py:84
  18.6 1.7 %pad_maximum_fusion.1 = bf16[4,2,2,320,256]{4,3,2,1,0:T(8,128)(2,1)} fusion(bf16[4,1,2,320,256]{4,3,2,1,0:T(8,128)(2,1)S(1)} %reverse_bitcast_fusion, bf16[4,1,2,320,256]{4,3,2,1,0:T(8,128)(2,1)S(1)} %bitcast.36), kind=kLoop, calls=%fused_computation.3 | loop fusion | flops 1310720 | bytes 5242880 | tf_op jit(solution)/shard_map/stack | solution.py:88
  20.3 1.9 %all-to-all-done = bf16[8,160,256]{2,1,0:T(8,128)(2,1)S(1)} async-done(((bf16[8,160,256]{2,1,0:T(8,128)(2,1)}), bf16[8,160,256]{2,1,0:T(8,128)(2,1)S(1)}, u32[]{:S(2)}, u32[]{:S(2)}) %all-to-all-start) | async-done | bytes 655392 | tf_op jit(solution)/shard_map/all_to_all | solution.py:79
  22.4 4.7 %all-to-all-start.1 = ((bf16[8,640,256]{2,1,0:T(8,128)(2,1)}), bf16[8,640,256]{2,1,0:T(8,128)(2,1)S(1)}, u32[]{:S(2)}, u32[]{:S(2)}) async-start(bf16[8,640,256]{2,1,0:T(8,128)(2,1)} %bitcast.11), calls=%async_computation.1 | async-start | bytes 5242880 | tf_op jit(solution)/shard_map/all_to_all | solution.py:92
  27.1 5.9 %collective-permute-start.2 = (bf16[160,256]{1,0:T(8,128)(2,1)S(1)}, bf16[160,256]{1,0:T(8,128)(2,1)S(1)}, u32[]{:S(2)}, u32[]{:S(2)}) collective-permute-start(bf16[160,256]{1,0:T(8,128)(2,1)S(1)} %get-tuple-element.83), channel_id=1, source_target_pairs={{0,14},{1,15},{2,0},{3,1},{4,2},{5,3},{6,4},{7,5},{8,6},{9,7},{10,... | collective-permute-start | bytes 245768 | tf_op jit(solution)/shard_map/ppermute | solution.py:23
  33.1 1.9 %collective-permute-start.3 = (bf16[160,256]{1,0:T(8,128)(2,1)S(1)}, bf16[160,256]{1,0:T(8,128)(2,1)S(1)}, u32[]{:S(2)}, u32[]{:S(2)}) collective-permute-start(bf16[160,256]{1,0:T(8,128)(2,1)S(1)} %get-tuple-element.82), channel_id=1, source_target_pairs={{0,10},{1,11},{2,12},{3,13},{4,14},{5,15},{6,0},{7,1},{8,2},{9,3},... | collective-permute-start | bytes 245768 | tf_op jit(solution)/shard_map/ppermute | solution.py:23
  35.0 3.4 %collective-permute-start.5 = (bf16[160,256]{1,0:T(8,128)(2,1)S(1)}, bf16[160,256]{1,0:T(8,128)(2,1)S(1)}, u32[]{:S(2)}, u32[]{:S(2)}) collective-permute-start(bf16[160,256]{1,0:T(8,128)(2,1)S(1)} %get-tuple-element.80), channel_id=1, source_target_pairs={{0,6},{1,7},{2,8},{3,9},{4,10},{5,11},{6,12},{7,13},{8,14},{9,15},... | collective-permute-start | bytes 245768 | tf_op jit(solution)/shard_map/ppermute | solution.py:23
  38.5 4.5 %collective-permute-done.3 = bf16[160,256]{1,0:T(8,128)(2,1)S(1)} collective-permute-done((bf16[160,256]{1,0:T(8,128)(2,1)S(1)}, bf16[160,256]{1,0:T(8,128)(2,1)S(1)}, u32[]{:S(2)}, u32[]{:S(2)}) %collective-permute-start.3) | collective-permute-done | bytes 81952 | tf_op jit(solution)/shard_map/ppermute | solution.py:23
  43.0 2.2 %collective-permute-done.4 = bf16[160,256]{1,0:T(8,128)(2,1)S(1)} collective-permute-done((bf16[160,256]{1,0:T(8,128)(2,1)S(1)}, bf16[160,256]{1,0:T(8,128)(2,1)S(1)}, u32[]{:S(2)}, u32[]{:S(2)}) %collective-permute-start.4) | collective-permute-done | bytes 81952 | tf_op jit(solution)/shard_map/ppermute | solution.py:23
  45.2 1.8 %collective-permute-done.5 = bf16[160,256]{1,0:T(8,128)(2,1)S(1)} collective-permute-done((bf16[160,256]{1,0:T(8,128)(2,1)S(1)}, bf16[160,256]{1,0:T(8,128)(2,1)S(1)}, u32[]{:S(2)}, u32[]{:S(2)}) %collective-permute-start.5) | collective-permute-done | bytes 81952 | tf_op jit(solution)/shard_map/ppermute | solution.py:23
  47.0 2.7 %collective-permute-start.6 = (bf16[160,256]{1,0:T(8,128)(2,1)S(1)}, bf16[160,256]{1,0:T(8,128)(2,1)S(1)}, u32[]{:S(2)}, u32[]{:S(2)}) collective-permute-start(bf16[160,256]{1,0:T(8,128)(2,1)S(1)} %get-tuple-element.79), channel_id=1, source_target_pairs={{0,12},{1,13},{2,14},{3,15},{4,0},{5,1},{6,2},{7,3},{8,4},{9,5},{1... | collective-permute-start | bytes 245768 | tf_op jit(solution)/shard_map/ppermute | solution.py:23
  50.0 1.7 %collective-permute-start.8 = (bf16[160,256]{1,0:T(8,128)(2,1)S(1)}, bf16[160,256]{1,0:T(8,128)(2,1)S(1)}, u32[]{:S(2)}, u32[]{:S(2)}) collective-permute-start(bf16[160,256]{1,0:T(8,128)(2,1)S(1)} %get-tuple-element.77), channel_id=1, source_target_pairs={{0,2},{1,3},{2,4},{3,5},{4,6},{5,7},{6,8},{7,9},{8,10},{9,11},{10,... | collective-permute-start | bytes 245768 | tf_op jit(solution)/shard_map/ppermute | solution.py:23
  52.6 4.2 %collective-permute-done.7 = bf16[160,256]{1,0:T(8,128)(2,1)S(1)} collective-permute-done((bf16[160,256]{1,0:T(8,128)(2,1)S(1)}, bf16[160,256]{1,0:T(8,128)(2,1)S(1)}, u32[]{:S(2)}, u32[]{:S(2)}) %collective-permute-start.7) | collective-permute-done | bytes 81952 | tf_op jit(solution)/shard_map/ppermute | solution.py:23
  62.0 1.2 reduce_sum.12
  63.2 1.6 %collective-permute-start.9 = (bf16[640,256]{1,0:T(8,128)(2,1)}, bf16[640,256]{1,0:T(8,128)(2,1)}, u32[]{:S(2)}, u32[]{:S(2)}) collective-permute-start(bf16[640,256]{1,0:T(8,128)(2,1)} %reduce_sum.12), channel_id=1, source_target_pairs={{0,14},{1,15},{2,0},{3,1},{4,2},{5,3},{6,4},{7,5},{8,6},{9,7},{10,... | collective-permute-start | bytes 983048 | tf_op jit(solution)/shard_map/ppermute | solution.py:23
  65.2 1.5 %collective-permute-start.13 = (bf16[160,2048]{1,0:T(8,128)(2,1)}, bf16[160,2048]{1,0:T(8,128)(2,1)S(1)}, u32[]{:S(2)}, u32[]{:S(2)}) collective-permute-start(bf16[160,2048]{1,0:T(8,128)(2,1)} %constant_dynamic-update-slice_fusion.2), channel_id=1, source_target_pairs={{0,64},{1,65},{2,66},{3,67},{4,68},{5,69},{6,70},{7,71},{8,72},{9,... | collective-permute-start | bytes 1966088 | tf_op jit(solution)/shard_map/ppermute | solution.py:23
  66.7 1.7 %collective-permute-start.14 = (bf16[160,2048]{1,0:T(8,128)(2,1)}, bf16[160,2048]{1,0:T(8,128)(2,1)}, u32[]{:S(2)}, u32[]{:S(2)}) collective-permute-start(bf16[160,2048]{1,0:T(8,128)(2,1)} %constant_dynamic-update-slice_fusion.2), channel_id=1, source_target_pairs={{0,192},{1,193},{2,194},{3,195},{4,196},{5,197},{6,198},{7,199},{8... | collective-permute-start | bytes 1966088 | tf_op jit(solution)/shard_map/ppermute | solution.py:23
  68.4 2.1 %collective-permute-done.9 = bf16[640,256]{1,0:T(8,128)(2,1)} collective-permute-done((bf16[640,256]{1,0:T(8,128)(2,1)}, bf16[640,256]{1,0:T(8,128)(2,1)}, u32[]{:S(2)}, u32[]{:S(2)}) %collective-permute-start.9) | collective-permute-done | bytes 327712 | tf_op jit(solution)/shard_map/ppermute | solution.py:23
  70.6 2.9 %collective-permute-done.10 = bf16[640,256]{1,0:T(8,128)(2,1)} collective-permute-done((bf16[640,256]{1,0:T(8,128)(2,1)}, bf16[640,256]{1,0:T(8,128)(2,1)}, u32[]{:S(2)}, u32[]{:S(2)}) %collective-permute-start.10) | collective-permute-done | bytes 327712 | tf_op jit(solution)/shard_map/ppermute | solution.py:23
  73.8 1.7 %collective-permute-start.12 = (bf16[640,256]{1,0:T(8,128)(2,1)}, bf16[640,256]{1,0:T(8,128)(2,1)S(1)}, u32[]{:S(2)}, u32[]{:S(2)}) collective-permute-start(bf16[640,256]{1,0:T(8,128)(2,1)} %collective-permute-done.10), channel_id=1, source_target_pairs={{0,2},{1,3},{2,4},{3,5},{4,6},{5,7},{6,8},{7,9},{8,10},{9,11},{10,... | collective-permute-start | bytes 983048 | tf_op jit(solution)/shard_map/ppermute | solution.py:23
  75.8 1.1 constant_dynamic-update-slice_fusion.12
  77.0 2.2 %pad_maximum_fusion.4 = bf16[640,768]{1,0:T(8,128)(2,1)} fusion(bf16[640,256]{1,0:T(8,128)(2,1)} %collective-permute-done.10, bf16[640,256]{1,0:T(8,128)(2,1)} %collective-permute-done.9, bf16[640,256]{1,0:T(8,128)(2,1)} %reduce_sum.12), kind=kLoop, calls=%fused_computation.20 | loop fusion | flops 2949120 | bytes 1966080 | tf_op jit(solution)/shard_map/concatenate | solution.py:106
  79.2 1.6 %collective-permute-done.13 = bf16[160,2048]{1,0:T(8,128)(2,1)S(1)} collective-permute-done((bf16[160,2048]{1,0:T(8,128)(2,1)}, bf16[160,2048]{1,0:T(8,128)(2,1)S(1)}, u32[]{:S(2)}, u32[]{:S(2)}) %collective-permute-start.13) | collective-permute-done | bytes 655392 | tf_op jit(solution)/shard_map/ppermute | solution.py:23
  80.8 1.0 collective-permute-done.14
  82.2 2.4 %collective-permute-start.15 = (bf16[640,256]{1,0:T(8,128)(2,1)S(1)}, bf16[640,256]{1,0:T(8,128)(2,1)S(1)}, u32[]{:S(2)}, u32[]{:S(2)}) collective-permute-start(bf16[640,256]{1,0:T(8,128)(2,1)S(1)} %collective-permute-done.11), channel_id=1, source_target_pairs={{0,14},{1,15},{2,0},{3,1},{4,2},{5,3},{6,4},{7,5},{8,6},{9,7},{10,... | collective-permute-start | bytes 983048 | tf_op jit(solution)/shard_map/ppermute | solution.py:23
  84.7 2.9 %collective-permute-start.17 = (bf16[160,1024]{1,0:T(8,128)(2,1)S(1)}, bf16[160,1024]{1,0:T(8,128)(2,1)S(1)}, u32[]{:S(2)}, u32[]{:S(2)}) collective-permute-start(bf16[160,1024]{1,0:T(8,128)(2,1)S(1)} %slice.95), channel_id=1, source_target_pairs={{0,64},{1,65},{2,66},{3,67},{4,68},{5,69},{6,70},{7,71},{8,72},{9,... | collective-permute-start | bytes 983048 | tf_op jit(solution)/shard_map/ppermute | solution.py:23
  87.7 1.0 slice.96
  89.1 1.1 constant_dynamic-update-slice_fusion.11
  90.3 1.1 constant_dynamic-update-slice_fusion.10
  91.5 1.5 %collective-permute-done.16 = bf16[640,256]{1,0:T(8,128)(2,1)S(1)} collective-permute-done((bf16[640,256]{1,0:T(8,128)(2,1)S(1)}, bf16[640,256]{1,0:T(8,128)(2,1)S(1)}, u32[]{:S(2)}, u32[]{:S(2)}) %collective-permute-start.16) | collective-permute-done | bytes 327712 | tf_op jit(solution)/shard_map/ppermute | solution.py:23
  93.1 2.7 %collective-permute-done.18 = bf16[160,1024]{1,0:T(8,128)(2,1)S(1)} collective-permute-done((bf16[160,1024]{1,0:T(8,128)(2,1)S(1)}, bf16[160,1024]{1,0:T(8,128)(2,1)S(1)}, u32[]{:S(2)}, u32[]{:S(2)}) %collective-permute-start.18) | collective-permute-done | bytes 327712 | tf_op jit(solution)/shard_map/ppermute | solution.py:23
  98.2 3.1 %collective-permute-start.20 = (bf16[320,256]{1,0:T(8,128)(2,1)S(1)}, bf16[320,256]{1,0:T(8,128)(2,1)S(1)}, u32[]{:S(2)}, u32[]{:S(2)}) collective-permute-start(bf16[320,256]{1,0:T(8,128)(2,1)S(1)} %slice.99), channel_id=1, source_target_pairs={{0,14},{1,15},{2,0},{3,1},{4,2},{5,3},{6,4},{7,5},{8,6},{9,7},{10,... | collective-permute-start | bytes 491528 | tf_op jit(solution)/shard_map/ppermute | solution.py:23
  101.3 2.1 %broadcast_select_fusion = (bf16[640,2048]{1,0:T(8,128)(2,1)S(1)}, bf16[640,2048]{1,0:T(8,128)(2,1)S(1)}) fusion(bf16[640,2048]{1,0:T(8,128)(2,1)} %collective-permute-done.19, bf16[640,2048]{1,0:T(8,128)(2,1)S(1)} %maximum_dynamic-update-slice_fusion, pred[]{:T(512)S(6)} %eq.9), kind=kLoop, calls=%fused_computation.4 | loop fusion | flops 2621440 | bytes 10485761 | tf_op jit(solution)/shard_map/jit(_where)/select_n | solution.py:119
  103.4 1.0 fusion.10
  105.1 1.0 fusion.4
  107.1 1.0 fusion.29
  108.3 1.3 %collective-permute-start.22 = (bf16[160,640]{1,0:T(8,128)(2,1)S(1)}, bf16[160,640]{1,0:T(8,128)(2,1)S(1)}, u32[]{:S(2)}, u32[]{:S(2)}) collective-permute-start(bf16[160,640]{1,0:T(8,128)(2,1)S(1)} %get-tuple-element.75), channel_id=1, source_target_pairs={{0,32},{1,33},{2,34},{3,35},{4,36},{5,37},{6,38},{7,39},{8,40},{9,... | collective-permute-start | bytes 614408 | tf_op jit(solution)/shard_map/ppermute | solution.py:23
  109.6 1.0 add_add_fusion.1
  110.6 5.7 %collective-permute-done.24 = bf16[160,640]{1,0:T(8,128)(2,1)S(1)} collective-permute-done((bf16[160,640]{1,0:T(8,128)(2,1)S(1)}, bf16[160,640]{1,0:T(8,128)(2,1)S(1)}, u32[]{:S(2)}, u32[]{:S(2)}) %collective-permute-start.24) | collective-permute-done | bytes 204832 | tf_op jit(solution)/shard_map/ppermute | solution.py:23
  116.6 1.6 %collective-permute-start.23 = (bf16[320,640]{1,0:T(8,128)(2,1)S(1)}, bf16[320,640]{1,0:T(8,128)(2,1)S(1)}, u32[]{:S(2)}, u32[]{:S(2)}) collective-permute-start(bf16[320,640]{1,0:T(8,128)(2,1)S(1)} %fusion.13), channel_id=1, source_target_pairs={{0,33},{1,32},{2,35},{3,34},{4,37},{5,36},{6,39},{7,38},{8,41},{9,... | collective-permute-start | bytes 1228808 | tf_op jit(solution)/shard_map/ppermute | solution.py:23
  118.3 8.7 %collective-permute-done.25 = bf16[320,640]{1,0:T(8,128)(2,1)S(1)} collective-permute-done((bf16[320,640]{1,0:T(8,128)(2,1)S(1)}, bf16[320,640]{1,0:T(8,128)(2,1)S(1)}, u32[]{:S(2)}, u32[]{:S(2)}) %collective-permute-start.25) | collective-permute-done | bytes 409632 | tf_op jit(solution)/shard_map/ppermute | solution.py:23
  127.0 1.4 %collective-permute-done.23 = bf16[320,640]{1,0:T(8,128)(2,1)S(1)} collective-permute-done((bf16[320,640]{1,0:T(8,128)(2,1)S(1)}, bf16[320,640]{1,0:T(8,128)(2,1)S(1)}, u32[]{:S(2)}, u32[]{:S(2)}) %collective-permute-start.23) | collective-permute-done | bytes 409632 | tf_op jit(solution)/shard_map/ppermute | solution.py:23
  (69 shorter events, 16.6 us)
Async XLA Ops:
  0.0 2.1 %copy-start.7 = (bf16[256,512]{1,0:T(8,128)(2,1)S(1)}, bf16[256,512]{1,0:T(8,128)(2,1)}, u32[]{:S(2)}) copy-start(bf16[256,512]{1,0:T(8,128)(2,1)} %param.3) | copy-start | bytes 786436
  0.0 2.6 %copy-start.6 = (bf16[640,512]{1,0:T(8,128)(2,1)S(1)}, bf16[640,512]{1,0:T(8,128)(2,1)}, u32[]{:S(2)}) copy-start(bf16[640,512]{1,0:T(8,128)(2,1)} %param.5) | copy-start | bytes 1966084
  2.0 3.6 %collective-permute-start = (bf16[4,2,320,256]{3,2,1,0:T(8,128)(2,1)S(1)}, bf16[4,2,320,256]{3,2,1,0:T(8,128)(2,1)}, u32[]{:S(2)}, u32[]{:S(2)}) collective-permute-start(bf16[4,2,320,256]{3,2,1,0:T(8,128)(2,1)S(1)} %get-tuple-element.74), channel_id=1, source_target_pairs={{0,16},{1,17},{2,18},{3,19},{4,20},{5,21},{6,22},{7,23},{8,24},{9,... | collective-permute-start | bytes 3932168 | tf_op jit(solution)/shard_map/ppermute | solution.py:23
  2.1 3.5 %collective-permute-start.1 = (bf16[256,512]{1,0:T(8,128)(2,1)S(1)}, bf16[256,512]{1,0:T(8,128)(2,1)}, u32[]{:S(2)}, u32[]{:S(2)}) collective-permute-start(bf16[256,512]{1,0:T(8,128)(2,1)S(1)} %copy-done.7), channel_id=1, source_target_pairs={{0,16},{1,17},{2,18},{3,19},{4,20},{5,21},{6,22},{7,23},{8,24},{9,... | collective-permute-start | bytes 786440 | tf_op jit(solution)/shard_map/ppermute | solution.py:23
  5.6 16.6 %all-to-all-start = ((bf16[8,160,256]{2,1,0:T(8,128)(2,1)}), bf16[8,160,256]{2,1,0:T(8,128)(2,1)S(1)}, u32[]{:S(2)}, u32[]{:S(2)}) async-start(bf16[8,160,256]{2,1,0:T(8,128)(2,1)} %bitcast.5), calls=%async_computation | async-start | bytes 1310720 | tf_op jit(solution)/shard_map/all_to_all | solution.py:79
  15.4 1.0 copy-start.8
  22.4 39.6 %all-to-all-start.1 = ((bf16[8,640,256]{2,1,0:T(8,128)(2,1)}), bf16[8,640,256]{2,1,0:T(8,128)(2,1)S(1)}, u32[]{:S(2)}, u32[]{:S(2)}) async-start(bf16[8,640,256]{2,1,0:T(8,128)(2,1)} %bitcast.11), calls=%async_computation.1 | async-start | bytes 5242880 | tf_op jit(solution)/shard_map/all_to_all | solution.py:92
  27.1 11.3 %collective-permute-start.2 = (bf16[160,256]{1,0:T(8,128)(2,1)S(1)}, bf16[160,256]{1,0:T(8,128)(2,1)S(1)}, u32[]{:S(2)}, u32[]{:S(2)}) collective-permute-start(bf16[160,256]{1,0:T(8,128)(2,1)S(1)} %get-tuple-element.83), channel_id=1, source_target_pairs={{0,14},{1,15},{2,0},{3,1},{4,2},{5,3},{6,4},{7,5},{8,6},{9,7},{10,... | collective-permute-start | bytes 245768 | tf_op jit(solution)/shard_map/ppermute | solution.py:23
  33.1 9.9 %collective-permute-start.3 = (bf16[160,256]{1,0:T(8,128)(2,1)S(1)}, bf16[160,256]{1,0:T(8,128)(2,1)S(1)}, u32[]{:S(2)}, u32[]{:S(2)}) collective-permute-start(bf16[160,256]{1,0:T(8,128)(2,1)S(1)} %get-tuple-element.82), channel_id=1, source_target_pairs={{0,10},{1,11},{2,12},{3,13},{4,14},{5,15},{6,0},{7,1},{8,2},{9,3},... | collective-permute-start | bytes 245768 | tf_op jit(solution)/shard_map/ppermute | solution.py:23
  35.0 10.3 %collective-permute-start.4 = (bf16[160,256]{1,0:T(8,128)(2,1)S(1)}, bf16[160,256]{1,0:T(8,128)(2,1)S(1)}, u32[]{:S(2)}, u32[]{:S(2)}) collective-permute-start(bf16[160,256]{1,0:T(8,128)(2,1)S(1)} %get-tuple-element.81), channel_id=1, source_target_pairs={{0,8},{1,9},{2,10},{3,11},{4,12},{5,13},{6,14},{7,15},{8,0},{9,1},... | collective-permute-start | bytes 245768 | tf_op jit(solution)/shard_map/ppermute | solution.py:23
  35.0 12.0 %collective-permute-start.5 = (bf16[160,256]{1,0:T(8,128)(2,1)S(1)}, bf16[160,256]{1,0:T(8,128)(2,1)S(1)}, u32[]{:S(2)}, u32[]{:S(2)}) collective-permute-start(bf16[160,256]{1,0:T(8,128)(2,1)S(1)} %get-tuple-element.80), channel_id=1, source_target_pairs={{0,6},{1,7},{2,8},{3,9},{4,10},{5,11},{6,12},{7,13},{8,14},{9,15},... | collective-permute-start | bytes 245768 | tf_op jit(solution)/shard_map/ppermute | solution.py:23
  47.0 5.5 %collective-permute-start.6 = (bf16[160,256]{1,0:T(8,128)(2,1)S(1)}, bf16[160,256]{1,0:T(8,128)(2,1)S(1)}, u32[]{:S(2)}, u32[]{:S(2)}) collective-permute-start(bf16[160,256]{1,0:T(8,128)(2,1)S(1)} %get-tuple-element.79), channel_id=1, source_target_pairs={{0,12},{1,13},{2,14},{3,15},{4,0},{5,1},{6,2},{7,3},{8,4},{9,5},{1... | collective-permute-start | bytes 245768 | tf_op jit(solution)/shard_map/ppermute | solution.py:23
  49.7 7.1 %collective-permute-start.7 = (bf16[160,256]{1,0:T(8,128)(2,1)S(1)}, bf16[160,256]{1,0:T(8,128)(2,1)S(1)}, u32[]{:S(2)}, u32[]{:S(2)}) collective-permute-start(bf16[160,256]{1,0:T(8,128)(2,1)S(1)} %get-tuple-element.78), channel_id=1, source_target_pairs={{0,4},{1,5},{2,6},{3,7},{4,8},{5,9},{6,10},{7,11},{8,12},{9,13},{1... | collective-permute-start | bytes 245768 | tf_op jit(solution)/shard_map/ppermute | solution.py:23
  50.0 6.8 %collective-permute-start.8 = (bf16[160,256]{1,0:T(8,128)(2,1)S(1)}, bf16[160,256]{1,0:T(8,128)(2,1)S(1)}, u32[]{:S(2)}, u32[]{:S(2)}) collective-permute-start(bf16[160,256]{1,0:T(8,128)(2,1)S(1)} %get-tuple-element.77), channel_id=1, source_target_pairs={{0,2},{1,3},{2,4},{3,5},{4,6},{5,7},{6,8},{7,9},{8,10},{9,11},{10,... | collective-permute-start | bytes 245768 | tf_op jit(solution)/shard_map/ppermute | solution.py:23
  63.2 7.4 %collective-permute-start.9 = (bf16[640,256]{1,0:T(8,128)(2,1)}, bf16[640,256]{1,0:T(8,128)(2,1)}, u32[]{:S(2)}, u32[]{:S(2)}) collective-permute-start(bf16[640,256]{1,0:T(8,128)(2,1)} %reduce_sum.12), channel_id=1, source_target_pairs={{0,14},{1,15},{2,0},{3,1},{4,2},{5,3},{6,4},{7,5},{8,6},{9,7},{10,... | collective-permute-start | bytes 983048 | tf_op jit(solution)/shard_map/ppermute | solution.py:23
  64.8 8.7 %collective-permute-start.10 = (bf16[640,256]{1,0:T(8,128)(2,1)}, bf16[640,256]{1,0:T(8,128)(2,1)}, u32[]{:S(2)}, u32[]{:S(2)}) collective-permute-start(bf16[640,256]{1,0:T(8,128)(2,1)} %reduce_sum.12), channel_id=1, source_target_pairs={{0,2},{1,3},{2,4},{3,5},{4,6},{5,7},{6,8},{7,9},{8,10},{9,11},{10,... | collective-permute-start | bytes 983048 | tf_op jit(solution)/shard_map/ppermute | solution.py:23
  65.2 15.6 %collective-permute-start.13 = (bf16[160,2048]{1,0:T(8,128)(2,1)}, bf16[160,2048]{1,0:T(8,128)(2,1)S(1)}, u32[]{:S(2)}, u32[]{:S(2)}) collective-permute-start(bf16[160,2048]{1,0:T(8,128)(2,1)} %constant_dynamic-update-slice_fusion.2), channel_id=1, source_target_pairs={{0,64},{1,65},{2,66},{3,67},{4,68},{5,69},{6,70},{7,71},{8,72},{9,... | collective-permute-start | bytes 1966088 | tf_op jit(solution)/shard_map/ppermute | solution.py:23
  66.7 15.0 %collective-permute-start.14 = (bf16[160,2048]{1,0:T(8,128)(2,1)}, bf16[160,2048]{1,0:T(8,128)(2,1)}, u32[]{:S(2)}, u32[]{:S(2)}) collective-permute-start(bf16[160,2048]{1,0:T(8,128)(2,1)} %constant_dynamic-update-slice_fusion.2), channel_id=1, source_target_pairs={{0,192},{1,193},{2,194},{3,195},{4,196},{5,197},{6,198},{7,199},{8... | collective-permute-start | bytes 1966088 | tf_op jit(solution)/shard_map/ppermute | solution.py:23
  73.5 8.3 %collective-permute-start.11 = (bf16[640,256]{1,0:T(8,128)(2,1)}, bf16[640,256]{1,0:T(8,128)(2,1)S(1)}, u32[]{:S(2)}, u32[]{:S(2)}) collective-permute-start(bf16[640,256]{1,0:T(8,128)(2,1)} %collective-permute-done.9), channel_id=1, source_target_pairs={{0,14},{1,15},{2,0},{3,1},{4,2},{5,3},{6,4},{7,5},{8,6},{9,7},{10,... | collective-permute-start | bytes 983048 | tf_op jit(solution)/shard_map/ppermute | solution.py:23
  73.8 8.5 %collective-permute-start.12 = (bf16[640,256]{1,0:T(8,128)(2,1)}, bf16[640,256]{1,0:T(8,128)(2,1)S(1)}, u32[]{:S(2)}, u32[]{:S(2)}) collective-permute-start(bf16[640,256]{1,0:T(8,128)(2,1)} %collective-permute-done.10), channel_id=1, source_target_pairs={{0,2},{1,3},{2,4},{3,5},{4,6},{5,7},{6,8},{7,9},{8,10},{9,11},{10,... | collective-permute-start | bytes 983048 | tf_op jit(solution)/shard_map/ppermute | solution.py:23
  80.8 8.4 %copy-start = (bf16[160,2048]{1,0:T(8,128)(2,1)}, bf16[160,2048]{1,0:T(8,128)(2,1)S(1)}, u32[]{:S(2)}) copy-start(bf16[160,2048]{1,0:T(8,128)(2,1)S(1)} %collective-permute-done.13) | copy-start | bytes 1966084
  82.2 9.2 %collective-permute-start.15 = (bf16[640,256]{1,0:T(8,128)(2,1)S(1)}, bf16[640,256]{1,0:T(8,128)(2,1)S(1)}, u32[]{:S(2)}, u32[]{:S(2)}) collective-permute-start(bf16[640,256]{1,0:T(8,128)(2,1)S(1)} %collective-permute-done.11), channel_id=1, source_target_pairs={{0,14},{1,15},{2,0},{3,1},{4,2},{5,3},{6,4},{7,5},{8,6},{9,7},{10,... | collective-permute-start | bytes 983048 | tf_op jit(solution)/shard_map/ppermute | solution.py:23
  84.7 8.3 %collective-permute-start.16 = (bf16[640,256]{1,0:T(8,128)(2,1)S(1)}, bf16[640,256]{1,0:T(8,128)(2,1)S(1)}, u32[]{:S(2)}, u32[]{:S(2)}) collective-permute-start(bf16[640,256]{1,0:T(8,128)(2,1)S(1)} %collective-permute-done.12), channel_id=1, source_target_pairs={{0,2},{1,3},{2,4},{3,5},{4,6},{5,7},{6,8},{7,9},{8,10},{9,11},{10,... | collective-permute-start | bytes 983048 | tf_op jit(solution)/shard_map/ppermute | solution.py:23
  84.7 8.4 %collective-permute-start.17 = (bf16[160,1024]{1,0:T(8,128)(2,1)S(1)}, bf16[160,1024]{1,0:T(8,128)(2,1)S(1)}, u32[]{:S(2)}, u32[]{:S(2)}) collective-permute-start(bf16[160,1024]{1,0:T(8,128)(2,1)S(1)} %slice.95), channel_id=1, source_target_pairs={{0,64},{1,65},{2,66},{3,67},{4,68},{5,69},{6,70},{7,71},{8,72},{9,... | collective-permute-start | bytes 983048 | tf_op jit(solution)/shard_map/ppermute | solution.py:23
  88.7 7.2 %collective-permute-start.18 = (bf16[160,1024]{1,0:T(8,128)(2,1)S(1)}, bf16[160,1024]{1,0:T(8,128)(2,1)S(1)}, u32[]{:S(2)}, u32[]{:S(2)}) collective-permute-start(bf16[160,1024]{1,0:T(8,128)(2,1)S(1)} %slice.96), channel_id=1, source_target_pairs={{0,192},{1,193},{2,194},{3,195},{4,196},{5,197},{6,198},{7,199},{8... | collective-permute-start | bytes 983048 | tf_op jit(solution)/shard_map/ppermute | solution.py:23
  91.5 4.4 %copy-start.2 = (bf16[640,256]{1,0:T(8,128)(2,1)}, bf16[640,256]{1,0:T(8,128)(2,1)S(1)}, u32[]{:S(2)}) copy-start(bf16[640,256]{1,0:T(8,128)(2,1)S(1)} %collective-permute-done.15) | copy-start | bytes 983044
  93.0 2.9 %copy-start.4 = (bf16[640,256]{1,0:T(8,128)(2,1)}, bf16[640,256]{1,0:T(8,128)(2,1)S(1)}, u32[]{:S(2)}) copy-start(bf16[640,256]{1,0:T(8,128)(2,1)S(1)} %collective-permute-done.16) | copy-start | bytes 983044
  95.9 5.4 %collective-permute-start.19 = (bf16[640,2048]{1,0:T(8,128)(2,1)S(1)}, bf16[640,2048]{1,0:T(8,128)(2,1)}, u32[]{:S(2)}, u32[]{:S(2)}) collective-permute-start(bf16[640,2048]{1,0:T(8,128)(2,1)S(1)} %maximum_dynamic-update-slice_fusion), channel_id=1, source_target_pairs={{0,16},{1,17},{2,18},{3,19},{4,20},{5,21},{6,22},{7,23},{8,24},{9,... | collective-permute-start | bytes 7864328 | tf_op jit(solution)/shard_map/ppermute | solution.py:23
  97.0 9.8 %collective-permute-start.21 = (bf16[320,256]{1,0:T(8,128)(2,1)S(1)}, bf16[320,256]{1,0:T(8,128)(2,1)S(1)}, u32[]{:S(2)}, u32[]{:S(2)}) collective-permute-start(bf16[320,256]{1,0:T(8,128)(2,1)S(1)} %slice.100), channel_id=1, source_target_pairs={{0,2},{1,3},{2,4},{3,5},{4,6},{5,7},{6,8},{7,9},{8,10},{9,11},{10,... | collective-permute-start | bytes 491528 | tf_op jit(solution)/shard_map/ppermute | solution.py:23
  98.2 5.2 %copy-start.1 = (bf16[640,768]{1,0:T(8,128)(2,1)S(1)}, bf16[640,768]{1,0:T(8,128)(2,1)}, u32[]{:S(2)}) copy-start(bf16[640,768]{1,0:T(8,128)(2,1)} %pad_maximum_fusion.4) | copy-start | bytes 2949124
  98.2 8.6 %collective-permute-start.20 = (bf16[320,256]{1,0:T(8,128)(2,1)S(1)}, bf16[320,256]{1,0:T(8,128)(2,1)S(1)}, u32[]{:S(2)}, u32[]{:S(2)}) collective-permute-start(bf16[320,256]{1,0:T(8,128)(2,1)S(1)} %slice.99), channel_id=1, source_target_pairs={{0,14},{1,15},{2,0},{3,1},{4,2},{5,3},{6,4},{7,5},{8,6},{9,7},{10,... | collective-permute-start | bytes 491528 | tf_op jit(solution)/shard_map/ppermute | solution.py:23
  106.0 1.0 copy-start.3
  106.0 1.1 copy-start.5
  108.2 8.2 %collective-permute-start.24 = (bf16[160,640]{1,0:T(8,128)(2,1)S(1)}, bf16[160,640]{1,0:T(8,128)(2,1)S(1)}, u32[]{:S(2)}, u32[]{:S(2)}) collective-permute-start(bf16[160,640]{1,0:T(8,128)(2,1)S(1)} %get-tuple-element.76), channel_id=1, source_target_pairs={{0,33},{1,32},{2,35},{3,34},{4,37},{5,36},{6,39},{7,38},{8,41},{9,... | collective-permute-start | bytes 614408 | tf_op jit(solution)/shard_map/ppermute | solution.py:23
  108.3 8.3 %collective-permute-start.22 = (bf16[160,640]{1,0:T(8,128)(2,1)S(1)}, bf16[160,640]{1,0:T(8,128)(2,1)S(1)}, u32[]{:S(2)}, u32[]{:S(2)}) collective-permute-start(bf16[160,640]{1,0:T(8,128)(2,1)S(1)} %get-tuple-element.75), channel_id=1, source_target_pairs={{0,32},{1,33},{2,34},{3,35},{4,36},{5,37},{6,38},{7,39},{8,40},{9,... | collective-permute-start | bytes 614408 | tf_op jit(solution)/shard_map/ppermute | solution.py:23
  116.4 10.5 %collective-permute-start.25 = (bf16[320,640]{1,0:T(8,128)(2,1)S(1)}, bf16[320,640]{1,0:T(8,128)(2,1)S(1)}, u32[]{:S(2)}, u32[]{:S(2)}) collective-permute-start(bf16[320,640]{1,0:T(8,128)(2,1)S(1)} %fusion.12), channel_id=1, source_target_pairs={{0,32},{1,33},{2,34},{3,35},{4,36},{5,37},{6,38},{7,39},{8,40},{9,... | collective-permute-start | bytes 1228808 | tf_op jit(solution)/shard_map/ppermute | solution.py:23
  116.6 11.7 %collective-permute-start.23 = (bf16[320,640]{1,0:T(8,128)(2,1)S(1)}, bf16[320,640]{1,0:T(8,128)(2,1)S(1)}, u32[]{:S(2)}, u32[]{:S(2)}) collective-permute-start(bf16[320,640]{1,0:T(8,128)(2,1)S(1)} %fusion.13), channel_id=1, source_target_pairs={{0,33},{1,32},{2,35},{3,34},{4,37},{5,36},{6,39},{7,38},{8,41},{9,... | collective-permute-start | bytes 1228808 | tf_op jit(solution)/shard_map/ppermute | solution.py:23

commit v5 on v4

--- a/solution.py
+++ b/solution.py
@@ -113,7 +113,7 @@
     for shift, block in ((0, cols), (1, above), (3, below), (2, jnp.concatenate(far, 1))):
         full = lax.dynamic_update_slice_in_dim(full, block, (y + shift) % 4 * quarter, 0)
     other = send(full, other_core)
-    across = jnp.concatenate([send(up3[:m], z_by(-1)), send(down3[m:], z_by(1))])
+    across = send(up3, z_by(-1))
     third = jnp.concatenate((up3, down3, across), 1)
     near = jnp.where(xh == co, full, other)
     far = jnp.where(xh == co, other, full)

time: 130 us -> 136 us (1.046)
  waiting for transfers between devices: 45.2 us -> 51.4 us
  starting transfers between devices: 46.9 us -> 45.1 us
    ppermute x26 -> x25, waiting for transfers between devices: 43.4 us -> 49.5 us  [send(): return lax.ppermute(value, AXES, pairs(move))]
    slice x2 -> x0, local copies, waits for them, and re-layouts: 1.86 us -> none  [the longest x1 0.93 us: on_device(): down3[m:]]
    ppermute x26 -> x25, starting transfers between devices: 36.3 us -> 34.5 us  [send(): return lax.ppermute(value, AXES, pairs(move))]
    unnamed x26 -> x22, local copies, waits for them, and re-layouts: 6.56 us -> 8.27 us
  transfers between devices with their start and end apart: 28 -> 27, of which waited for: 19 -> 20; matrix products, arithmetic and copies ran while one was open for 23% -> 19% of each run, Pallas kernels for 0% -> 0%
where the time goes in v5:
time: 136 us; the launch traced here: 135 us
  waiting for transfers between devices  51.4 us (38%)
  starting transfers between devices  45.1 us (33%)
  local copies, waits for them, and re-layouts  18.5 us (14%)
  matrix products  9.76 us (7%)
  other arithmetic  9.54 us (7%)
    ppermute x25, waiting for transfers between devices, send(): return lax.ppermute(value, AXES, pairs(move))  49.5 us
    ppermute x25, starting transfers between devices, send(): return lax.ppermute(value, AXES, pairs(move))  34.5 us
    unnamed x22, local copies, waits for them, and re-layouts  8.27 us
    all_to_all x1, starting transfers between devices, on_device(): pieces = lax.all_to_all(pieces, ('y', 'xl'), 0, 0, tiled=True)  5.93 us
    dot_general x6, matrix products, dot_f32(): lax.dot_general(left, right, (((1,), (1,)), ((), ())), preferred_element_...  5.42 us
    all_to_all x1, starting transfers between devices, on_device(): part = lax.all_to_all(part, ('y', 'xl'), 0, 0, tiled=True)  4.71 us
    dot_general x2, matrix products, on_device(): jnp.dot(left, right[:, i * half:(i + 1) * half], preferred_element_type=j...  4.34 us
    dynamic_update_slice x3, local copies, waits for them, and re-layouts, on_device(): lax.dynamic_update_slice_in_dim(full, block, (y + shift) % 4 * quarter, 0)  3.41 us
  transfers between devices with their start and end apart: 27, of which 20 were waited for; matrix products, arithmetic and copies ran while one was open for 19% of the time, Pallas kernels for 0%

profile of v5, /device:TPU:6, one launch (start us, length us, event | category | flops | bytes accessed | tf_op | source)
XLA Modules:
  0.0 134.6 jit_solution(16790333449915894555)
XLA Ops:
  0.0 2.0 %constant_dynamic-slice_fusion = (bf16[4,2,1,320,256]{4,3,2,1,0:T(8,128)(2,1)S(1)}, bf16[4,2,320,256]{3,2,1,0:T(8,128)(2,1)S(1)}) fusion(bf16[4,2,2,320,256]{4,3,2,1,0:T(8,128)(2,1)} %bitcast.37, s32[]{:T(128)S(6)} %select_n.53, s32[]{:T(128)S(6)} %select_n.54), kind=kLoop, calls=%fused_computation.62 | loop fusion | bytes 5242888 | tf_op jit(solution)/shard_map/jit(dynamic_index_in_dim)/dynamic_slice | solution.py:71
  4.2 1.4 %collective-permute-done.1 = bf16[256,512]{1,0:T(8,128)(2,1)} collective-permute-done((bf16[256,512]{1,0:T(8,128)(2,1)S(1)}, bf16[256,512]{1,0:T(8,128)(2,1)}, u32[]{:S(2)}, u32[]{:S(2)}) %collective-permute-start.1) | collective-permute-done | bytes 262176 | tf_op jit(solution)/shard_map/ppermute | solution.py:23
  5.6 5.9 %all-to-all-start = ((bf16[8,160,256]{2,1,0:T(8,128)(2,1)}), bf16[8,160,256]{2,1,0:T(8,128)(2,1)S(1)}, u32[]{:S(2)}, u32[]{:S(2)}) async-start(bf16[8,160,256]{2,1,0:T(8,128)(2,1)} %bitcast.5), calls=%async_computation | async-start | bytes 1310720 | tf_op jit(solution)/shard_map/all_to_all | solution.py:79
  11.5 1.7 %constant_dynamic-update-slice_fusion = bf16[512,512]{1,0:T(8,128)(2,1)} fusion(bf16[512,512]{1,0:T(8,128)(2,1)} %constant_dynamic-update-slice_fusion.1, bf16[256,512]{1,0:T(8,128)(2,1)} %collective-permute-done.1), kind=kLoop, calls=%fused_computation.46 | loop fusion | bytes 524288 | tf_op jit(solution)/shard_map/concatenate | solution.py:82
  13.2 2.2 %convolution_convert_fusion = bf16[2560,256]{1,0:T(8,128)(2,1)S(1)} fusion(bf16[2560,256]{1,0:T(8,128)(2,1)} %bitcast.6, bf16[2560,256]{1,0:T(8,128)(2,1)S(1)} %bitcast.42, bf16[512,512]{1,0:T(8,128)(2,1)} %constant_dynamic-update-slice_fusion), kind=kOutput, calls=%fused_computation | convolution fusion | flops 676986880 | bytes 4194304 | tf_op jit(solution)/shard_map/dot_general | solution.py:84
  16.4 2.2 %convolution_convert_fusion.1 = bf16[2560,256]{1,0:T(8,128)(2,1)S(1)} fusion(bf16[2560,256]{1,0:T(8,128)(2,1)} %bitcast.6, bf16[2560,256]{1,0:T(8,128)(2,1)S(1)} %bitcast.43, bf16[512,512]{1,0:T(8,128)(2,1)S(1)} %copy-done.5), kind=kOutput, calls=%fused_computation.1 | convolution fusion | flops 676986880 | bytes 4194304 | tf_op jit(solution)/shard_map/dot_general | solution.py:84
  18.6 1.7 %pad_maximum_fusion.1 = bf16[4,2,2,320,256]{4,3,2,1,0:T(8,128)(2,1)} fusion(bf16[4,1,2,320,256]{4,3,2,1,0:T(8,128)(2,1)S(1)} %reverse_bitcast_fusion, bf16[4,1,2,320,256]{4,3,2,1,0:T(8,128)(2,1)S(1)} %bitcast.38), kind=kLoop, calls=%fused_computation.3 | loop fusion | flops 1310720 | bytes 5242880 | tf_op jit(solution)/shard_map/stack | solution.py:88
  20.3 1.8 %all-to-all-done = bf16[8,160,256]{2,1,0:T(8,128)(2,1)S(1)} async-done(((bf16[8,160,256]{2,1,0:T(8,128)(2,1)}), bf16[8,160,256]{2,1,0:T(8,128)(2,1)S(1)}, u32[]{:S(2)}, u32[]{:S(2)}) %all-to-all-start) | async-done | bytes 655392 | tf_op jit(solution)/shard_map/all_to_all | solution.py:79
  22.4 4.7 %all-to-all-start.1 = ((bf16[8,640,256]{2,1,0:T(8,128)(2,1)}), bf16[8,640,256]{2,1,0:T(8,128)(2,1)S(1)}, u32[]{:S(2)}, u32[]{:S(2)}) async-start(bf16[8,640,256]{2,1,0:T(8,128)(2,1)} %bitcast.11), calls=%async_computation.1 | async-start | bytes 5242880 | tf_op jit(solution)/shard_map/all_to_all | solution.py:92
  27.1 5.9 %collective-permute-start.2 = (bf16[160,256]{1,0:T(8,128)(2,1)S(1)}, bf16[160,256]{1,0:T(8,128)(2,1)S(1)}, u32[]{:S(2)}, u32[]{:S(2)}) collective-permute-start(bf16[160,256]{1,0:T(8,128)(2,1)S(1)} %get-tuple-element.83), channel_id=1, source_target_pairs={{0,14},{1,15},{2,0},{3,1},{4,2},{5,3},{6,4},{7,5},{8,6},{9,7},{10,... | collective-permute-start | bytes 245768 | tf_op jit(solution)/shard_map/ppermute | solution.py:23
  33.1 1.9 %collective-permute-start.3 = (bf16[160,256]{1,0:T(8,128)(2,1)S(1)}, bf16[160,256]{1,0:T(8,128)(2,1)S(1)}, u32[]{:S(2)}, u32[]{:S(2)}) collective-permute-start(bf16[160,256]{1,0:T(8,128)(2,1)S(1)} %get-tuple-element.82), channel_id=1, source_target_pairs={{0,10},{1,11},{2,12},{3,13},{4,14},{5,15},{6,0},{7,1},{8,2},{9,3},... | collective-permute-start | bytes 245768 | tf_op jit(solution)/shard_map/ppermute | solution.py:23
  35.0 3.4 %collective-permute-start.5 = (bf16[160,256]{1,0:T(8,128)(2,1)S(1)}, bf16[160,256]{1,0:T(8,128)(2,1)S(1)}, u32[]{:S(2)}, u32[]{:S(2)}) collective-permute-start(bf16[160,256]{1,0:T(8,128)(2,1)S(1)} %get-tuple-element.80), channel_id=1, source_target_pairs={{0,6},{1,7},{2,8},{3,9},{4,10},{5,11},{6,12},{7,13},{8,14},{9,15},... | collective-permute-start | bytes 245768 | tf_op jit(solution)/shard_map/ppermute | solution.py:23
  38.5 4.5 %collective-permute-done.3 = bf16[160,256]{1,0:T(8,128)(2,1)S(1)} collective-permute-done((bf16[160,256]{1,0:T(8,128)(2,1)S(1)}, bf16[160,256]{1,0:T(8,128)(2,1)S(1)}, u32[]{:S(2)}, u32[]{:S(2)}) %collective-permute-start.3) | collective-permute-done | bytes 81952 | tf_op jit(solution)/shard_map/ppermute | solution.py:23
  43.0 2.2 %collective-permute-done.4 = bf16[160,256]{1,0:T(8,128)(2,1)S(1)} collective-permute-done((bf16[160,256]{1,0:T(8,128)(2,1)S(1)}, bf16[160,256]{1,0:T(8,128)(2,1)S(1)}, u32[]{:S(2)}, u32[]{:S(2)}) %collective-permute-start.4) | collective-permute-done | bytes 81952 | tf_op jit(solution)/shard_map/ppermute | solution.py:23
  45.2 1.8 %collective-permute-done.5 = bf16[160,256]{1,0:T(8,128)(2,1)S(1)} collective-permute-done((bf16[160,256]{1,0:T(8,128)(2,1)S(1)}, bf16[160,256]{1,0:T(8,128)(2,1)S(1)}, u32[]{:S(2)}, u32[]{:S(2)}) %collective-permute-start.5) | collective-permute-done | bytes 81952 | tf_op jit(solution)/shard_map/ppermute | solution.py:23
  47.0 2.7 %collective-permute-start.6 = (bf16[160,256]{1,0:T(8,128)(2,1)S(1)}, bf16[160,256]{1,0:T(8,128)(2,1)S(1)}, u32[]{:S(2)}, u32[]{:S(2)}) collective-permute-start(bf16[160,256]{1,0:T(8,128)(2,1)S(1)} %get-tuple-element.79), channel_id=1, source_target_pairs={{0,12},{1,13},{2,14},{3,15},{4,0},{5,1},{6,2},{7,3},{8,4},{9,5},{1... | collective-permute-start | bytes 245768 | tf_op jit(solution)/shard_map/ppermute | solution.py:23
  50.0 1.7 %collective-permute-start.8 = (bf16[160,256]{1,0:T(8,128)(2,1)S(1)}, bf16[160,256]{1,0:T(8,128)(2,1)S(1)}, u32[]{:S(2)}, u32[]{:S(2)}) collective-permute-start(bf16[160,256]{1,0:T(8,128)(2,1)S(1)} %get-tuple-element.77), channel_id=1, source_target_pairs={{0,2},{1,3},{2,4},{3,5},{4,6},{5,7},{6,8},{7,9},{8,10},{9,11},{10,... | collective-permute-start | bytes 245768 | tf_op jit(solution)/shard_map/ppermute | solution.py:23
  52.6 4.2 %collective-permute-done.7 = bf16[160,256]{1,0:T(8,128)(2,1)S(1)} collective-permute-done((bf16[160,256]{1,0:T(8,128)(2,1)S(1)}, bf16[160,256]{1,0:T(8,128)(2,1)S(1)}, u32[]{:S(2)}, u32[]{:S(2)}) %collective-permute-start.7) | collective-permute-done | bytes 81952 | tf_op jit(solution)/shard_map/ppermute | solution.py:23
  62.0 1.2 reduce_sum.12
  63.2 1.6 %collective-permute-start.9 = (bf16[640,256]{1,0:T(8,128)(2,1)}, bf16[640,256]{1,0:T(8,128)(2,1)}, u32[]{:S(2)}, u32[]{:S(2)}) collective-permute-start(bf16[640,256]{1,0:T(8,128)(2,1)} %reduce_sum.12), channel_id=1, source_target_pairs={{0,14},{1,15},{2,0},{3,1},{4,2},{5,3},{6,4},{7,5},{8,6},{9,7},{10,... | collective-permute-start | bytes 983048 | tf_op jit(solution)/shard_map/ppermute | solution.py:23
  65.2 1.5 %collective-permute-start.13 = (bf16[160,2048]{1,0:T(8,128)(2,1)}, bf16[160,2048]{1,0:T(8,128)(2,1)S(1)}, u32[]{:S(2)}, u32[]{:S(2)}) collective-permute-start(bf16[160,2048]{1,0:T(8,128)(2,1)} %constant_dynamic-update-slice_fusion.2), channel_id=1, source_target_pairs={{0,64},{1,65},{2,66},{3,67},{4,68},{5,69},{6,70},{7,71},{8,72},{9,... | collective-permute-start | bytes 1966088 | tf_op jit(solution)/shard_map/ppermute | solution.py:23
  66.7 1.7 %collective-permute-start.14 = (bf16[160,2048]{1,0:T(8,128)(2,1)}, bf16[160,2048]{1,0:T(8,128)(2,1)}, u32[]{:S(2)}, u32[]{:S(2)}) collective-permute-start(bf16[160,2048]{1,0:T(8,128)(2,1)} %constant_dynamic-update-slice_fusion.2), channel_id=1, source_target_pairs={{0,192},{1,193},{2,194},{3,195},{4,196},{5,197},{6,198},{7,199},{8... | collective-permute-start | bytes 1966088 | tf_op jit(solution)/shard_map/ppermute | solution.py:23
  68.5 2.1 %collective-permute-done.9 = bf16[640,256]{1,0:T(8,128)(2,1)} collective-permute-done((bf16[640,256]{1,0:T(8,128)(2,1)}, bf16[640,256]{1,0:T(8,128)(2,1)}, u32[]{:S(2)}, u32[]{:S(2)}) %collective-permute-start.9) | collective-permute-done | bytes 327712 | tf_op jit(solution)/shard_map/ppermute | solution.py:23
  70.6 2.9 %collective-permute-done.10 = bf16[640,256]{1,0:T(8,128)(2,1)} collective-permute-done((bf16[640,256]{1,0:T(8,128)(2,1)}, bf16[640,256]{1,0:T(8,128)(2,1)}, u32[]{:S(2)}, u32[]{:S(2)}) %collective-permute-start.10) | collective-permute-done | bytes 327712 | tf_op jit(solution)/shard_map/ppermute | solution.py:23
  73.8 1.7 %collective-permute-start.12 = (bf16[640,256]{1,0:T(8,128)(2,1)}, bf16[640,256]{1,0:T(8,128)(2,1)S(1)}, u32[]{:S(2)}, u32[]{:S(2)}) collective-permute-start(bf16[640,256]{1,0:T(8,128)(2,1)} %collective-permute-done.10), channel_id=1, source_target_pairs={{0,2},{1,3},{2,4},{3,5},{4,6},{5,7},{6,8},{7,9},{8,10},{9,11},{10,... | collective-permute-start | bytes 983048 | tf_op jit(solution)/shard_map/ppermute | solution.py:23
  75.8 1.1 constant_dynamic-update-slice_fusion.15
  77.0 2.2 %pad_maximum_fusion.4 = bf16[640,768]{1,0:T(8,128)(2,1)} fusion(bf16[640,256]{1,0:T(8,128)(2,1)} %collective-permute-done.10, bf16[640,256]{1,0:T(8,128)(2,1)} %collective-permute-done.9, bf16[640,256]{1,0:T(8,128)(2,1)} %reduce_sum.12), kind=kLoop, calls=%fused_computation.20 | loop fusion | flops 2949120 | bytes 1966080 | tf_op jit(solution)/shard_map/concatenate | solution.py:106
  79.2 1.6 %collective-permute-done.13 = bf16[160,2048]{1,0:T(8,128)(2,1)S(1)} collective-permute-done((bf16[160,2048]{1,0:T(8,128)(2,1)}, bf16[160,2048]{1,0:T(8,128)(2,1)S(1)}, u32[]{:S(2)}, u32[]{:S(2)}) %collective-permute-start.13) | collective-permute-done | bytes 655392 | tf_op jit(solution)/shard_map/ppermute | solution.py:23
  82.2 2.4 %collective-permute-start.15 = (bf16[640,256]{1,0:T(8,128)(2,1)S(1)}, bf16[640,256]{1,0:T(8,128)(2,1)}, u32[]{:S(2)}, u32[]{:S(2)}) collective-permute-start(bf16[640,256]{1,0:T(8,128)(2,1)S(1)} %collective-permute-done.11), channel_id=1, source_target_pairs={{0,14},{1,15},{2,0},{3,1},{4,2},{5,3},{6,4},{7,5},{8,6},{9,7},{10,... | collective-permute-start | bytes 983048 | tf_op jit(solution)/shard_map/ppermute | solution.py:23
  84.7 2.9 %collective-permute-start.17 = (bf16[160,1024]{1,0:T(8,128)(2,1)S(1)}, bf16[160,1024]{1,0:T(8,128)(2,1)S(1)}, u32[]{:S(2)}, u32[]{:S(2)}) collective-permute-start(bf16[160,1024]{1,0:T(8,128)(2,1)S(1)} %slice.89), channel_id=1, source_target_pairs={{0,64},{1,65},{2,66},{3,67},{4,68},{5,69},{6,70},{7,71},{8,72},{9,... | collective-permute-start | bytes 983048 | tf_op jit(solution)/shard_map/ppermute | solution.py:23
  87.6 1.0 slice.90
  89.1 1.1 constant_dynamic-update-slice_fusion.14
  90.3 1.1 constant_dynamic-update-slice_fusion.13
  91.5 1.5 %collective-permute-done.16 = bf16[640,256]{1,0:T(8,128)(2,1)S(1)} collective-permute-done((bf16[640,256]{1,0:T(8,128)(2,1)S(1)}, bf16[640,256]{1,0:T(8,128)(2,1)S(1)}, u32[]{:S(2)}, u32[]{:S(2)}) %collective-permute-start.16) | collective-permute-done | bytes 327712 | tf_op jit(solution)/shard_map/ppermute | solution.py:23
  93.1 2.7 %collective-permute-done.18 = bf16[160,1024]{1,0:T(8,128)(2,1)S(1)} collective-permute-done((bf16[160,1024]{1,0:T(8,128)(2,1)S(1)}, bf16[160,1024]{1,0:T(8,128)(2,1)S(1)}, u32[]{:S(2)}, u32[]{:S(2)}) %collective-permute-start.18) | collective-permute-done | bytes 327712 | tf_op jit(solution)/shard_map/ppermute | solution.py:23
  96.0 1.6 %collective-permute-start.20 = (bf16[640,256]{1,0:T(8,128)(2,1)}, bf16[640,256]{1,0:T(8,128)(2,1)}, u32[]{:S(2)}, u32[]{:S(2)}) collective-permute-start(bf16[640,256]{1,0:T(8,128)(2,1)} %collective-permute-done.15), channel_id=1, source_target_pairs={{0,14},{1,15},{2,0},{3,1},{4,2},{5,3},{6,4},{7,5},{8,6},{9,7},{10,... | collective-permute-start | bytes 983048 | tf_op jit(solution)/shard_map/ppermute | solution.py:23
  97.5 1.0 constant_dynamic-update-slice_fusion.12
  98.6 1.0 constant_dynamic-update-slice_fusion.11
  99.6 6.8 %collective-permute-done.20 = bf16[640,256]{1,0:T(8,128)(2,1)} collective-permute-done((bf16[640,256]{1,0:T(8,128)(2,1)}, bf16[640,256]{1,0:T(8,128)(2,1)}, u32[]{:S(2)}, u32[]{:S(2)}) %collective-permute-start.20) | collective-permute-done | bytes 327712 | tf_op jit(solution)/shard_map/ppermute | solution.py:23
  106.4 1.0 constant_dynamic-update-slice_fusion.10
  107.4 2.2 %broadcast_select_fusion = (bf16[640,2048]{1,0:T(8,128)(2,1)S(1)}, bf16[640,2048]{1,0:T(8,128)(2,1)S(1)}) fusion(bf16[640,2048]{1,0:T(8,128)(2,1)} %collective-permute-done.19, bf16[640,2048]{1,0:T(8,128)(2,1)S(1)} %maximum_dynamic-update-slice_fusion, pred[]{:T(512)S(6)} %eq.9), kind=kLoop, calls=%fused_computation.4 | loop fusion | flops 2621440 | bytes 10485761 | tf_op jit(solution)/shard_map/jit(_where)/select_n | solution.py:119
  113.0 1.0 fusion.27
  114.2 1.3 %collective-permute-start.21 = (bf16[160,640]{1,0:T(8,128)(2,1)S(1)}, bf16[160,640]{1,0:T(8,128)(2,1)S(1)}, u32[]{:S(2)}, u32[]{:S(2)}) collective-permute-start(bf16[160,640]{1,0:T(8,128)(2,1)S(1)} %get-tuple-element.75), channel_id=1, source_target_pairs={{0,32},{1,33},{2,34},{3,35},{4,36},{5,37},{6,38},{7,39},{8,40},{9,... | collective-permute-start | bytes 614408 | tf_op jit(solution)/shard_map/ppermute | solution.py:23
  115.5 1.0 add_add_fusion.1
  116.5 5.4 %collective-permute-done.23 = bf16[160,640]{1,0:T(8,128)(2,1)S(1)} collective-permute-done((bf16[160,640]{1,0:T(8,128)(2,1)S(1)}, bf16[160,640]{1,0:T(8,128)(2,1)S(1)}, u32[]{:S(2)}, u32[]{:S(2)}) %collective-permute-start.23) | collective-permute-done | bytes 204832 | tf_op jit(solution)/shard_map/ppermute | solution.py:23
  122.2 1.6 %collective-permute-start.22 = (bf16[320,640]{1,0:T(8,128)(2,1)S(1)}, bf16[320,640]{1,0:T(8,128)(2,1)S(1)}, u32[]{:S(2)}, u32[]{:S(2)}) collective-permute-start(bf16[320,640]{1,0:T(8,128)(2,1)S(1)} %fusion.13), channel_id=1, source_target_pairs={{0,33},{1,32},{2,35},{3,34},{4,37},{5,36},{6,39},{7,38},{8,41},{9,... | collective-permute-start | bytes 1228808 | tf_op jit(solution)/shard_map/ppermute | solution.py:23
  123.9 8.4 %collective-permute-done.24 = bf16[320,640]{1,0:T(8,128)(2,1)S(1)} collective-permute-done((bf16[320,640]{1,0:T(8,128)(2,1)S(1)}, bf16[320,640]{1,0:T(8,128)(2,1)S(1)}, u32[]{:S(2)}, u32[]{:S(2)}) %collective-permute-start.24) | collective-permute-done | bytes 409632 | tf_op jit(solution)/shard_map/ppermute | solution.py:23
  132.2 1.4 %collective-permute-done.22 = bf16[320,640]{1,0:T(8,128)(2,1)S(1)} collective-permute-done((bf16[320,640]{1,0:T(8,128)(2,1)S(1)}, bf16[320,640]{1,0:T(8,128)(2,1)S(1)}, u32[]{:S(2)}, u32[]{:S(2)}) %collective-permute-start.22) | collective-permute-done | bytes 409632 | tf_op jit(solution)/shard_map/ppermute | solution.py:23
  (62 shorter events, 18.0 us)
Async XLA Ops:
  0.0 2.1 %copy-start.4 = (bf16[256,512]{1,0:T(8,128)(2,1)S(1)}, bf16[256,512]{1,0:T(8,128)(2,1)}, u32[]{:S(2)}) copy-start(bf16[256,512]{1,0:T(8,128)(2,1)} %param.3) | copy-start | bytes 786436
  0.0 2.6 %copy-start.2 = (bf16[640,512]{1,0:T(8,128)(2,1)S(1)}, bf16[640,512]{1,0:T(8,128)(2,1)}, u32[]{:S(2)}) copy-start(bf16[640,512]{1,0:T(8,128)(2,1)} %param.5) | copy-start | bytes 1966084
  2.0 3.6 %collective-permute-start = (bf16[4,2,320,256]{3,2,1,0:T(8,128)(2,1)S(1)}, bf16[4,2,320,256]{3,2,1,0:T(8,128)(2,1)}, u32[]{:S(2)}, u32[]{:S(2)}) collective-permute-start(bf16[4,2,320,256]{3,2,1,0:T(8,128)(2,1)S(1)} %get-tuple-element.74), channel_id=1, source_target_pairs={{0,16},{1,17},{2,18},{3,19},{4,20},{5,21},{6,22},{7,23},{8,24},{9,... | collective-permute-start | bytes 3932168 | tf_op jit(solution)/shard_map/ppermute | solution.py:23
  2.1 3.5 %collective-permute-start.1 = (bf16[256,512]{1,0:T(8,128)(2,1)S(1)}, bf16[256,512]{1,0:T(8,128)(2,1)}, u32[]{:S(2)}, u32[]{:S(2)}) collective-permute-start(bf16[256,512]{1,0:T(8,128)(2,1)S(1)} %copy-done.4), channel_id=1, source_target_pairs={{0,16},{1,17},{2,18},{3,19},{4,20},{5,21},{6,22},{7,23},{8,24},{9,... | collective-permute-start | bytes 786440 | tf_op jit(solution)/shard_map/ppermute | solution.py:23
  5.6 16.6 %all-to-all-start = ((bf16[8,160,256]{2,1,0:T(8,128)(2,1)}), bf16[8,160,256]{2,1,0:T(8,128)(2,1)S(1)}, u32[]{:S(2)}, u32[]{:S(2)}) async-start(bf16[8,160,256]{2,1,0:T(8,128)(2,1)} %bitcast.5), calls=%async_computation | async-start | bytes 1310720 | tf_op jit(solution)/shard_map/all_to_all | solution.py:79
  15.4 1.0 copy-start.5
  22.4 39.6 %all-to-all-start.1 = ((bf16[8,640,256]{2,1,0:T(8,128)(2,1)}), bf16[8,640,256]{2,1,0:T(8,128)(2,1)S(1)}, u32[]{:S(2)}, u32[]{:S(2)}) async-start(bf16[8,640,256]{2,1,0:T(8,128)(2,1)} %bitcast.11), calls=%async_computation.1 | async-start | bytes 5242880 | tf_op jit(solution)/shard_map/all_to_all | solution.py:92
  27.1 11.3 %collective-permute-start.2 = (bf16[160,256]{1,0:T(8,128)(2,1)S(1)}, bf16[160,256]{1,0:T(8,128)(2,1)S(1)}, u32[]{:S(2)}, u32[]{:S(2)}) collective-permute-start(bf16[160,256]{1,0:T(8,128)(2,1)S(1)} %get-tuple-element.83), channel_id=1, source_target_pairs={{0,14},{1,15},{2,0},{3,1},{4,2},{5,3},{6,4},{7,5},{8,6},{9,7},{10,... | collective-permute-start | bytes 245768 | tf_op jit(solution)/shard_map/ppermute | solution.py:23
  33.1 9.9 %collective-permute-start.3 = (bf16[160,256]{1,0:T(8,128)(2,1)S(1)}, bf16[160,256]{1,0:T(8,128)(2,1)S(1)}, u32[]{:S(2)}, u32[]{:S(2)}) collective-permute-start(bf16[160,256]{1,0:T(8,128)(2,1)S(1)} %get-tuple-element.82), channel_id=1, source_target_pairs={{0,10},{1,11},{2,12},{3,13},{4,14},{5,15},{6,0},{7,1},{8,2},{9,3},... | collective-permute-start | bytes 245768 | tf_op jit(solution)/shard_map/ppermute | solution.py:23
  35.0 10.3 %collective-permute-start.4 = (bf16[160,256]{1,0:T(8,128)(2,1)S(1)}, bf16[160,256]{1,0:T(8,128)(2,1)S(1)}, u32[]{:S(2)}, u32[]{:S(2)}) collective-permute-start(bf16[160,256]{1,0:T(8,128)(2,1)S(1)} %get-tuple-element.81), channel_id=1, source_target_pairs={{0,8},{1,9},{2,10},{3,11},{4,12},{5,13},{6,14},{7,15},{8,0},{9,1},... | collective-permute-start | bytes 245768 | tf_op jit(solution)/shard_map/ppermute | solution.py:23
  35.0 12.0 %collective-permute-start.5 = (bf16[160,256]{1,0:T(8,128)(2,1)S(1)}, bf16[160,256]{1,0:T(8,128)(2,1)S(1)}, u32[]{:S(2)}, u32[]{:S(2)}) collective-permute-start(bf16[160,256]{1,0:T(8,128)(2,1)S(1)} %get-tuple-element.80), channel_id=1, source_target_pairs={{0,6},{1,7},{2,8},{3,9},{4,10},{5,11},{6,12},{7,13},{8,14},{9,15},... | collective-permute-start | bytes 245768 | tf_op jit(solution)/shard_map/ppermute | solution.py:23
  47.0 5.5 %collective-permute-start.6 = (bf16[160,256]{1,0:T(8,128)(2,1)S(1)}, bf16[160,256]{1,0:T(8,128)(2,1)S(1)}, u32[]{:S(2)}, u32[]{:S(2)}) collective-permute-start(bf16[160,256]{1,0:T(8,128)(2,1)S(1)} %get-tuple-element.79), channel_id=1, source_target_pairs={{0,12},{1,13},{2,14},{3,15},{4,0},{5,1},{6,2},{7,3},{8,4},{9,5},{1... | collective-permute-start | bytes 245768 | tf_op jit(solution)/shard_map/ppermute | solution.py:23
  49.7 7.1 %collective-permute-start.7 = (bf16[160,256]{1,0:T(8,128)(2,1)S(1)}, bf16[160,256]{1,0:T(8,128)(2,1)S(1)}, u32[]{:S(2)}, u32[]{:S(2)}) collective-permute-start(bf16[160,256]{1,0:T(8,128)(2,1)S(1)} %get-tuple-element.78), channel_id=1, source_target_pairs={{0,4},{1,5},{2,6},{3,7},{4,8},{5,9},{6,10},{7,11},{8,12},{9,13},{1... | collective-permute-start | bytes 245768 | tf_op jit(solution)/shard_map/ppermute | solution.py:23
  50.0 6.8 %collective-permute-start.8 = (bf16[160,256]{1,0:T(8,128)(2,1)S(1)}, bf16[160,256]{1,0:T(8,128)(2,1)S(1)}, u32[]{:S(2)}, u32[]{:S(2)}) collective-permute-start(bf16[160,256]{1,0:T(8,128)(2,1)S(1)} %get-tuple-element.77), channel_id=1, source_target_pairs={{0,2},{1,3},{2,4},{3,5},{4,6},{5,7},{6,8},{7,9},{8,10},{9,11},{10,... | collective-permute-start | bytes 245768 | tf_op jit(solution)/shard_map/ppermute | solution.py:23
  63.2 7.4 %collective-permute-start.9 = (bf16[640,256]{1,0:T(8,128)(2,1)}, bf16[640,256]{1,0:T(8,128)(2,1)}, u32[]{:S(2)}, u32[]{:S(2)}) collective-permute-start(bf16[640,256]{1,0:T(8,128)(2,1)} %reduce_sum.12), channel_id=1, source_target_pairs={{0,14},{1,15},{2,0},{3,1},{4,2},{5,3},{6,4},{7,5},{8,6},{9,7},{10,... | collective-permute-start | bytes 983048 | tf_op jit(solution)/shard_map/ppermute | solution.py:23
  64.8 8.7 %collective-permute-start.10 = (bf16[640,256]{1,0:T(8,128)(2,1)}, bf16[640,256]{1,0:T(8,128)(2,1)}, u32[]{:S(2)}, u32[]{:S(2)}) collective-permute-start(bf16[640,256]{1,0:T(8,128)(2,1)} %reduce_sum.12), channel_id=1, source_target_pairs={{0,2},{1,3},{2,4},{3,5},{4,6},{5,7},{6,8},{7,9},{8,10},{9,11},{10,... | collective-permute-start | bytes 983048 | tf_op jit(solution)/shard_map/ppermute | solution.py:23
  65.2 15.5 %collective-permute-start.13 = (bf16[160,2048]{1,0:T(8,128)(2,1)}, bf16[160,2048]{1,0:T(8,128)(2,1)S(1)}, u32[]{:S(2)}, u32[]{:S(2)}) collective-permute-start(bf16[160,2048]{1,0:T(8,128)(2,1)} %constant_dynamic-update-slice_fusion.2), channel_id=1, source_target_pairs={{0,64},{1,65},{2,66},{3,67},{4,68},{5,69},{6,70},{7,71},{8,72},{9,... | collective-permute-start | bytes 1966088 | tf_op jit(solution)/shard_map/ppermute | solution.py:23
  66.7 15.0 %collective-permute-start.14 = (bf16[160,2048]{1,0:T(8,128)(2,1)}, bf16[160,2048]{1,0:T(8,128)(2,1)}, u32[]{:S(2)}, u32[]{:S(2)}) collective-permute-start(bf16[160,2048]{1,0:T(8,128)(2,1)} %constant_dynamic-update-slice_fusion.2), channel_id=1, source_target_pairs={{0,192},{1,193},{2,194},{3,195},{4,196},{5,197},{6,198},{7,199},{8... | collective-permute-start | bytes 1966088 | tf_op jit(solution)/shard_map/ppermute | solution.py:23
  73.5 8.3 %collective-permute-start.11 = (bf16[640,256]{1,0:T(8,128)(2,1)}, bf16[640,256]{1,0:T(8,128)(2,1)S(1)}, u32[]{:S(2)}, u32[]{:S(2)}) collective-permute-start(bf16[640,256]{1,0:T(8,128)(2,1)} %collective-permute-done.9), channel_id=1, source_target_pairs={{0,14},{1,15},{2,0},{3,1},{4,2},{5,3},{6,4},{7,5},{8,6},{9,7},{10,... | collective-permute-start | bytes 983048 | tf_op jit(solution)/shard_map/ppermute | solution.py:23
  73.8 8.5 %collective-permute-start.12 = (bf16[640,256]{1,0:T(8,128)(2,1)}, bf16[640,256]{1,0:T(8,128)(2,1)S(1)}, u32[]{:S(2)}, u32[]{:S(2)}) collective-permute-start(bf16[640,256]{1,0:T(8,128)(2,1)} %collective-permute-done.10), channel_id=1, source_target_pairs={{0,2},{1,3},{2,4},{3,5},{4,6},{5,7},{6,8},{7,9},{8,10},{9,11},{10,... | collective-permute-start | bytes 983048 | tf_op jit(solution)/shard_map/ppermute | solution.py:23
  80.8 8.4 %copy-start = (bf16[160,2048]{1,0:T(8,128)(2,1)}, bf16[160,2048]{1,0:T(8,128)(2,1)S(1)}, u32[]{:S(2)}) copy-start(bf16[160,2048]{1,0:T(8,128)(2,1)S(1)} %collective-permute-done.13) | copy-start | bytes 1966084
  82.2 9.2 %collective-permute-start.15 = (bf16[640,256]{1,0:T(8,128)(2,1)S(1)}, bf16[640,256]{1,0:T(8,128)(2,1)}, u32[]{:S(2)}, u32[]{:S(2)}) collective-permute-start(bf16[640,256]{1,0:T(8,128)(2,1)S(1)} %collective-permute-done.11), channel_id=1, source_target_pairs={{0,14},{1,15},{2,0},{3,1},{4,2},{5,3},{6,4},{7,5},{8,6},{9,7},{10,... | collective-permute-start | bytes 983048 | tf_op jit(solution)/shard_map/ppermute | solution.py:23
  84.7 8.3 %collective-permute-start.16 = (bf16[640,256]{1,0:T(8,128)(2,1)S(1)}, bf16[640,256]{1,0:T(8,128)(2,1)S(1)}, u32[]{:S(2)}, u32[]{:S(2)}) collective-permute-start(bf16[640,256]{1,0:T(8,128)(2,1)S(1)} %collective-permute-done.12), channel_id=1, source_target_pairs={{0,2},{1,3},{2,4},{3,5},{4,6},{5,7},{6,8},{7,9},{8,10},{9,11},{10,... | collective-permute-start | bytes 983048 | tf_op jit(solution)/shard_map/ppermute | solution.py:23
  84.7 8.4 %collective-permute-start.17 = (bf16[160,1024]{1,0:T(8,128)(2,1)S(1)}, bf16[160,1024]{1,0:T(8,128)(2,1)S(1)}, u32[]{:S(2)}, u32[]{:S(2)}) collective-permute-start(bf16[160,1024]{1,0:T(8,128)(2,1)S(1)} %slice.89), channel_id=1, source_target_pairs={{0,64},{1,65},{2,66},{3,67},{4,68},{5,69},{6,70},{7,71},{8,72},{9,... | collective-permute-start | bytes 983048 | tf_op jit(solution)/shard_map/ppermute | solution.py:23
  88.6 7.2 %collective-permute-start.18 = (bf16[160,1024]{1,0:T(8,128)(2,1)S(1)}, bf16[160,1024]{1,0:T(8,128)(2,1)S(1)}, u32[]{:S(2)}, u32[]{:S(2)}) collective-permute-start(bf16[160,1024]{1,0:T(8,128)(2,1)S(1)} %slice.90), channel_id=1, source_target_pairs={{0,192},{1,193},{2,194},{3,195},{4,196},{5,197},{6,198},{7,199},{8... | collective-permute-start | bytes 983048 | tf_op jit(solution)/shard_map/ppermute | solution.py:23
  93.0 2.9 %copy-start.3 = (bf16[640,256]{1,0:T(8,128)(2,1)}, bf16[640,256]{1,0:T(8,128)(2,1)S(1)}, u32[]{:S(2)}) copy-start(bf16[640,256]{1,0:T(8,128)(2,1)S(1)} %collective-permute-done.16) | copy-start | bytes 983044
  95.9 11.6 %collective-permute-start.19 = (bf16[640,2048]{1,0:T(8,128)(2,1)S(1)}, bf16[640,2048]{1,0:T(8,128)(2,1)}, u32[]{:S(2)}, u32[]{:S(2)}) collective-permute-start(bf16[640,2048]{1,0:T(8,128)(2,1)S(1)} %maximum_dynamic-update-slice_fusion), channel_id=1, source_target_pairs={{0,16},{1,17},{2,18},{3,19},{4,20},{5,21},{6,22},{7,23},{8,24},{9,... | collective-permute-start | bytes 7864328 | tf_op jit(solution)/shard_map/ppermute | solution.py:23
  96.0 10.4 %collective-permute-start.20 = (bf16[640,256]{1,0:T(8,128)(2,1)}, bf16[640,256]{1,0:T(8,128)(2,1)}, u32[]{:S(2)}, u32[]{:S(2)}) collective-permute-start(bf16[640,256]{1,0:T(8,128)(2,1)} %collective-permute-done.15), channel_id=1, source_target_pairs={{0,14},{1,15},{2,0},{3,1},{4,2},{5,3},{6,4},{7,5},{8,6},{9,7},{10,... | collective-permute-start | bytes 983048 | tf_op jit(solution)/shard_map/ppermute | solution.py:23
  107.4 2.2 %copy-start.1 = (bf16[640,768]{1,0:T(8,128)(2,1)S(1)}, bf16[640,768]{1,0:T(8,128)(2,1)}, u32[]{:S(2)}) copy-start(bf16[640,768]{1,0:T(8,128)(2,1)} %pad_maximum_fusion.4) | copy-start | bytes 2949124
  114.1 7.9 %collective-permute-start.23 = (bf16[160,640]{1,0:T(8,128)(2,1)S(1)}, bf16[160,640]{1,0:T(8,128)(2,1)S(1)}, u32[]{:S(2)}, u32[]{:S(2)}) collective-permute-start(bf16[160,640]{1,0:T(8,128)(2,1)S(1)} %get-tuple-element.76), channel_id=1, source_target_pairs={{0,33},{1,32},{2,35},{3,34},{4,37},{5,36},{6,39},{7,38},{8,41},{9,... | collective-permute-start | bytes 614408 | tf_op jit(solution)/shard_map/ppermute | solution.py:23
  114.2 8.0 %collective-permute-start.21 = (bf16[160,640]{1,0:T(8,128)(2,1)S(1)}, bf16[160,640]{1,0:T(8,128)(2,1)S(1)}, u32[]{:S(2)}, u32[]{:S(2)}) collective-permute-start(bf16[160,640]{1,0:T(8,128)(2,1)S(1)} %get-tuple-element.75), channel_id=1, source_target_pairs={{0,32},{1,33},{2,34},{3,35},{4,36},{5,37},{6,38},{7,39},{8,40},{9,... | collective-permute-start | bytes 614408 | tf_op jit(solution)/shard_map/ppermute | solution.py:23
  122.0 10.2 %collective-permute-start.24 = (bf16[320,640]{1,0:T(8,128)(2,1)S(1)}, bf16[320,640]{1,0:T(8,128)(2,1)S(1)}, u32[]{:S(2)}, u32[]{:S(2)}) collective-permute-start(bf16[320,640]{1,0:T(8,128)(2,1)S(1)} %fusion.12), channel_id=1, source_target_pairs={{0,32},{1,33},{2,34},{3,35},{4,36},{5,37},{6,38},{7,39},{8,40},{9,... | collective-permute-start | bytes 1228808 | tf_op jit(solution)/shard_map/ppermute | solution.py:23
  122.2 11.4 %collective-permute-start.22 = (bf16[320,640]{1,0:T(8,128)(2,1)S(1)}, bf16[320,640]{1,0:T(8,128)(2,1)S(1)}, u32[]{:S(2)}, u32[]{:S(2)}) collective-permute-start(bf16[320,640]{1,0:T(8,128)(2,1)S(1)} %fusion.13), channel_id=1, source_target_pairs={{0,33},{1,32},{2,35},{3,34},{4,37},{5,36},{6,39},{7,38},{8,41},{9,... | collective-permute-start | bytes 1228808 | tf_op jit(solution)/shard_map/ppermute | solution.py:23

commit v6 on v4

--- a/solution.py
+++ b/solution.py
@@ -101,7 +101,6 @@
 
     up1, down1 = send(inner, z_by(-1)), send(inner, z_by(1))
     below, above = send(cols, y_by(1)), send(cols, y_by(-1))
-    up1, down1 = barrier((up1, down1))
     up2, down2 = send(up1, z_by(-1)), send(down1, z_by(1))
     first = jnp.concatenate((inner, up1, down1), 1)
     up2, down2, below, above, first = barrier((up2, down2, below, above, first))

time: 130 us -> 130 us (level)
  transfers between devices with their start and end apart: 28 -> 28, of which waited for: 19 -> 18; matrix products, arithmetic and copies ran while one was open for 23% -> 23% of each run, Pallas kernels for 0% -> 0%
where the time goes in v6:
time: 130 us; the launch traced here: 129 us
  starting transfers between devices  47.5 us (37%)
  waiting for transfers between devices  44.7 us (34%)
  local copies, waits for them, and re-layouts  17.7 us (14%)
  matrix products  9.72 us (7%)
  other arithmetic  9.39 us (7%)
    ppermute x26, waiting for transfers between devices, send(): return lax.ppermute(value, AXES, pairs(move))  42.8 us
    ppermute x26, starting transfers between devices, send(): return lax.ppermute(value, AXES, pairs(move))  36.8 us
    unnamed x26, local copies, waits for them, and re-layouts  6.56 us
    all_to_all x1, starting transfers between devices, on_device(): pieces = lax.all_to_all(pieces, ('y', 'xl'), 0, 0, tiled=True)  5.93 us
    dot_general x6, matrix products, dot_f32(): lax.dot_general(left, right, (((1,), (1,)), ((), ())), preferred_element_...  5.37 us
    all_to_all x1, starting transfers between devices, on_device(): part = lax.all_to_all(part, ('y', 'xl'), 0, 0, tiled=True)  4.71 us
    dot_general x2, matrix products, on_device(): jnp.dot(left, right[:, i * half:(i + 1) * half], preferred_element_type=j...  4.35 us
    dynamic_update_slice x3, local copies, waits for them, and re-layouts, on_device(): lax.dynamic_update_slice_in_dim(full, block, (y + shift) % 4 * quarter, 0)  3.41 us
  transfers between devices with their start and end apart: 28, of which 18 were waited for; matrix products, arithmetic and copies ran while one was open for 23% of the time, Pallas kernels for 0%

profile of v6, /device:TPU:6, one launch (start us, length us, event | category | flops | bytes accessed | tf_op | source)
XLA Modules:
  0.0 129.2 jit_solution(16269899622075097006)
XLA Ops:
  0.0 2.0 %constant_dynamic-slice_fusion = (bf16[4,2,1,320,256]{4,3,2,1,0:T(8,128)(2,1)S(1)}, bf16[4,2,320,256]{3,2,1,0:T(8,128)(2,1)S(1)}) fusion(bf16[4,2,2,320,256]{4,3,2,1,0:T(8,128)(2,1)} %bitcast.35, s32[]{:T(128)S(6)} %select_n.53, s32[]{:T(128)S(6)} %select_n.54), kind=kLoop, calls=%fused_computation.60 | loop fusion | bytes 5242888 | tf_op jit(solution)/shard_map/jit(dynamic_index_in_dim)/dynamic_slice | solution.py:71
  4.3 1.3 %collective-permute-done.1 = bf16[256,512]{1,0:T(8,128)(2,1)} collective-permute-done((bf16[256,512]{1,0:T(8,128)(2,1)S(1)}, bf16[256,512]{1,0:T(8,128)(2,1)}, u32[]{:S(2)}, u32[]{:S(2)}) %collective-permute-start.1) | collective-permute-done | bytes 262176 | tf_op jit(solution)/shard_map/ppermute | solution.py:23
  5.6 5.9 %all-to-all-start = ((bf16[8,160,256]{2,1,0:T(8,128)(2,1)}), bf16[8,160,256]{2,1,0:T(8,128)(2,1)S(1)}, u32[]{:S(2)}, u32[]{:S(2)}) async-start(bf16[8,160,256]{2,1,0:T(8,128)(2,1)} %bitcast.5), calls=%async_computation | async-start | bytes 1310720 | tf_op jit(solution)/shard_map/all_to_all | solution.py:79
  11.5 1.7 %constant_dynamic-update-slice_fusion = bf16[512,512]{1,0:T(8,128)(2,1)} fusion(bf16[512,512]{1,0:T(8,128)(2,1)} %constant_dynamic-update-slice_fusion.1, bf16[256,512]{1,0:T(8,128)(2,1)} %collective-permute-done.1), kind=kLoop, calls=%fused_computation.47 | loop fusion | bytes 524288 | tf_op jit(solution)/shard_map/concatenate | solution.py:82
  13.2 2.2 %convolution_convert_fusion = bf16[2560,256]{1,0:T(8,128)(2,1)S(1)} fusion(bf16[2560,256]{1,0:T(8,128)(2,1)} %bitcast.6, bf16[2560,256]{1,0:T(8,128)(2,1)S(1)} %bitcast.40, bf16[512,512]{1,0:T(8,128)(2,1)} %constant_dynamic-update-slice_fusion), kind=kOutput, calls=%fused_computation | convolution fusion | flops 676986880 | bytes 4194304 | tf_op jit(solution)/shard_map/dot_general | solution.py:84
  15.5 0.9 copy-done.8
  16.4 2.2 %convolution_convert_fusion.1 = bf16[2560,256]{1,0:T(8,128)(2,1)S(1)} fusion(bf16[2560,256]{1,0:T(8,128)(2,1)} %bitcast.6, bf16[2560,256]{1,0:T(8,128)(2,1)S(1)} %bitcast.41, bf16[512,512]{1,0:T(8,128)(2,1)S(1)} %copy-done.8), kind=kOutput, calls=%fused_computation.1 | convolution fusion | flops 676986880 | bytes 4194304 | tf_op jit(solution)/shard_map/dot_general | solution.py:84
  18.6 1.7 %pad_maximum_fusion.1 = bf16[4,2,2,320,256]{4,3,2,1,0:T(8,128)(2,1)} fusion(bf16[4,1,2,320,256]{4,3,2,1,0:T(8,128)(2,1)S(1)} %reverse_bitcast_fusion, bf16[4,1,2,320,256]{4,3,2,1,0:T(8,128)(2,1)S(1)} %bitcast.36), kind=kLoop, calls=%fused_computation.3 | loop fusion | flops 1310720 | bytes 5242880 | tf_op jit(solution)/shard_map/stack | solution.py:88
  20.3 1.9 %all-to-all-done = bf16[8,160,256]{2,1,0:T(8,128)(2,1)S(1)} async-done(((bf16[8,160,256]{2,1,0:T(8,128)(2,1)}), bf16[8,160,256]{2,1,0:T(8,128)(2,1)S(1)}, u32[]{:S(2)}, u32[]{:S(2)}) %all-to-all-start) | async-done | bytes 655392 | tf_op jit(solution)/shard_map/all_to_all | solution.py:79
  22.4 4.7 %all-to-all-start.1 = ((bf16[8,640,256]{2,1,0:T(8,128)(2,1)}), bf16[8,640,256]{2,1,0:T(8,128)(2,1)S(1)}, u32[]{:S(2)}, u32[]{:S(2)}) async-start(bf16[8,640,256]{2,1,0:T(8,128)(2,1)} %bitcast.11), calls=%async_computation.1 | async-start | bytes 5242880 | tf_op jit(solution)/shard_map/all_to_all | solution.py:92
  27.1 5.9 %collective-permute-start.2 = (bf16[160,256]{1,0:T(8,128)(2,1)S(1)}, bf16[160,256]{1,0:T(8,128)(2,1)S(1)}, u32[]{:S(2)}, u32[]{:S(2)}) collective-permute-start(bf16[160,256]{1,0:T(8,128)(2,1)S(1)} %get-tuple-element.79), channel_id=1, source_target_pairs={{0,14},{1,15},{2,0},{3,1},{4,2},{5,3},{6,4},{7,5},{8,6},{9,7},{10,... | collective-permute-start | bytes 245768 | tf_op jit(solution)/shard_map/ppermute | solution.py:23
  33.1 1.9 %collective-permute-start.3 = (bf16[160,256]{1,0:T(8,128)(2,1)S(1)}, bf16[160,256]{1,0:T(8,128)(2,1)S(1)}, u32[]{:S(2)}, u32[]{:S(2)}) collective-permute-start(bf16[160,256]{1,0:T(8,128)(2,1)S(1)} %get-tuple-element.78), channel_id=1, source_target_pairs={{0,10},{1,11},{2,12},{3,13},{4,14},{5,15},{6,0},{7,1},{8,2},{9,3},... | collective-permute-start | bytes 245768 | tf_op jit(solution)/shard_map/ppermute | solution.py:23
  35.0 3.4 %collective-permute-start.5 = (bf16[160,256]{1,0:T(8,128)(2,1)S(1)}, bf16[160,256]{1,0:T(8,128)(2,1)S(1)}, u32[]{:S(2)}, u32[]{:S(2)}) collective-permute-start(bf16[160,256]{1,0:T(8,128)(2,1)S(1)} %get-tuple-element.76), channel_id=1, source_target_pairs={{0,6},{1,7},{2,8},{3,9},{4,10},{5,11},{6,12},{7,13},{8,14},{9,15},... | collective-permute-start | bytes 245768 | tf_op jit(solution)/shard_map/ppermute | solution.py:23
  38.5 4.5 %collective-permute-done.3 = bf16[160,256]{1,0:T(8,128)(2,1)S(1)} collective-permute-done((bf16[160,256]{1,0:T(8,128)(2,1)S(1)}, bf16[160,256]{1,0:T(8,128)(2,1)S(1)}, u32[]{:S(2)}, u32[]{:S(2)}) %collective-permute-start.3) | collective-permute-done | bytes 81952 | tf_op jit(solution)/shard_map/ppermute | solution.py:23
  43.0 2.2 %collective-permute-done.4 = bf16[160,256]{1,0:T(8,128)(2,1)S(1)} collective-permute-done((bf16[160,256]{1,0:T(8,128)(2,1)S(1)}, bf16[160,256]{1,0:T(8,128)(2,1)S(1)}, u32[]{:S(2)}, u32[]{:S(2)}) %collective-permute-start.4) | collective-permute-done | bytes 81952 | tf_op jit(solution)/shard_map/ppermute | solution.py:23
  45.2 1.8 %collective-permute-done.5 = bf16[160,256]{1,0:T(8,128)(2,1)S(1)} collective-permute-done((bf16[160,256]{1,0:T(8,128)(2,1)S(1)}, bf16[160,256]{1,0:T(8,128)(2,1)S(1)}, u32[]{:S(2)}, u32[]{:S(2)}) %collective-permute-start.5) | collective-permute-done | bytes 81952 | tf_op jit(solution)/shard_map/ppermute | solution.py:23
  47.0 2.7 %collective-permute-start.6 = (bf16[160,256]{1,0:T(8,128)(2,1)S(1)}, bf16[160,256]{1,0:T(8,128)(2,1)S(1)}, u32[]{:S(2)}, u32[]{:S(2)}) collective-permute-start(bf16[160,256]{1,0:T(8,128)(2,1)S(1)} %get-tuple-element.75), channel_id=1, source_target_pairs={{0,12},{1,13},{2,14},{3,15},{4,0},{5,1},{6,2},{7,3},{8,4},{9,5},{1... | collective-permute-start | bytes 245768 | tf_op jit(solution)/shard_map/ppermute | solution.py:23
  50.0 1.7 %collective-permute-start.8 = (bf16[160,256]{1,0:T(8,128)(2,1)S(1)}, bf16[160,256]{1,0:T(8,128)(2,1)S(1)}, u32[]{:S(2)}, u32[]{:S(2)}) collective-permute-start(bf16[160,256]{1,0:T(8,128)(2,1)S(1)} %get-tuple-element.73), channel_id=1, source_target_pairs={{0,2},{1,3},{2,4},{3,5},{4,6},{5,7},{6,8},{7,9},{8,10},{9,11},{10,... | collective-permute-start | bytes 245768 | tf_op jit(solution)/shard_map/ppermute | solution.py:23
  52.6 4.2 %collective-permute-done.7 = bf16[160,256]{1,0:T(8,128)(2,1)S(1)} collective-permute-done((bf16[160,256]{1,0:T(8,128)(2,1)S(1)}, bf16[160,256]{1,0:T(8,128)(2,1)S(1)}, u32[]{:S(2)}, u32[]{:S(2)}) %collective-permute-start.7) | collective-permute-done | bytes 81952 | tf_op jit(solution)/shard_map/ppermute | solution.py:23
  62.0 1.2 reduce_sum.12
  63.2 1.6 %collective-permute-start.9 = (bf16[640,256]{1,0:T(8,128)(2,1)}, bf16[640,256]{1,0:T(8,128)(2,1)}, u32[]{:S(2)}, u32[]{:S(2)}) collective-permute-start(bf16[640,256]{1,0:T(8,128)(2,1)} %reduce_sum.12), channel_id=1, source_target_pairs={{0,14},{1,15},{2,0},{3,1},{4,2},{5,3},{6,4},{7,5},{8,6},{9,7},{10,... | collective-permute-start | bytes 983048 | tf_op jit(solution)/shard_map/ppermute | solution.py:23
  65.2 1.5 %collective-permute-start.13 = (bf16[160,2048]{1,0:T(8,128)(2,1)}, bf16[160,2048]{1,0:T(8,128)(2,1)S(1)}, u32[]{:S(2)}, u32[]{:S(2)}) collective-permute-start(bf16[160,2048]{1,0:T(8,128)(2,1)} %constant_dynamic-update-slice_fusion.2), channel_id=1, source_target_pairs={{0,64},{1,65},{2,66},{3,67},{4,68},{5,69},{6,70},{7,71},{8,72},{9,... | collective-permute-start | bytes 1966088 | tf_op jit(solution)/shard_map/ppermute | solution.py:23
  66.7 1.7 %collective-permute-start.14 = (bf16[160,2048]{1,0:T(8,128)(2,1)}, bf16[160,2048]{1,0:T(8,128)(2,1)}, u32[]{:S(2)}, u32[]{:S(2)}) collective-permute-start(bf16[160,2048]{1,0:T(8,128)(2,1)} %constant_dynamic-update-slice_fusion.2), channel_id=1, source_target_pairs={{0,192},{1,193},{2,194},{3,195},{4,196},{5,197},{6,198},{7,199},{8... | collective-permute-start | bytes 1966088 | tf_op jit(solution)/shard_map/ppermute | solution.py:23
  68.4 2.7 %collective-permute-done.9 = bf16[640,256]{1,0:T(8,128)(2,1)} collective-permute-done((bf16[640,256]{1,0:T(8,128)(2,1)}, bf16[640,256]{1,0:T(8,128)(2,1)}, u32[]{:S(2)}, u32[]{:S(2)}) %collective-permute-start.9) | collective-permute-done | bytes 327712 | tf_op jit(solution)/shard_map/ppermute | solution.py:23
  71.2 2.6 %collective-permute-start.10 = (bf16[640,256]{1,0:T(8,128)(2,1)}, bf16[640,256]{1,0:T(8,128)(2,1)S(1)}, u32[]{:S(2)}, u32[]{:S(2)}) collective-permute-start(bf16[640,256]{1,0:T(8,128)(2,1)} %collective-permute-done.9), channel_id=1, source_target_pairs={{0,14},{1,15},{2,0},{3,1},{4,2},{5,3},{6,4},{7,5},{8,6},{9,7},{10,... | collective-permute-start | bytes 983048 | tf_op jit(solution)/shard_map/ppermute | solution.py:23
  74.1 1.1 constant_dynamic-update-slice_fusion.12
  75.2 2.2 %pad_maximum_fusion.4 = bf16[640,768]{1,0:T(8,128)(2,1)} fusion(bf16[640,256]{1,0:T(8,128)(2,1)} %collective-permute-done.11, bf16[640,256]{1,0:T(8,128)(2,1)} %collective-permute-done.9, bf16[640,256]{1,0:T(8,128)(2,1)} %reduce_sum.12), kind=kLoop, calls=%fused_computation.20 | loop fusion | flops 2949120 | bytes 1966080 | tf_op jit(solution)/shard_map/concatenate | solution.py:105
  77.4 3.3 %collective-permute-done.13 = bf16[160,2048]{1,0:T(8,128)(2,1)S(1)} collective-permute-done((bf16[160,2048]{1,0:T(8,128)(2,1)}, bf16[160,2048]{1,0:T(8,128)(2,1)S(1)}, u32[]{:S(2)}, u32[]{:S(2)}) %collective-permute-start.13) | collective-permute-done | bytes 655392 | tf_op jit(solution)/shard_map/ppermute | solution.py:23
  80.8 1.0 collective-permute-done.14
  82.2 2.4 %collective-permute-start.15 = (bf16[640,256]{1,0:T(8,128)(2,1)S(1)}, bf16[640,256]{1,0:T(8,128)(2,1)S(1)}, u32[]{:S(2)}, u32[]{:S(2)}) collective-permute-start(bf16[640,256]{1,0:T(8,128)(2,1)S(1)} %collective-permute-done.10), channel_id=1, source_target_pairs={{0,14},{1,15},{2,0},{3,1},{4,2},{5,3},{6,4},{7,5},{8,6},{9,7},{10,... | collective-permute-start | bytes 983048 | tf_op jit(solution)/shard_map/ppermute | solution.py:23
  84.7 2.9 %collective-permute-start.17 = (bf16[160,1024]{1,0:T(8,128)(2,1)S(1)}, bf16[160,1024]{1,0:T(8,128)(2,1)S(1)}, u32[]{:S(2)}, u32[]{:S(2)}) collective-permute-start(bf16[160,1024]{1,0:T(8,128)(2,1)S(1)} %slice.95), channel_id=1, source_target_pairs={{0,64},{1,65},{2,66},{3,67},{4,68},{5,69},{6,70},{7,71},{8,72},{9,... | collective-permute-start | bytes 983048 | tf_op jit(solution)/shard_map/ppermute | solution.py:23
  87.7 1.0 slice.96
  89.1 1.1 constant_dynamic-update-slice_fusion.11
  90.3 1.1 constant_dynamic-update-slice_fusion.10
  91.5 1.5 %collective-permute-done.16 = bf16[640,256]{1,0:T(8,128)(2,1)S(1)} collective-permute-done((bf16[640,256]{1,0:T(8,128)(2,1)S(1)}, bf16[640,256]{1,0:T(8,128)(2,1)S(1)}, u32[]{:S(2)}, u32[]{:S(2)}) %collective-permute-start.16) | collective-permute-done | bytes 327712 | tf_op jit(solution)/shard_map/ppermute | solution.py:23
  93.1 2.7 %collective-permute-done.18 = bf16[160,1024]{1,0:T(8,128)(2,1)S(1)} collective-permute-done((bf16[160,1024]{1,0:T(8,128)(2,1)S(1)}, bf16[160,1024]{1,0:T(8,128)(2,1)S(1)}, u32[]{:S(2)}, u32[]{:S(2)}) %collective-permute-start.18) | collective-permute-done | bytes 327712 | tf_op jit(solution)/shard_map/ppermute | solution.py:23
  96.0 0.9 slice.100
  98.0 3.3 %collective-permute-start.20 = (bf16[320,256]{1,0:T(8,128)(2,1)S(1)}, bf16[320,256]{1,0:T(8,128)(2,1)S(1)}, u32[]{:S(2)}, u32[]{:S(2)}) collective-permute-start(bf16[320,256]{1,0:T(8,128)(2,1)S(1)} %slice.99), channel_id=1, source_target_pairs={{0,14},{1,15},{2,0},{3,1},{4,2},{5,3},{6,4},{7,5},{8,6},{9,7},{10,... | collective-permute-start | bytes 491528 | tf_op jit(solution)/shard_map/ppermute | solution.py:23
  101.3 2.1 %broadcast_select_fusion = (bf16[640,2048]{1,0:T(8,128)(2,1)S(1)}, bf16[640,2048]{1,0:T(8,128)(2,1)S(1)}) fusion(bf16[640,2048]{1,0:T(8,128)(2,1)} %collective-permute-done.19, bf16[640,2048]{1,0:T(8,128)(2,1)S(1)} %maximum_dynamic-update-slice_fusion, pred[]{:T(512)S(6)} %eq.9), kind=kLoop, calls=%fused_computation.4 | loop fusion | flops 2621440 | bytes 10485761 | tf_op jit(solution)/shard_map/jit(_where)/select_n | solution.py:118
  103.4 1.0 fusion.10
  105.1 1.0 fusion.4
  107.1 1.0 fusion.29
  108.3 1.3 %collective-permute-start.22 = (bf16[160,640]{1,0:T(8,128)(2,1)S(1)}, bf16[160,640]{1,0:T(8,128)(2,1)S(1)}, u32[]{:S(2)}, u32[]{:S(2)}) collective-permute-start(bf16[160,640]{1,0:T(8,128)(2,1)S(1)} %get-tuple-element.71), channel_id=1, source_target_pairs={{0,32},{1,33},{2,34},{3,35},{4,36},{5,37},{6,38},{7,39},{8,40},{9,... | collective-permute-start | bytes 614408 | tf_op jit(solution)/shard_map/ppermute | solution.py:23
  109.6 1.0 add_add_fusion.1
  110.6 5.7 %collective-permute-done.24 = bf16[160,640]{1,0:T(8,128)(2,1)S(1)} collective-permute-done((bf16[160,640]{1,0:T(8,128)(2,1)S(1)}, bf16[160,640]{1,0:T(8,128)(2,1)S(1)}, u32[]{:S(2)}, u32[]{:S(2)}) %collective-permute-start.24) | collective-permute-done | bytes 204832 | tf_op jit(solution)/shard_map/ppermute | solution.py:23
  116.6 1.6 %collective-permute-start.23 = (bf16[320,640]{1,0:T(8,128)(2,1)S(1)}, bf16[320,640]{1,0:T(8,128)(2,1)S(1)}, u32[]{:S(2)}, u32[]{:S(2)}) collective-permute-start(bf16[320,640]{1,0:T(8,128)(2,1)S(1)} %fusion.13), channel_id=1, source_target_pairs={{0,33},{1,32},{2,35},{3,34},{4,37},{5,36},{6,39},{7,38},{8,41},{9,... | collective-permute-start | bytes 1228808 | tf_op jit(solution)/shard_map/ppermute | solution.py:23
  118.3 8.7 %collective-permute-done.25 = bf16[320,640]{1,0:T(8,128)(2,1)S(1)} collective-permute-done((bf16[320,640]{1,0:T(8,128)(2,1)S(1)}, bf16[320,640]{1,0:T(8,128)(2,1)S(1)}, u32[]{:S(2)}, u32[]{:S(2)}) %collective-permute-start.25) | collective-permute-done | bytes 409632 | tf_op jit(solution)/shard_map/ppermute | solution.py:23
  127.0 1.4 %collective-permute-done.23 = bf16[320,640]{1,0:T(8,128)(2,1)S(1)} collective-permute-done((bf16[320,640]{1,0:T(8,128)(2,1)S(1)}, bf16[320,640]{1,0:T(8,128)(2,1)S(1)}, u32[]{:S(2)}, u32[]{:S(2)}) %collective-permute-start.23) | collective-permute-done | bytes 409632 | tf_op jit(solution)/shard_map/ppermute | solution.py:23
  (69 shorter events, 15.2 us)
Async XLA Ops:
  0.0 2.1 %copy-start.7 = (bf16[256,512]{1,0:T(8,128)(2,1)S(1)}, bf16[256,512]{1,0:T(8,128)(2,1)}, u32[]{:S(2)}) copy-start(bf16[256,512]{1,0:T(8,128)(2,1)} %param.3) | copy-start | bytes 786436
  0.0 2.6 %copy-start.6 = (bf16[640,512]{1,0:T(8,128)(2,1)S(1)}, bf16[640,512]{1,0:T(8,128)(2,1)}, u32[]{:S(2)}) copy-start(bf16[640,512]{1,0:T(8,128)(2,1)} %param.5) | copy-start | bytes 1966084
  2.0 3.6 %collective-permute-start = (bf16[4,2,320,256]{3,2,1,0:T(8,128)(2,1)S(1)}, bf16[4,2,320,256]{3,2,1,0:T(8,128)(2,1)}, u32[]{:S(2)}, u32[]{:S(2)}) collective-permute-start(bf16[4,2,320,256]{3,2,1,0:T(8,128)(2,1)S(1)} %get-tuple-element.70), channel_id=1, source_target_pairs={{0,16},{1,17},{2,18},{3,19},{4,20},{5,21},{6,22},{7,23},{8,24},{9,... | collective-permute-start | bytes 3932168 | tf_op jit(solution)/shard_map/ppermute | solution.py:23
  2.1 3.5 %collective-permute-start.1 = (bf16[256,512]{1,0:T(8,128)(2,1)S(1)}, bf16[256,512]{1,0:T(8,128)(2,1)}, u32[]{:S(2)}, u32[]{:S(2)}) collective-permute-start(bf16[256,512]{1,0:T(8,128)(2,1)S(1)} %copy-done.7), channel_id=1, source_target_pairs={{0,16},{1,17},{2,18},{3,19},{4,20},{5,21},{6,22},{7,23},{8,24},{9,... | collective-permute-start | bytes 786440 | tf_op jit(solution)/shard_map/ppermute | solution.py:23
  5.6 16.6 %all-to-all-start = ((bf16[8,160,256]{2,1,0:T(8,128)(2,1)}), bf16[8,160,256]{2,1,0:T(8,128)(2,1)S(1)}, u32[]{:S(2)}, u32[]{:S(2)}) async-start(bf16[8,160,256]{2,1,0:T(8,128)(2,1)} %bitcast.5), calls=%async_computation | async-start | bytes 1310720 | tf_op jit(solution)/shard_map/all_to_all | solution.py:79
  15.4 1.0 copy-start.8
  22.4 39.6 %all-to-all-start.1 = ((bf16[8,640,256]{2,1,0:T(8,128)(2,1)}), bf16[8,640,256]{2,1,0:T(8,128)(2,1)S(1)}, u32[]{:S(2)}, u32[]{:S(2)}) async-start(bf16[8,640,256]{2,1,0:T(8,128)(2,1)} %bitcast.11), calls=%async_computation.1 | async-start | bytes 5242880 | tf_op jit(solution)/shard_map/all_to_all | solution.py:92
  27.1 11.3 %collective-permute-start.2 = (bf16[160,256]{1,0:T(8,128)(2,1)S(1)}, bf16[160,256]{1,0:T(8,128)(2,1)S(1)}, u32[]{:S(2)}, u32[]{:S(2)}) collective-permute-start(bf16[160,256]{1,0:T(8,128)(2,1)S(1)} %get-tuple-element.79), channel_id=1, source_target_pairs={{0,14},{1,15},{2,0},{3,1},{4,2},{5,3},{6,4},{7,5},{8,6},{9,7},{10,... | collective-permute-start | bytes 245768 | tf_op jit(solution)/shard_map/ppermute | solution.py:23
  33.1 9.9 %collective-permute-start.3 = (bf16[160,256]{1,0:T(8,128)(2,1)S(1)}, bf16[160,256]{1,0:T(8,128)(2,1)S(1)}, u32[]{:S(2)}, u32[]{:S(2)}) collective-permute-start(bf16[160,256]{1,0:T(8,128)(2,1)S(1)} %get-tuple-element.78), channel_id=1, source_target_pairs={{0,10},{1,11},{2,12},{3,13},{4,14},{5,15},{6,0},{7,1},{8,2},{9,3},... | collective-permute-start | bytes 245768 | tf_op jit(solution)/shard_map/ppermute | solution.py:23
  35.0 10.3 %collective-permute-start.4 = (bf16[160,256]{1,0:T(8,128)(2,1)S(1)}, bf16[160,256]{1,0:T(8,128)(2,1)S(1)}, u32[]{:S(2)}, u32[]{:S(2)}) collective-permute-start(bf16[160,256]{1,0:T(8,128)(2,1)S(1)} %get-tuple-element.77), channel_id=1, source_target_pairs={{0,8},{1,9},{2,10},{3,11},{4,12},{5,13},{6,14},{7,15},{8,0},{9,1},... | collective-permute-start | bytes 245768 | tf_op jit(solution)/shard_map/ppermute | solution.py:23
  35.0 12.0 %collective-permute-start.5 = (bf16[160,256]{1,0:T(8,128)(2,1)S(1)}, bf16[160,256]{1,0:T(8,128)(2,1)S(1)}, u32[]{:S(2)}, u32[]{:S(2)}) collective-permute-start(bf16[160,256]{1,0:T(8,128)(2,1)S(1)} %get-tuple-element.76), channel_id=1, source_target_pairs={{0,6},{1,7},{2,8},{3,9},{4,10},{5,11},{6,12},{7,13},{8,14},{9,15},... | collective-permute-start | bytes 245768 | tf_op jit(solution)/shard_map/ppermute | solution.py:23
  47.0 5.5 %collective-permute-start.6 = (bf16[160,256]{1,0:T(8,128)(2,1)S(1)}, bf16[160,256]{1,0:T(8,128)(2,1)S(1)}, u32[]{:S(2)}, u32[]{:S(2)}) collective-permute-start(bf16[160,256]{1,0:T(8,128)(2,1)S(1)} %get-tuple-element.75), channel_id=1, source_target_pairs={{0,12},{1,13},{2,14},{3,15},{4,0},{5,1},{6,2},{7,3},{8,4},{9,5},{1... | collective-permute-start | bytes 245768 | tf_op jit(solution)/shard_map/ppermute | solution.py:23
  49.7 7.1 %collective-permute-start.7 = (bf16[160,256]{1,0:T(8,128)(2,1)S(1)}, bf16[160,256]{1,0:T(8,128)(2,1)S(1)}, u32[]{:S(2)}, u32[]{:S(2)}) collective-permute-start(bf16[160,256]{1,0:T(8,128)(2,1)S(1)} %get-tuple-element.74), channel_id=1, source_target_pairs={{0,4},{1,5},{2,6},{3,7},{4,8},{5,9},{6,10},{7,11},{8,12},{9,13},{1... | collective-permute-start | bytes 245768 | tf_op jit(solution)/shard_map/ppermute | solution.py:23
  50.0 6.8 %collective-permute-start.8 = (bf16[160,256]{1,0:T(8,128)(2,1)S(1)}, bf16[160,256]{1,0:T(8,128)(2,1)S(1)}, u32[]{:S(2)}, u32[]{:S(2)}) collective-permute-start(bf16[160,256]{1,0:T(8,128)(2,1)S(1)} %get-tuple-element.73), channel_id=1, source_target_pairs={{0,2},{1,3},{2,4},{3,5},{4,6},{5,7},{6,8},{7,9},{8,10},{9,11},{10,... | collective-permute-start | bytes 245768 | tf_op jit(solution)/shard_map/ppermute | solution.py:23
  63.2 8.0 %collective-permute-start.9 = (bf16[640,256]{1,0:T(8,128)(2,1)}, bf16[640,256]{1,0:T(8,128)(2,1)}, u32[]{:S(2)}, u32[]{:S(2)}) collective-permute-start(bf16[640,256]{1,0:T(8,128)(2,1)} %reduce_sum.12), channel_id=1, source_target_pairs={{0,14},{1,15},{2,0},{3,1},{4,2},{5,3},{6,4},{7,5},{8,6},{9,7},{10,... | collective-permute-start | bytes 983048 | tf_op jit(solution)/shard_map/ppermute | solution.py:23
  64.8 9.0 %collective-permute-start.11 = (bf16[640,256]{1,0:T(8,128)(2,1)}, bf16[640,256]{1,0:T(8,128)(2,1)}, u32[]{:S(2)}, u32[]{:S(2)}) collective-permute-start(bf16[640,256]{1,0:T(8,128)(2,1)} %reduce_sum.12), channel_id=1, source_target_pairs={{0,2},{1,3},{2,4},{3,5},{4,6},{5,7},{6,8},{7,9},{8,10},{9,11},{10,... | collective-permute-start | bytes 983048 | tf_op jit(solution)/shard_map/ppermute | solution.py:23
  65.2 15.6 %collective-permute-start.13 = (bf16[160,2048]{1,0:T(8,128)(2,1)}, bf16[160,2048]{1,0:T(8,128)(2,1)S(1)}, u32[]{:S(2)}, u32[]{:S(2)}) collective-permute-start(bf16[160,2048]{1,0:T(8,128)(2,1)} %constant_dynamic-update-slice_fusion.2), channel_id=1, source_target_pairs={{0,64},{1,65},{2,66},{3,67},{4,68},{5,69},{6,70},{7,71},{8,72},{9,... | collective-permute-start | bytes 1966088 | tf_op jit(solution)/shard_map/ppermute | solution.py:23
  66.7 15.0 %collective-permute-start.14 = (bf16[160,2048]{1,0:T(8,128)(2,1)}, bf16[160,2048]{1,0:T(8,128)(2,1)}, u32[]{:S(2)}, u32[]{:S(2)}) collective-permute-start(bf16[160,2048]{1,0:T(8,128)(2,1)} %constant_dynamic-update-slice_fusion.2), channel_id=1, source_target_pairs={{0,192},{1,193},{2,194},{3,195},{4,196},{5,197},{6,198},{7,199},{8... | collective-permute-start | bytes 1966088 | tf_op jit(solution)/shard_map/ppermute | solution.py:23
  71.2 10.6 %collective-permute-start.10 = (bf16[640,256]{1,0:T(8,128)(2,1)}, bf16[640,256]{1,0:T(8,128)(2,1)S(1)}, u32[]{:S(2)}, u32[]{:S(2)}) collective-permute-start(bf16[640,256]{1,0:T(8,128)(2,1)} %collective-permute-done.9), channel_id=1, source_target_pairs={{0,14},{1,15},{2,0},{3,1},{4,2},{5,3},{6,4},{7,5},{8,6},{9,7},{10,... | collective-permute-start | bytes 983048 | tf_op jit(solution)/shard_map/ppermute | solution.py:23
  73.8 8.5 %collective-permute-start.12 = (bf16[640,256]{1,0:T(8,128)(2,1)}, bf16[640,256]{1,0:T(8,128)(2,1)S(1)}, u32[]{:S(2)}, u32[]{:S(2)}) collective-permute-start(bf16[640,256]{1,0:T(8,128)(2,1)} %collective-permute-done.11), channel_id=1, source_target_pairs={{0,2},{1,3},{2,4},{3,5},{4,6},{5,7},{6,8},{7,9},{8,10},{9,11},{10,... | collective-permute-start | bytes 983048 | tf_op jit(solution)/shard_map/ppermute | solution.py:23
  80.8 8.4 %copy-start = (bf16[160,2048]{1,0:T(8,128)(2,1)}, bf16[160,2048]{1,0:T(8,128)(2,1)S(1)}, u32[]{:S(2)}) copy-start(bf16[160,2048]{1,0:T(8,128)(2,1)S(1)} %collective-permute-done.13) | copy-start | bytes 1966084
  82.2 9.2 %collective-permute-start.15 = (bf16[640,256]{1,0:T(8,128)(2,1)S(1)}, bf16[640,256]{1,0:T(8,128)(2,1)S(1)}, u32[]{:S(2)}, u32[]{:S(2)}) collective-permute-start(bf16[640,256]{1,0:T(8,128)(2,1)S(1)} %collective-permute-done.10), channel_id=1, source_target_pairs={{0,14},{1,15},{2,0},{3,1},{4,2},{5,3},{6,4},{7,5},{8,6},{9,7},{10,... | collective-permute-start | bytes 983048 | tf_op jit(solution)/shard_map/ppermute | solution.py:23
  84.7 8.3 %collective-permute-start.16 = (bf16[640,256]{1,0:T(8,128)(2,1)S(1)}, bf16[640,256]{1,0:T(8,128)(2,1)S(1)}, u32[]{:S(2)}, u32[]{:S(2)}) collective-permute-start(bf16[640,256]{1,0:T(8,128)(2,1)S(1)} %collective-permute-done.12), channel_id=1, source_target_pairs={{0,2},{1,3},{2,4},{3,5},{4,6},{5,7},{6,8},{7,9},{8,10},{9,11},{10,... | collective-permute-start | bytes 983048 | tf_op jit(solution)/shard_map/ppermute | solution.py:23
  84.7 8.4 %collective-permute-start.17 = (bf16[160,1024]{1,0:T(8,128)(2,1)S(1)}, bf16[160,1024]{1,0:T(8,128)(2,1)S(1)}, u32[]{:S(2)}, u32[]{:S(2)}) collective-permute-start(bf16[160,1024]{1,0:T(8,128)(2,1)S(1)} %slice.95), channel_id=1, source_target_pairs={{0,64},{1,65},{2,66},{3,67},{4,68},{5,69},{6,70},{7,71},{8,72},{9,... | collective-permute-start | bytes 983048 | tf_op jit(solution)/shard_map/ppermute | solution.py:23
  88.7 7.2 %collective-permute-start.18 = (bf16[160,1024]{1,0:T(8,128)(2,1)S(1)}, bf16[160,1024]{1,0:T(8,128)(2,1)S(1)}, u32[]{:S(2)}, u32[]{:S(2)}) collective-permute-start(bf16[160,1024]{1,0:T(8,128)(2,1)S(1)} %slice.96), channel_id=1, source_target_pairs={{0,192},{1,193},{2,194},{3,195},{4,196},{5,197},{6,198},{7,199},{8... | collective-permute-start | bytes 983048 | tf_op jit(solution)/shard_map/ppermute | solution.py:23
  91.5 4.4 %copy-start.2 = (bf16[640,256]{1,0:T(8,128)(2,1)}, bf16[640,256]{1,0:T(8,128)(2,1)S(1)}, u32[]{:S(2)}) copy-start(bf16[640,256]{1,0:T(8,128)(2,1)S(1)} %collective-permute-done.15) | copy-start | bytes 983044
  93.0 2.9 %copy-start.4 = (bf16[640,256]{1,0:T(8,128)(2,1)}, bf16[640,256]{1,0:T(8,128)(2,1)S(1)}, u32[]{:S(2)}) copy-start(bf16[640,256]{1,0:T(8,128)(2,1)S(1)} %collective-permute-done.16) | copy-start | bytes 983044
  95.9 5.4 %collective-permute-start.19 = (bf16[640,2048]{1,0:T(8,128)(2,1)S(1)}, bf16[640,2048]{1,0:T(8,128)(2,1)}, u32[]{:S(2)}, u32[]{:S(2)}) collective-permute-start(bf16[640,2048]{1,0:T(8,128)(2,1)S(1)} %maximum_dynamic-update-slice_fusion), channel_id=1, source_target_pairs={{0,16},{1,17},{2,18},{3,19},{4,20},{5,21},{6,22},{7,23},{8,24},{9,... | collective-permute-start | bytes 7864328 | tf_op jit(solution)/shard_map/ppermute | solution.py:23
  97.0 9.8 %collective-permute-start.21 = (bf16[320,256]{1,0:T(8,128)(2,1)S(1)}, bf16[320,256]{1,0:T(8,128)(2,1)S(1)}, u32[]{:S(2)}, u32[]{:S(2)}) collective-permute-start(bf16[320,256]{1,0:T(8,128)(2,1)S(1)} %slice.100), channel_id=1, source_target_pairs={{0,2},{1,3},{2,4},{3,5},{4,6},{5,7},{6,8},{7,9},{8,10},{9,11},{10,... | collective-permute-start | bytes 491528 | tf_op jit(solution)/shard_map/ppermute | solution.py:23
  98.0 5.4 %copy-start.1 = (bf16[640,768]{1,0:T(8,128)(2,1)S(1)}, bf16[640,768]{1,0:T(8,128)(2,1)}, u32[]{:S(2)}) copy-start(bf16[640,768]{1,0:T(8,128)(2,1)} %pad_maximum_fusion.4) | copy-start | bytes 2949124
  98.0 8.8 %collective-permute-start.20 = (bf16[320,256]{1,0:T(8,128)(2,1)S(1)}, bf16[320,256]{1,0:T(8,128)(2,1)S(1)}, u32[]{:S(2)}, u32[]{:S(2)}) collective-permute-start(bf16[320,256]{1,0:T(8,128)(2,1)S(1)} %slice.99), channel_id=1, source_target_pairs={{0,14},{1,15},{2,0},{3,1},{4,2},{5,3},{6,4},{7,5},{8,6},{9,7},{10,... | collective-permute-start | bytes 491528 | tf_op jit(solution)/shard_map/ppermute | solution.py:23
  106.0 1.0 copy-start.3
  106.0 1.1 copy-start.5
  108.2 8.2 %collective-permute-start.24 = (bf16[160,640]{1,0:T(8,128)(2,1)S(1)}, bf16[160,640]{1,0:T(8,128)(2,1)S(1)}, u32[]{:S(2)}, u32[]{:S(2)}) collective-permute-start(bf16[160,640]{1,0:T(8,128)(2,1)S(1)} %get-tuple-element.72), channel_id=1, source_target_pairs={{0,33},{1,32},{2,35},{3,34},{4,37},{5,36},{6,39},{7,38},{8,41},{9,... | collective-permute-start | bytes 614408 | tf_op jit(solution)/shard_map/ppermute | solution.py:23
  108.3 8.3 %collective-permute-start.22 = (bf16[160,640]{1,0:T(8,128)(2,1)S(1)}, bf16[160,640]{1,0:T(8,128)(2,1)S(1)}, u32[]{:S(2)}, u32[]{:S(2)}) collective-permute-start(bf16[160,640]{1,0:T(8,128)(2,1)S(1)} %get-tuple-element.71), channel_id=1, source_target_pairs={{0,32},{1,33},{2,34},{3,35},{4,36},{5,37},{6,38},{7,39},{8,40},{9,... | collective-permute-start | bytes 614408 | tf_op jit(solution)/shard_map/ppermute | solution.py:23
  116.4 10.5 %collective-permute-start.25 = (bf16[320,640]{1,0:T(8,128)(2,1)S(1)}, bf16[320,640]{1,0:T(8,128)(2,1)S(1)}, u32[]{:S(2)}, u32[]{:S(2)}) collective-permute-start(bf16[320,640]{1,0:T(8,128)(2,1)S(1)} %fusion.12), channel_id=1, source_target_pairs={{0,32},{1,33},{2,34},{3,35},{4,36},{5,37},{6,38},{7,39},{8,40},{9,... | collective-permute-start | bytes 1228808 | tf_op jit(solution)/shard_map/ppermute | solution.py:23
  116.6 11.7 %collective-permute-start.23 = (bf16[320,640]{1,0:T(8,128)(2,1)S(1)}, bf16[320,640]{1,0:T(8,128)(2,1)S(1)}, u32[]{:S(2)}, u32[]{:S(2)}) collective-permute-start(bf16[320,640]{1,0:T(8,128)(2,1)S(1)} %fusion.13), channel_id=1, source_target_pairs={{0,33},{1,32},{2,35},{3,34},{4,37},{5,36},{6,39},{7,38},{8,41},{9,... | collective-permute-start | bytes 1228808 | tf_op jit(solution)/shard_map/ppermute | solution.py:23
